TPU v7x, 32 devices: a whole 2x2x4 slice. The times are simulated.
32 devices in a mesh: batch: 8 (over z, y), branch: 4 (over x, core).
Axes of the slice: x: 2, y: 2, z: 4, core: 2. Of those that a mesh axis runs over, the one named last changes fastest.
Arguments:
- inputs: bfloat16 [16384, 1024], P('batch'), may hold values from -6 to 6
- ln_gain: float32 [1024], replicated, may hold values from 0.5 to 1.5
- ln_shift: float32 [1024], replicated, may hold values from -1 to 1
- qkv_weight: bfloat16 [1024, 3072], P(None, 'branch'), may hold values from -0.1875 to 0.1875
- qkv_bias: float32 [3072], P('branch'), may hold values from -0.12 to 0.12
- out_weight: bfloat16 [1024, 1024], P('branch'), may hold values from -3 to 3
- up_weight: bfloat16 [1024, 4096], P(None, 'branch'), may hold values from -0.1875 to 0.1875
- up_bias: float32 [4096], P('branch'), may hold values from -1 to 1
- down_weight: bfloat16 [4096, 1024], P('branch'), may hold values from -0.09375 to 0.09375
- out_bias: float32 [1024], replicated, may hold values from -1 to 1
- feature_samples: float32 [64, 64], replicated, may hold values from -4 to 4
- lengths: int32 [8], replicated, may hold values from 1 to 15360, as said below
- cotangent: bfloat16 [16384, 1024], P('batch'), may hold values from -6 to 6
Outputs:
- output: bfloat16 [16384, 1024], P(('batch', 'branch'))
- input_grad: float32 [16384, 1024], P(('batch', 'branch'))
- gain_grad: float32 [1024], replicated
- shift_grad: float32 [1024], replicated
- qkv_weight_grad: float32 [1024, 3072], P('batch', 'branch')
- qkv_bias_grad: float32 [3072], replicated
- out_weight_grad: float32 [1024, 1024], P('branch', 'batch')
- up_weight_grad: float32 [1024, 4096], P('batch', 'branch')
- up_bias_grad: float32 [4096], replicated
- down_weight_grad: float32 [4096, 1024], P('branch', 'batch')
- out_bias_grad: float32 [1024], replicated
Inputs may be any that keep to these rules, and one draw needn't show every extreme that they name: `lengths`: the 8 sequences fill the 16384 tokens in order; exactly one has 15360 tokens, the others together 16384 - 15360.
All inputs are finite; a program needn't handle non-finite values.
Results may differ from a plain program's by a relative error of at most 0.012.
The roundings to bfloat16 on the way count: a program that leaves them out, or rounds other values in their place, can miss the bound.
Values sent between devices are 32-bit elements; how exact they have to be, the bound alone decides.
No kernel may reach another device: no remote copies, remote signals or barrier semaphores. Data moves between devices by JAX's collectives and lax.ppermute only.
A program may use at most 256 MiB of HBM per device.

v0:
```python
import math

import jax
import jax.numpy as jnp
from jax import lax
from jax.sharding import PartitionSpec as P

ROT = 16
GROUP = 64


highest = lax.Precision.HIGHEST
epsilon = 1e-05


def entering(shard, axis, combine, identity, reverse):
    devices, here = (lax.axis_size(axis), lax.axis_index(axis))
    everything = jax.tree.map(lambda part: lax.all_gather(part, axis), shard)
    start = jax.tree.map(
        lambda part, zero: jnp.broadcast_to(jnp.asarray(zero, part.dtype), part.shape),
        shard,
        identity,
    )

    def turn(k, before):
        at = devices - 1 - k if reverse else k
        reached = at > here if reverse else at < here
        new = combine(before, jax.tree.map(lambda part: part[at], everything))
        return jax.tree.map(lambda a, b: jnp.where(reached, a, b), new, before)

    return lax.fori_loop(0, devices, turn, start)


def dct_table(order_size):
    row_ids = jnp.arange(order_size, dtype=jnp.float32)[:, None]
    col_ids = jnp.arange(order_size, dtype=jnp.float32)[None, :]
    table = jnp.cos(math.pi * (col_ids + 0.5) * row_ids / order_size) * math.sqrt(2.0 / order_size)
    return jnp.where(row_ids == 0.0, table * math.sqrt(0.5), table)


def rotate(values_in, in_seq_place, rotary, direction):
    half_rot = rotary // 2
    frequency = 10000.0 ** (-2.0 * jnp.arange(half_rot, dtype=jnp.float32) / rotary)
    angles = in_seq_place.astype(jnp.float32)[:, None] * frequency[None, :]
    cosine = jnp.cos(angles)[:, None, :]
    sine_part = direction * jnp.sin(angles)[:, None, :]
    leading = values_in[..., :half_rot]
    trailing = values_in[..., half_rot:rotary]
    return jnp.concatenate(
        [
            leading * cosine - trailing * sine_part,
            trailing * cosine + leading * sine_part,
            values_in[..., rotary:],
        ],
        axis=-1,
    )


def gelu_slope(pre_act):
    return 0.5 * (1.0 + lax.erf(pre_act / math.sqrt(2.0))) + pre_act * jnp.exp(
        -0.5 * pre_act * pre_act
    ) / math.sqrt(2.0 * math.pi)


def combine_carry(earlier, later):
    open_part = 1.0 - later[2]
    return (
        later[0] + open_part * earlier[0],
        later[1] + open_part * earlier[1],
        jnp.maximum(earlier[2], later[2]),
    )


def per_device(
    inputs,
    ln_gain,
    ln_shift,
    qkv_weight,
    qkv_bias,
    out_weight,
    up_weight,
    up_bias,
    down_weight,
    out_bias,
    feature_samples,
    lengths,
    cotangent,
):
    f32 = jnp.float32
    tok_count, model_width = inputs.shape
    feat_count, head_size = feature_samples.shape
    local_heads = qkv_weight.shape[1] // (3 * head_size)
    branch_count = lax.axis_size("branch")
    row_share = tok_count // branch_count
    batch_pos = lax.axis_index("batch")
    branch_pos = lax.axis_index("branch")
    row_start = branch_pos * row_share
    seq_ends = jnp.cumsum(lengths, dtype=jnp.int32)
    first_pos = batch_pos * tok_count
    position = first_pos + jnp.arange(tok_count, dtype=jnp.int32)
    passed = position[:, None] >= seq_ends[None, :]
    segment = jnp.sum(passed.astype(jnp.int32), axis=1, dtype=jnp.int32)
    in_seq_place = position - jnp.sum(
        jnp.where(passed, lengths[None, :], 0), axis=1, dtype=jnp.int32
    )
    seg_before = jnp.where(
        first_pos == 0, -1, jnp.sum((first_pos - 1 >= seq_ends).astype(jnp.int32), dtype=jnp.int32)
    )
    seg_final = segment[-1]
    float_inputs = inputs.astype(f32)
    centered = float_inputs - jnp.mean(float_inputs, axis=1, keepdims=True)
    inv_std = lax.rsqrt(jnp.mean(centered * centered, axis=1, keepdims=True) + epsilon)
    unit_rows = centered * inv_std
    normed = (unit_rows * ln_gain + ln_shift).astype(jnp.bfloat16)
    projected = (jnp.dot(normed, qkv_weight, preferred_element_type=f32) + qkv_bias).astype(
        jnp.bfloat16
    )
    triple = projected.reshape(tok_count, local_heads, 3, head_size).astype(f32)
    value_rows = triple[:, :, 2]
    q_turn = rotate(triple[:, :, 0], in_seq_place, ROT, 1.0)
    k_turn = rotate(triple[:, :, 1], in_seq_place, ROT, 1.0)
    samples_dct = jnp.dot(feature_samples, dct_table(head_size), precision=highest)
    root_four = head_size**0.25

    def featurize(turned):
        argument = jnp.einsum(
            "thd,fd->thf", turned, samples_dct, precision=highest
        ) / root_four - jnp.sum(turned * turned, axis=-1, keepdims=True) / (
            2.0 * math.sqrt(head_size)
        )
        return jnp.exp(argument) / math.sqrt(feat_count)

    def feature_grad(turned, feat_rows, grad_feat):
        weighted = grad_feat * feat_rows
        return jnp.einsum(
            "thf,fd->thd", weighted, samples_dct, precision=highest
        ) / root_four - jnp.sum(weighted, axis=-1, keepdims=True) * turned / math.sqrt(head_size)

    feat_q = featurize(q_turn)
    feat_k = featurize(k_turn)
    blocks = tok_count // GROUP

    def grouped(tensor):
        return tensor.reshape((blocks, GROUP) + tensor.shape[1:])

    block_q = grouped(feat_q)
    block_k = grouped(feat_k)
    block_v = grouped(value_rows)
    seg_block = grouped(segment)
    lead_seg = seg_block[:, 0]
    tail_seg = seg_block[:, -1]
    index_c = jnp.arange(GROUP)
    causal = index_c[:, None] >= index_c[None, :]
    window = (causal[None] & (seg_block[:, :, None] == seg_block[:, None, :])).astype(f32)
    scores = jnp.einsum("cthf,cshf->chts", block_q, block_k, precision=highest) * window[:, None]
    tail_mask = (seg_block == tail_seg[:, None]).astype(f32)
    lead_mask = (seg_block == lead_seg[:, None]).astype(f32)
    tail_state = jnp.einsum("cshf,cs,cshd->chfd", block_k, tail_mask, block_v, precision=highest)
    tail_norm = jnp.einsum("cshf,cs->chf", block_k, tail_mask)
    block_ids = jnp.arange(blocks)
    block_link = (
        (block_ids[None, :] < block_ids[:, None]) & (tail_seg[None, :] == lead_seg[:, None])
    ).astype(f32)
    from_before = (lead_seg == seg_before).astype(f32)
    last_mask = (segment == seg_final).astype(f32)
    sum_state = jnp.einsum("thf,t,thd->hfd", feat_k, last_mask, value_rows, precision=highest)
    sum_norm = jnp.einsum("thf,t->hf", feat_k, last_mask)
    has_break = (seg_before != seg_final).astype(f32)
    identity = (jnp.zeros_like(sum_state), jnp.zeros_like(sum_norm), jnp.zeros((), f32))
    in_state, in_norm, _ = entering(
        (sum_state, sum_norm, has_break), "batch", combine_carry, identity, False
    )
    prefix_state = (
        jnp.einsum("cz,zhfd->chfd", block_link, tail_state, precision=highest)
        + from_before[:, None, None, None] * in_state
    )
    prefix_norm = (
        jnp.einsum("cz,zhf->chf", block_link, tail_norm, precision=highest)
        + from_before[:, None, None] * in_norm
    )
    numerator = jnp.einsum("chts,cshd->cthd", scores, block_v, precision=highest) + lead_mask[
        :, :, None, None
    ] * jnp.einsum("cthf,chfd->cthd", block_q, prefix_state, precision=highest)
    denominator = jnp.einsum("chts->cth", scores) + lead_mask[:, :, None] * jnp.einsum(
        "cthf,chf->cth", block_q, prefix_norm, precision=highest
    )
    attended = numerator / denominator[..., None]
    mixed_rows = attended.reshape(tok_count, local_heads * head_size).astype(jnp.bfloat16)
    pre_act = jnp.dot(normed, up_weight, preferred_element_type=f32) + up_bias
    hidden = jax.nn.gelu(pre_act, approximate=False).astype(jnp.bfloat16)
    branch_sum = lax.psum_scatter(
        jnp.dot(mixed_rows, out_weight, preferred_element_type=f32)
        + jnp.dot(hidden, down_weight, preferred_element_type=f32),
        "branch",
        scatter_dimension=0,
        tiled=True,
    )
    own_inputs = lax.dynamic_slice_in_dim(float_inputs, row_start, row_share, 0)
    output = (own_inputs + branch_sum + out_bias).astype(jnp.bfloat16)
    grad_hidden = jnp.einsum("td,fd->tf", cotangent, down_weight, preferred_element_type=f32)
    grad_pre = (grad_hidden * gelu_slope(pre_act)).astype(jnp.bfloat16)
    grad_up_w = jnp.einsum("td,tf->df", normed, grad_pre, preferred_element_type=f32)
    grad_down_w = jnp.einsum("tf,td->fd", hidden, cotangent, preferred_element_type=f32)
    up_bias_part = jnp.sum(grad_pre, axis=0, dtype=f32)
    grad_out_w = jnp.einsum("te,td->ed", mixed_rows, cotangent, preferred_element_type=f32)
    grad_att = grouped(
        jnp.einsum("td,ed->te", cotangent, out_weight, preferred_element_type=f32).reshape(
            tok_count, local_heads, head_size
        )
    )
    g_num = grad_att / denominator[..., None]
    g_den = -jnp.sum(grad_att * attended, axis=-1) / denominator
    mixing = (
        jnp.einsum("cthd,cshd->chts", g_num, block_v, precision=highest)
        + jnp.transpose(g_den, (0, 2, 1))[:, :, :, None]
    ) * window[:, None]
    g_fq = jnp.einsum("chts,cshf->cthf", mixing, block_k, precision=highest) + lead_mask[
        :, :, None, None
    ] * (
        jnp.einsum("cthd,chfd->cthf", g_num, prefix_state, precision=highest)
        + g_den[..., None] * prefix_norm[:, None]
    )
    g_fk = jnp.einsum("chts,cthf->cshf", mixing, block_q, precision=highest)
    g_value = jnp.einsum("chts,cthd->cshd", scores, g_num, precision=highest)
    g_prefix_state = jnp.einsum("cthf,ct,cthd->chfd", block_q, lead_mask, g_num, precision=highest)
    g_prefix_norm = jnp.einsum("cthf,ct,cth->chf", block_q, lead_mask, g_den, precision=highest)
    g_tail_state = jnp.einsum("cz,chfd->zhfd", block_link, g_prefix_state, precision=highest)
    g_tail_norm = jnp.einsum("cz,chf->zhf", block_link, g_prefix_norm, precision=highest)
    back_state = jnp.einsum("c,chfd->hfd", from_before, g_prefix_state)
    back_norm = jnp.einsum("c,chf->hf", from_before, g_prefix_norm)
    out_state, out_norm, _ = entering(
        (back_state, back_norm, has_break), "batch", combine_carry, identity, True
    )
    g_fk = g_fk + tail_mask[:, :, None, None] * (
        jnp.einsum("zhfd,zshd->zshf", g_tail_state, block_v, precision=highest)
        + g_tail_norm[:, None]
    )
    g_value = g_value + tail_mask[:, :, None, None] * jnp.einsum(
        "zhfd,zshf->zshd", g_tail_state, block_k, precision=highest
    )
    g_fq = g_fq.reshape(tok_count, local_heads, feat_count)
    g_fk = g_fk.reshape(tok_count, local_heads, feat_count) + last_mask[:, None, None] * (
        jnp.einsum("hfd,thd->thf", out_state, value_rows, precision=highest) + out_norm[None]
    )
    g_value = g_value.reshape(tok_count, local_heads, head_size) + last_mask[
        :, None, None
    ] * jnp.einsum("hfd,thf->thd", out_state, feat_k, precision=highest)
    grad_query = rotate(feature_grad(q_turn, feat_q, g_fq), in_seq_place, ROT, -1.0)
    grad_key = rotate(feature_grad(k_turn, feat_k, g_fk), in_seq_place, ROT, -1.0)
    grad_proj = (
        jnp.stack([grad_query, grad_key, g_value], axis=2)
        .reshape(tok_count, 3 * local_heads * head_size)
        .astype(jnp.bfloat16)
    )
    grad_qkv_w = jnp.einsum("td,te->de", normed, grad_proj, preferred_element_type=f32)
    qkv_bias_part = jnp.sum(grad_proj, axis=0, dtype=f32)
    qkv_sum, out_sum, up_sum, down_sum = (
        lax.psum_scatter(grad_qkv_w, "batch", scatter_dimension=0, tiled=True),
        lax.psum_scatter(grad_out_w, "batch", scatter_dimension=1, tiled=True),
        lax.psum_scatter(grad_up_w, "batch", scatter_dimension=0, tiled=True),
        lax.psum_scatter(grad_down_w, "batch", scatter_dimension=1, tiled=True),
    )
    grad_normed = lax.psum_scatter(
        jnp.einsum("te,de->td", grad_proj, qkv_weight, preferred_element_type=f32)
        + jnp.einsum("tf,df->td", grad_pre, up_weight, preferred_element_type=f32),
        "branch",
        scatter_dimension=0,
        tiled=True,
    )
    own_unit = lax.dynamic_slice_in_dim(unit_rows, row_start, row_share, 0)
    own_inv = lax.dynamic_slice_in_dim(inv_std, row_start, row_share, 0)
    own_cot = lax.dynamic_slice_in_dim(cotangent, row_start, row_share, 0).astype(f32)
    grad_unit = grad_normed * ln_gain
    input_grad = (
        own_inv
        * (
            grad_unit
            - jnp.mean(grad_unit, axis=1, keepdims=True)
            - own_unit * jnp.mean(grad_unit * own_unit, axis=1, keepdims=True)
        )
        + own_cot
    )
    gain_part = jnp.sum(grad_normed * own_unit, axis=0)
    shift_part = jnp.sum(grad_normed, axis=0)
    out_bias_part = jnp.sum(own_cot, axis=0)
    qkv_local = qkv_bias.shape[0]
    up_local = up_bias.shape[0]
    qkv_bias_full = lax.dynamic_update_slice_in_dim(
        jnp.zeros((qkv_local * branch_count,), f32), qkv_bias_part, branch_pos * qkv_local, 0
    )
    up_bias_full = lax.dynamic_update_slice_in_dim(
        jnp.zeros((up_local * branch_count,), f32), up_bias_part, branch_pos * up_local, 0
    )
    gain_grad, shift_grad, out_bias_grad, qkv_bias_grad, up_bias_grad = lax.psum(
        (gain_part, shift_part, out_bias_part, qkv_bias_full, up_bias_full), ("batch", "branch")
    )
    return (
        output,
        input_grad,
        gain_grad,
        shift_grad,
        qkv_sum,
        qkv_bias_grad,
        out_sum,
        up_sum,
        up_bias_grad,
        down_sum,
        out_bias_grad,
    )


def solution(mesh):
    placed = (
        P("batch", None),
        P(),
        P(),
        P(None, "branch"),
        P("branch"),
        P("branch", None),
        P(None, "branch"),
        P("branch"),
        P("branch", None),
        P(),
        P(),
        P(),
        P("batch", None),
    )
    return jax.shard_map(
        per_device,
        mesh=mesh,
        in_specs=placed,
        out_specs=(
            P(("batch", "branch"), None),
            P(("batch", "branch"), None),
            P(),
            P(),
            P("batch", "branch"),
            P(),
            P("branch", "batch"),
            P("batch", "branch"),
            P(),
            P("branch", "batch"),
            P(),
        ),
        check_vma=False,
    )
```

profile of v0, /device:TPU:0, one launch (start us, length us, event | category | flops | bytes accessed | tf_op | source)
XLA Modules:
  0.0 1056.5 jit_solution(12436606949122273946)
XLA Ops:
  55.2 15.8 %fusion.26 = f32[32,4,64,64]{3,2,1,0:T(8,128)} fusion(f32[32,64,4,64]{1,0,3,2:T(8,128)S(1)} %convert_multiply_fusion, f32[32,64,4,64]{1,0,3,2:T(8,128)S(1)} %copy-done.4), kind=kOutput, calls=%fused_computation.53 | convolution fusion | flops 402653184 | bytes 6291456 | tf_op jit(solution)/shard_map/cshf,cs,cshd->chfd/dot_general | solution.py:158
  74.4 34.5 %all-gather = f32[32,64,64]{2,1,0:T(8,128)S(1)} all-gather(f32[4,64,64]{2,1,0:T(8,128)S(1)} %fusion.91), channel_id=2, replica_groups=mesh['batch'=8,'branch'=4] {'batch'}, dimensions={0}, use_global_device_ids=true | all-gather | bytes 589824 | tf_op jit(solution)/shard_map/all_gather | solution.py:18
  109.5 26.6 %all-gather.4 = f32[8,4,64]{2,1,0:T(4,128)} all-gather(f32[1,4,64]{2,1,0:T(4,128)S(1)} %bitcast.219), channel_id=3, replica_groups=mesh['batch'=8,'branch'=4] {'batch'}, dimensions={0}, use_global_device_ids=true | all-gather | bytes 9216 | tf_op jit(solution)/shard_map/all_gather | solution.py:18
  144.1 20.9 %all-reduce = f32[8]{0:T(128)} all-reduce(f32[8]{0:T(128)} %dynamic-update-slice), channel_id=1, replica_groups=mesh['batch'=8,'branch'=4] {'batch'}, use_global_device_ids=true, to_apply=%add | all-reduce | flops 8 | bytes 64
  165.0 26.0 %while.34 = (s32[]{:T(128)}, f32[4,64,64]{2,1,0:T(8,128)S(1)}, f32[4,64]{1,0:T(4,128)}, s32[]{:T(128)}, f32[8,4,64,64]{3,2,1,0:T(8,128)S(1)}, /*index=5*/f32[8]{...) while((s32[]{:T(128)}, f32[4,64,64]{2,1,0:T(8,128)S(1)}, f32[4,64]{1,0:T(4,128)}, ...), condition=%wide.region_9.10_spmd.clone, body=%wide.region_8.9_spmd.clone.sunk | while | flops 66565 | bytes 199843 | solution.py:31
  207.9 7.5 multiply_add_fusion
  215.4 16.2 %fusion.38 = f32[32,4,64,64]{3,2,1,0:T(8,128)} fusion(f32[32,4,64,64]{3,0,2,1:T(8,128)S(1)} %multiply_add_fusion, f32[32,64,4,64]{1,0,3,2:T(8,128)S(1)} %copy-done.1), kind=kOutput, calls=%fused_computation.69 | convolution fusion | flops 402653184 | bytes 6291456 | tf_op jit(solution)/shard_map/cthf,chfd->cthd/dot_general | solution.py:183
  247.4 13.5 %multiply_reduce_fusion.2 = (f32[32,4,64]{2,1,0:T(4,128)S(1)}, f32[32,4,64,64]{2,3,1,0:T(8,128)}) fusion(f32[32,64,64]{1,2,0:T(8,128)S(1)} %and_convert_fusion, f32[32,64,4,64]{3,1,2,0:T(8,128)} %copy.206, f32[32,64,4,64]{1,0,3,2:T(8,128)} %reshape.333), kind=kOutput, calls=%fused_computation.83 | convolution fusion | flops 403693568 | bytes 6848512 | tf_op jit(solution)/shard_map/cthf,cshf->chts/dot_general | solution.py:155
  267.2 12.0 %multiply_reduce_fusion.1 = (f32[32,64,4]{1,2,0:T(4,128)S(1)}, bf16[32,64,4,64]{1,3,2,0:T(8,128)(2,1)}) fusion(f32[32,64,4,64]{1,0,3,2:T(8,128)} %reshape_reshape.3, f32[32,64,4]{1,2,0:T(4,128)S(1)} %fusion.132, f32[32,4,64,64]{3,2,1,0:T(8,128)S(1)} %copy-done.24, f32[32,64]{1,0:T(8,128)S(1)} %copy-done.51, bf16[32,64,4,64]{3,1,2,0:T(8,128)(2,1)S(1)} %copy-done.18, ...), kind=kOutput, calls=%fused_computation.58 | convolution fusion | flops 406315008 | bytes 8986624 | tf_op jit(solution)/shard_map/chts,cshd->cthd/dot_general | solution.py:181
  280.6 9.5 fusion.43
  290.1 12.1 %fusion.42 = f32[32,4,64,64]{3,2,1,0:T(8,128)} fusion(f32[32,4,64,64]{2,3,1,0:T(8,128)S(1)} %fusion.150, f32[32,64,4,64]{1,0,3,2:T(8,128)S(1)} %copy-done.2, f32[32,4,64]{2,1,0:T(4,128)S(1)} %bitcast_divide_fusion.1, f32[32,64,64]{1,2,0:T(8,128)S(1)} %and_convert_fusion), kind=kOutput, calls=%fused_computation.75 | convolution fusion | flops 403701760 | bytes 6848512 | tf_op jit(solution)/shard_map/chts,cthf->cshf/dot_general | solution.py:223
  302.2 14.0 %fusion.28 = f32[32,4,64,64]{3,2,1,0:T(8,128)S(1)} fusion(f32[32,64,4,64]{1,0,3,2:T(8,128)S(1)} %copy-done.2, f32[32,64]{1,0:T(8,128)S(1)} %copy-done.51, f32[32,64,4,64]{1,0,3,2:T(8,128)S(1)} %copy-done.26, f32[32,64,4]{1,2,0:T(4,128)S(1)} %fusion.132), kind=kOutput, calls=%fused_computation.55 | convolution fusion | flops 403701760 | bytes 6332416 | tf_op jit(solution)/shard_map/cthf,ct,cthd->chfd/dot_general | solution.py:225
  316.2 9.7 fusion.56
  337.5 12.0 %fusion.23 = f32[32,64,4,64]{1,3,2,0:T(8,128)S(1)} fusion(f32[32,4,64,64]{3,2,1,0:T(8,128)} %fusion.43, f32[32,4,64,64]{3,0,2,1:T(8,128)} %copy-done.11, f32[32,4,64]{2,1,0:T(4,128)} %copy.227, f32[32,64,4]{1,2,0:T(4,128)} %get-tuple-element.409, f32[32,64]{1,0:T(8,128)S(1)} %copy-done.51, f32[32,64,4,64]{1,0,3,2:T(8,128)} %reshape_reshape.3, ...), kind=kOutput, calls=%fused_computation.49 | convolution fusion | flops 405274624 | bytes 8495104 | tf_op jit(solution)/shard_map/cthd,chfd->cthf/dot_general | solution.py:220
  367.8 11.9 %fusion.30 = f32[32,4,64,64]{2,3,1,0:T(8,128)} fusion(f32[32,64,4,64]{3,1,2,0:T(8,128)S(1)} %copy-done.7, f32[32,4,64,64]{3,0,2,1:T(8,128)S(1)} %copy-done.8), kind=kOutput, calls=%fused_computation.61 | convolution fusion | flops 402653184 | bytes 6291456 | tf_op jit(solution)/shard_map/zhfd,zshf->zshd/dot_general | solution.py:238
  379.7 7.3 bitcast_add_fusion.5
  396.5 26.6 %all-gather.5 = f32[8,4,64]{2,1,0:T(4,128)} all-gather(f32[1,4,64]{2,1,0:T(4,128)} %bitcast.220), channel_id=5, replica_groups=mesh['batch'=8,'branch'=4] {'batch'}, dimensions={0}, use_global_device_ids=true | all-gather | bytes 9216 | tf_op jit(solution)/shard_map/all_gather | solution.py:18
  423.1 34.5 %all-gather.2 = f32[32,64,64]{2,1,0:T(8,128)} all-gather(f32[4,64,64]{2,1,0:T(8,128)} %bitcast.217), channel_id=4, replica_groups=mesh['batch'=8,'branch'=4] {'batch'}, dimensions={0}, use_global_device_ids=true | all-gather | bytes 589824 | tf_op jit(solution)/shard_map/all_gather | solution.py:18
  457.6 33.3 %while.35 = (s32[]{:T(128)}, f32[4,64,64]{2,1,0:T(8,128)S(1)}, f32[4,64]{1,0:T(4,128)}, s32[]{:T(128)}, f32[8,4,64,64]{3,2,1,0:T(8,128)}, /*index=5*/f32[8]{0:T(...) while((s32[]{:T(128)}, f32[4,64,64]{2,1,0:T(8,128)S(1)}, ...), condition=%wide.region_15.16_spmd.clone, body=%wide.region_14.15_spmd.clone.sunk | while | flops 66569 | bytes 199905 | solution.py:31
  502.4 10.4 bitcast_add_fusion.4
  533.0 23.5 %fusion.8 = (bf16[2048,1024]{1,0:T(8,128)(2,1)}, f32[2048,1024]{1,0:T(8,128)}) fusion(f32[1024]{0:T(1024)S(1)} %copy-done.80, bf16[2048,1024]{1,0:T(8,128)(2,1)S(1)} %copy-done.22, bf16[1024,1024]{1,0:T(8,128)(2,1)S(1)} %copy-done), kind=kOutput, calls=%fused_computation.14 | convolution fusion | flops 4433379328 | bytes 18878464 | tf_op jit(solution)/shard_map/dot_general | solution.py:189
  556.5 9.6 convert_reduce_fusion
  583.1 7.8 fusion.154
  600.9 8.3 fusion.157
  609.2 10.4 fusion.159
  619.9 10.3 fusion.160
  651.7 40.6 %all-reduce.1 = (f32[1024]{0:T(1024)}, f32[1024]{0:T(1024)}, f32[3072]{0:T(1024)}, f32[4096]{0:T(1024)}, f32[1024]{0:T(1024)}) all-reduce(f32[1024]{0:T(1024)S(1)} %get-tuple-element.365, f32[1024]{0:T(1024)S(1)} %get-tuple-element.368, f32[3072]{0:T(1024)S(1)} %dynamic_update_slice.6, ...), channel_id=1, replica_groups=mesh['batch'=8,'branch'=4] {'batch','branch'}, use_global_device_ids=true, to_apply=%region_21.22 | all-reduce | flops 10240 | bytes 81920 | tf_op jit(solution)/shard_map/psum | solution.py:294
  692.3 27.5 %reduce-scatter.7.cloned.1.call-done = f32[512,1024]{1,0:T(8,128)} async-done(((f32[2048,1024]{1,0:T(8,128)}), f32[512,1024]{1,0:T(8,128)}) %reduce-scatter.7.cloned.1.call-update) | async-done | bytes 2097168 | tf_op jit(solution)/shard_map/reduce_scatter | solution.py:191
  723.6 64.2 %reduce-scatter.13.cloned.1.call-done = f32[256,128]{1,0:T(8,128)} async-done(((f32[256,1024]{1,0:T(8,128)}), f32[256,128]{1,0:T(8,128)}) %reduce-scatter.13.cloned.1.call-update) | async-done | bytes 131088 | tf_op jit(solution)/shard_map/reduce_scatter | solution.py:259
  787.7 77.8 %reduce-scatter.11.cloned.1.call-done = f32[128,768]{1,0:T(8,128)} async-done(((f32[1024,768]{1,0:T(8,128)}), f32[128,768]{1,0:T(8,128)}) %reduce-scatter.11.cloned.1.call-update) | async-done | bytes 393232 | tf_op jit(solution)/shard_map/reduce_scatter | solution.py:258
  865.6 91.5 %reduce-scatter.15.cloned.1.call-done = f32[128,1024]{1,0:T(8,128)} async-done(((f32[1024,1024]{1,0:T(8,128)}), f32[128,1024]{1,0:T(8,128)}) %reduce-scatter.15.cloned.1.call-update) | async-done | bytes 524304 | tf_op jit(solution)/shard_map/reduce_scatter | solution.py:260
  957.1 92.2 %reduce-scatter.17.cloned.1.call-done = f32[1024,128]{1,0:T(8,128)} async-done(((f32[1024,1024]{1,0:T(8,128)}), f32[1024,128]{1,0:T(8,128)}) %reduce-scatter.17.cloned.1.call-update) | async-done | bytes 524304 | tf_op jit(solution)/shard_map/reduce_scatter | solution.py:261
  (329 shorter events, 270.2 us)
Async XLA Ops:
  7.2 525.8 %copy-start = (bf16[1024,1024]{1,0:T(8,128)(2,1)S(1)}, bf16[1024,1024]{1,0:T(8,128)(2,1)}, u32[]{:S(2)}) copy-start(bf16[1024,1024]{1,0:T(8,128)(2,1)} %param.23) | copy-start | bytes 6291460
  7.2 637.5 %reduce-scatter.9.cloned.1.call-start = ((), (), s32[]{:S(2)}) async-start(), calls=%async_computation.7 | async-start | bytes 10485760 | tf_op jit(solution)/shard_map/reduce_scatter | solution.py:263
  55.2 15.8 %copy-start.6 = (f32[2048,4,64]{0,2,1:T(8,128)S(1)}, f32[2048,4,64]{0,2,1:T(8,128)}, u32[]{:S(2)}) copy-start(f32[2048,4,64]{0,2,1:T(8,128)} %fusion.72) | copy-start | bytes 6291460
  55.2 15.8 %copy-start.57 = (f32[2048]{0:T(1024)S(1)}, f32[2048]{0:T(1024)}, u32[]{:S(2)}) copy-start(f32[2048]{0:T(1024)} %get-tuple-element.410) | copy-start | bytes 24580
  71.0 37.9 %copy-start.70 = (pred[2048]{0:T(1024)(128)(4,1)S(1)}, pred[2048]{0:T(1024)(128)(4,1)}, u32[]{:S(2)}) copy-start(pred[2048]{0:T(1024)(128)(4,1)} %get-tuple-element.411) | copy-start | bytes 6148
  196.8 11.1 %copy-start.65 = (s32[32]{0:T(128)S(1)}, s32[32]{0:T(128)}, u32[]{:S(2)}) copy-start(s32[32]{0:T(128)} %copy-done.64) | copy-start | bytes 388
  196.8 11.1 %copy-start.68 = (s32[32]{0:T(128)S(1)}, s32[32]{0:T(128)}, u32[]{:S(2)}) copy-start(s32[32]{0:T(128)} %copy-done.67) | copy-start | bytes 388
  196.8 11.1 %copy-start.74 = (f32[32]{0:T(128)S(1)}, f32[32]{0:T(128)}, u32[]{:S(2)}) copy-start(f32[32]{0:T(128)} %fusion.145) | copy-start | bytes 388
  215.4 16.3 %copy-start.11 = (f32[32,4,64,64]{3,0,2,1:T(8,128)}, f32[32,4,64,64]{3,0,2,1:T(8,128)S(1)}, u32[]{:S(2)}) copy-start(f32[32,4,64,64]{3,0,2,1:T(8,128)S(1)} %multiply_add_fusion) | copy-start | bytes 6291460
  215.4 16.3 %copy-start.59 = (f32[4,64]{1,0:T(4,128)S(1)}, f32[4,64]{1,0:T(4,128)}, u32[]{:S(2)}) copy-start(f32[4,64]{1,0:T(4,128)} %get-tuple-element.314) | copy-start | bytes 3076
  215.4 23.8 %copy-start.63 = (pred[64,64]{0,1:T(8,128)(4,1)S(1)}, pred[64,64]{0,1:T(8,128)(4,1)}, u32[]{:S(2)}) copy-start(pred[64,64]{0,1:T(8,128)(4,1)} %iota_compare_fusion) | copy-start | bytes 12292
  247.4 13.5 %copy-start.51 = (f32[32,64]{1,0:T(8,128)S(1)}, f32[32,64]{1,0:T(8,128)}, u32[]{:S(2)}) copy-start(f32[32,64]{1,0:T(8,128)} %get-tuple-element.436) | copy-start | bytes 24580
  247.4 13.5 %copy-start.18 = (bf16[32,64,4,64]{3,1,2,0:T(8,128)(2,1)S(1)}, bf16[32,64,4,64]{3,1,2,0:T(8,128)(2,1)}, u32[]{:S(2)}) copy-start(bf16[32,64,4,64]{3,1,2,0:T(8,128)(2,1)} %copy.220) | copy-start | bytes 3145732
  247.4 13.5 %copy-start.25 = (f32[32,64,4,64]{1,0,3,2:T(8,128)S(1)}, f32[32,64,4,64]{1,0,3,2:T(8,128)}, u32[]{:S(2)}) copy-start(f32[32,64,4,64]{1,0,3,2:T(8,128)} %reshape_reshape.3) | copy-start | bytes 6291460
  261.0 41.2 %copy-start.48 = (f32[32,64,4]{1,2,0:T(4,128)}, f32[32,64,4]{1,2,0:T(4,128)S(1)}, u32[]{:S(2)}) copy-start(f32[32,64,4]{1,2,0:T(4,128)S(1)} %fusion.132) | copy-start | bytes 98308
  267.1 12.7 %copy-start.39 = (f32[32,4,64]{2,0,1:T(8,128)S(1)}, f32[32,4,64]{2,0,1:T(8,128)}, u32[]{:S(2)}) copy-start(f32[32,4,64]{2,0,1:T(8,128)} %copy-done.38) | copy-start | bytes 98308
  267.2 13.4 %copy-start.5 = (f32[32,64,4,64]{1,0,3,2:T(8,128)S(1)}, f32[32,64,4,64]{1,0,3,2:T(8,128)}, u32[]{:S(2)}) copy-start(f32[32,64,4,64]{1,0,3,2:T(8,128)} %reshape.334) | copy-start | bytes 6291460
  290.1 12.1 %copy-start.26 = (f32[32,64,4,64]{1,0,3,2:T(8,128)S(1)}, f32[32,64,4,64]{1,0,3,2:T(8,128)}, u32[]{:S(2)}) copy-start(f32[32,64,4,64]{1,0,3,2:T(8,128)} %reshape_reshape.3) | copy-start | bytes 6291460
  316.2 9.8 copy-start.66
  316.2 9.7 copy-start.69
  367.8 11.9 %copy-start.12 = (f32[32,4,64,64]{3,2,1,0:T(8,128)S(1)}, f32[32,4,64,64]{3,2,1,0:T(8,128)}, u32[]{:S(2)}) copy-start(f32[32,4,64,64]{3,2,1,0:T(8,128)} %fusion.42) | copy-start | bytes 6291460
  367.8 11.9 %copy-start.19 = (bf16[32,64,4,64]{3,1,2,0:T(8,128)(2,1)S(1)}, bf16[32,64,4,64]{3,1,2,0:T(8,128)(2,1)}, u32[]{:S(2)}) copy-start(bf16[32,64,4,64]{3,1,2,0:T(8,128)(2,1)} %copy.220) | copy-start | bytes 3145732
  367.8 11.9 %copy-start.54 = (f32[32,64]{1,0:T(8,128)S(1)}, f32[32,64]{1,0:T(8,128)}, u32[]{:S(2)}) copy-start(f32[32,64]{1,0:T(8,128)} %get-tuple-element.412) | copy-start | bytes 24580
  533.0 23.5 %copy-start.47 = (bf16[2048,1024]{1,0:T(8,128)(2,1)S(1)}, bf16[2048,1024]{1,0:T(8,128)(2,1)}, u32[]{:S(2)}) copy-start(bf16[2048,1024]{1,0:T(8,128)(2,1)} %param.29) | copy-start | bytes 12582916
  533.0 23.5 %copy-start.75 = (bf16[1024,1024]{1,0:T(8,128)(2,1)S(1)}, bf16[1024,1024]{1,0:T(8,128)(2,1)}, u32[]{:S(2)}) copy-start(bf16[1024,1024]{1,0:T(8,128)(2,1)} %param.25) | copy-start | bytes 6291460
  575.2 144.7 %reduce-scatter.7.cloned.1.call-start = ((), (), s32[]{:S(2)}) async-start(), calls=%async_computation.6 | async-start | bytes 10485760 | tf_op jit(solution)/shard_map/reduce_scatter | solution.py:191
  595.6 192.2 %reduce-scatter.13.cloned.1.call-start = ((), (), s32[]{:S(2)}) async-start(), calls=%async_computation.9 | async-start | bytes 1179648 | tf_op jit(solution)/shard_map/reduce_scatter | solution.py:259
  600.6 265.0 %reduce-scatter.11.cloned.1.call-start = ((), (), s32[]{:S(2)}) async-start(), calls=%async_computation.8 | async-start | bytes 3538944 | tf_op jit(solution)/shard_map/reduce_scatter | solution.py:258
  609.2 347.9 %reduce-scatter.15.cloned.1.call-start = ((), (), s32[]{:S(2)}) async-start(), calls=%async_computation.10 | async-start | bytes 4718592 | tf_op jit(solution)/shard_map/reduce_scatter | solution.py:260
  619.6 429.7 %reduce-scatter.17.cloned.1.call-start = ((), (), s32[]{:S(2)}) async-start(), calls=%async_computation.11 | async-start | bytes 4718592 | tf_op jit(solution)/shard_map/reduce_scatter | solution.py:261
  630.2 14.5 %copy-start.62 = (f32[1024]{0:T(1024)S(1)}, f32[1024]{0:T(1024)}, u32[]{:S(2)}) copy-start(f32[1024]{0:T(1024)} %param.18) | copy-start | bytes 12292
  647.7 72.1 %copy-start.72 = (f32[1024]{0:T(1024)S(1)}, f32[1024]{0:T(1024)}, u32[]{:S(2)}) copy-start(f32[1024]{0:T(1024)} %param.26) | copy-start | bytes 12292
  (56 other events, 270.2 us)
Sparse Core Ops, SparseCore 0:
  575.3 69.3 reduce-scatter.8
  647.4 72.3 reduce-scatter.6
  723.8 63.8 reduce-scatter.12
  792.2 73.3 reduce-scatter.10
  870.0 86.9 reduce-scatter.14
  961.1 88.0 reduce-scatter.16
where the time goes:
time: 1070 us; the launch traced here: 1060 us
  waiting for transfers between devices  360 us (34%)
  matrix products  308 us (29%)
  blocking collectives  184 us (17%)
  local copies, waits for them, and re-layouts  99.3 us (9%)
  other arithmetic  77.5 us (7%)
  between operations  17 us (2%)
    all_gather x4, blocking collectives, entering(): everything = jax.tree.map(lambda part: lax.all_gather(part, axis), shard)  122 us
    reduce_scatter x1, waiting for transfers between devices, per_device(): lax.psum_scatter(grad_down_w, 'batch', scatter_dimension=1, tiled=True)  92.2 us
    reduce_scatter x1, waiting for transfers between devices, per_device(): lax.psum_scatter(grad_up_w, 'batch', scatter_dimension=0, tiled=True)  91.5 us
    reduce_scatter x1, waiting for transfers between devices, per_device(): lax.psum_scatter(grad_qkv_w, 'batch', scatter_dimension=0, tiled=True)  77.8 us
    reduce_scatter x1, waiting for transfers between devices, per_device(): lax.psum_scatter(grad_out_w, 'batch', scatter_dimension=1, tiled=True)  64.2 us
    psum x1, blocking collectives, per_device(): lax.psum((gain_part, shift_part, out_bias_part, qkv_bias_full, up_bias_fu...  40.6 us
    select_n x32, other arithmetic, turn(): return jax.tree.map(lambda a, b: jnp.where(reached, a, b), new, before)  28.9 us
    reduce_scatter x1, waiting for transfers between devices, per_device(): lax.psum_scatter(jnp.dot(mixed_rows, out_weight, preferred_element_type=f...  27.5 us
  transfers between devices with their start and end apart: 6, of which 6 were waited for; matrix products, arithmetic and copies ran while one was open for 7% of the time, Pallas kernels for 0%

commit v1 on v0

v1 whole, which is shorter than its diff:
```python
import math

import numpy as np

import jax
import jax.numpy as jnp
from jax import lax
from jax.experimental import pallas as pl
from jax.experimental.pallas import tpu as pltpu
from jax.sharding import PartitionSpec as P

ROT = 16
CHUNK = 256
ROWS = 512
LANE = 128
epsilon = 1e-05
f32 = jnp.float32
bf16 = jnp.bfloat16
HALF_ROOT = math.sqrt(0.5)
GAUSS = 1.0 / math.sqrt(2.0 * math.pi)
VMEM_BYTES = 60 * 2**20


def nn(a, b):
    return lax.dot_general(a, b, (((1,), (0,)), ((), ())), preferred_element_type=f32)


def nt(a, b):
    return lax.dot_general(a, b, (((1,), (1,)), ((), ())), preferred_element_type=f32)


def tn(a, b):
    return lax.dot_general(a, b, (((0,), (0,)), ((), ())), preferred_element_type=f32)


def two(value):
    high = value.astype(bf16)
    return high, (value - high.astype(f32)).astype(bf16)


def exact3(dot, a, b):
    return dot(a[0], b[0]) + (dot(a[1], b[0]) + dot(a[0], b[1]))


def params(flops, moved, exps=0):
    return {
        "compiler_params": pltpu.CompilerParams(vmem_limit_bytes=VMEM_BYTES),
        "cost_estimate": pl.CostEstimate(
            flops=int(flops), bytes_accessed=int(moved), transcendentals=int(exps)
        ),
    }


def whole(*shape):
    return pl.BlockSpec(shape, lambda *ids: (0,) * len(shape))


SMEM = pl.BlockSpec(memory_space=pltpu.SMEM)


def dct_table(size):
    row = np.arange(size)[:, None]
    col = np.arange(size)[None, :]
    table = np.cos(math.pi * (col + 0.5) * row / size) * math.sqrt(2.0 / size)
    table[0] *= math.sqrt(0.5)
    return table.astype(np.float32)


def expand_table(head):
    half = ROT // 2
    table = np.zeros((ROT, 3 * LANE), np.float32)
    for lane in range(LANE):
        place = lane % head
        if place < half:
            table[place, lane] = 1.0
            table[half + place, LANE + lane] = -1.0
        elif place < ROT:
            table[place - half, lane] = 1.0
            table[place, 2 * LANE + lane] = 1.0
    return np.concatenate([table] * 3, axis=0)


def seq_start(info, place):
    start = jnp.zeros_like(place)
    for j in range(info.shape[0] - 4):
        end = info[4 + j]
        start = jnp.where(place >= end, end, start)
    return start


def head_block(head, rows, cols):
    r = lax.broadcasted_iota(jnp.int32, (rows, cols), 0) // head
    c = lax.broadcasted_iota(jnp.int32, (rows, cols), 1) // head
    return r == c


def head_lanes(head, h, width):
    return (lax.broadcasted_iota(jnp.int32, (1, width), 1) // head) == h


def turn_tables(cs, expand, head, width):
    wide = tn(cs, expand)
    lane = lax.broadcasted_iota(jnp.int32, (1, LANE), 1) % head
    cosine = wide[:, :LANE] + jnp.where(lane < ROT, 0.0, 1.0)
    times = width // LANE

    def tile(part):
        return jnp.concatenate([part] * times, axis=1)

    return tile(cosine), tile(wide[:, LANE : 2 * LANE]), tile(wide[:, 2 * LANE :])


def turn(value, tables, sign):
    cosine, up, down = tables
    width = value.shape[1]
    half = ROT // 2
    moved = pltpu.roll(value, width - half, 1) * up + pltpu.roll(value, half, 1) * down
    return value * cosine + moved if sign > 0 else value * cosine - moved


def fold_state(full, head, width):
    block = head_block(head, width, width)
    s_part = jnp.where(block, full[:, :width], 0.0)
    n_part = jnp.where(block, full[:, width:], 0.0)
    s_fold = sum(s_part[:, i * LANE : (i + 1) * LANE] for i in range(width // LANE))
    n_fold = sum(n_part[:, i * LANE : (i + 1) * LANE] for i in range(width // LANE))
    return s_fold + pltpu.roll(n_fold, LANE // 2, 1)


def unfold_state(packed, head, width):
    block = head_block(head, width, width)
    times = width // LANE
    s_part = jnp.concatenate([packed] * times, axis=1)
    n_part = jnp.concatenate([pltpu.roll(packed, LANE // 2, 1)] * times, axis=1)
    return jnp.concatenate([jnp.where(block, s_part, 0.0), jnp.where(block, n_part, 0.0)], axis=1)


def block_at(i, bit, side):
    low = i & ((1 << bit) - 1)
    return ((i >> bit) << (bit + 1)) + low + side * (1 << bit)


def feed_kernel(first, bit, info, x, gain, shift, up_w, up_b, down_w, cot, *refs):
    if first:
        normed_o, hidden_o, gpre_o, send_o, keep_o, ub_o, cb_o, down_acc, up_acc = refs
    else:
        hidden_o, gpre_o, send_o, keep_o, ub_o, down_acc, up_acc = refs
    step = pl.program_id(0)
    rows = cot.shape[0]
    width = up_w.shape[1]

    @pl.when(step == 0)
    def _():
        down_acc[...] = jnp.zeros_like(down_acc)
        up_acc[...] = jnp.zeros_like(up_acc)
        ub_o[...] = jnp.zeros_like(ub_o)
        if first:
            cb_o[...] = jnp.zeros_like(cb_o)

    if first:
        xf = x[...].astype(f32)
        centered = xf - jnp.mean(xf, axis=1, keepdims=True)
        inv = lax.rsqrt(jnp.mean(centered * centered, axis=1, keepdims=True) + epsilon)
        normed = (centered * inv * gain[...] + shift[...]).astype(bf16)
        normed_o[...] = normed
    else:
        normed = x[...]
    c = cot[...]
    pre = nn(normed, up_w[...]) + up_b[...]
    grad_hidden = nt(c, down_w[...])
    phi = 0.5 + 0.5 * lax.erf(pre * HALF_ROOT)
    hidden = (pre * phi).astype(bf16)
    hidden_o[...] = hidden
    down_acc[...] += tn(hidden, c)
    slope = phi + pre * jnp.exp(-0.5 * pre * pre) * GAUSS
    gpre = (grad_hidden * slope).astype(bf16)
    gpre_o[...] = gpre
    up_acc[...] += tn(normed, gpre)
    ub_o[...] += jnp.sum(gpre.astype(f32).reshape(rows // 8, 8, width), axis=0)
    if first:
        cb_o[...] += jnp.sum(c.astype(f32).reshape(rows // 8, 8, c.shape[1]), axis=0)

    @pl.when(step == pl.num_programs(0) - 1)
    def _():
        mine = info[1]
        for out, side in ((send_o, 1 - mine), (keep_o, mine)):
            for i in range(out.shape[0]):
                at = pl.multiple_of(block_at(i, bit, side) * LANE, LANE)
                out[i, :width, :] = down_acc[:, pl.ds(at, LANE)]
                for j in range(width // LANE):
                    out[i, width + j * LANE : width + (j + 1) * LANE, :] = up_acc[
                        pl.ds(at, LANE), j * LANE : (j + 1) * LANE
                    ]


def feed(part, bit, info, x, gain, shift, up_w, up_b, down_w, cot):
    first = part == 0
    tokens, model = cot.shape
    width = up_w.shape[1] // 2
    blocks = model // LANE // 2
    row = lambda n: pl.BlockSpec((ROWS, n), lambda i: (i, 0))
    piece = jax.ShapeDtypeStruct((blocks, width + (width // LANE) * LANE, LANE), f32)
    shapes = [
        jax.ShapeDtypeStruct((tokens, width), bf16),
        jax.ShapeDtypeStruct((tokens, width), bf16),
        piece,
        piece,
        jax.ShapeDtypeStruct((8, width), f32),
    ]
    specs = [row(width), row(width), whole(*piece.shape), whole(*piece.shape), whole(8, width)]
    if first:
        shapes = [jax.ShapeDtypeStruct((tokens, model), bf16), *shapes]
        specs = [row(model), *specs, whole(8, model)]
        shapes.append(jax.ShapeDtypeStruct((8, model), f32))

    def body(*refs):
        feed_kernel(first, bit, *refs)

    return pl.pallas_call(
        body,
        grid=(tokens // ROWS,),
        in_specs=[
            SMEM,
            row(model),
            whole(1, model),
            whole(1, model),
            pl.BlockSpec((model, width), lambda i: (0, part)),
            pl.BlockSpec((1, width), lambda i: (0, part)),
            pl.BlockSpec((width, model), lambda i: (part, 0)),
            row(model),
        ],
        out_specs=specs,
        out_shape=shapes,
        scratch_shapes=[pltpu.VMEM((width, model), f32), pltpu.VMEM((model, width), f32)],
        name="feed_forward",
        **params(8 * tokens * model * width, 16 * tokens * model, 2 * tokens * width),
    )(info, x, gain, shift, up_w, up_b, down_w, cot)


def project_kernel(
    head, info, normed, w_in, b_in, cs, expand, samples, dct_t, cot, out_w,
    qf_o, kf_o, v_o, qt_o, kt_o, ga_o, w_o, basis_o, state_o, w_s, b_s, basis_s, state_s,
):
    step = pl.program_id(0)
    width = out_w.shape[0]
    heads = width // head
    rows = normed.shape[0]

    @pl.when(step == 0)
    def _():
        for part in range(3):
            at = [(3 * h + part) * head for h in range(heads)]
            w_s[:, part * width : (part + 1) * width] = jnp.concatenate(
                [w_in[:, a : a + head] for a in at], axis=1
            )
            b_s[:, part * width : (part + 1) * width] = jnp.concatenate(
                [b_in[:, a : a + head] for a in at], axis=1
            )
        basis = lax.dot_general(
            dct_t[...], samples[...], (((1,), (1,)), ((), ())),
            preferred_element_type=f32, precision=lax.Precision.HIGHEST,
        )
        basis = basis * (1.0 / head**0.25)
        wide = jnp.concatenate([jnp.concatenate([basis] * heads, axis=1)] * heads, axis=0)
        basis_s[...] = jnp.where(head_block(head, width, width), wide, 0.0)
        basis_o[...] = basis_s[...]
        w_o[...] = w_s[...]
        state_s[...] = jnp.zeros_like(state_s)

    projected = (nn(normed[...], w_s[...]) + b_s[...]).astype(bf16)
    tables = turn_tables(cs[...], expand[...], head, width)
    basis = two(basis_s[...])
    ones = jnp.where(head_block(head, width, width), 1.0 / (2.0 * math.sqrt(head)), 0.0).astype(bf16)

    def features(part):
        turned = turn(part.astype(f32), tables, 1)
        square = two(turned * turned)
        argument = exact3(nn, two(turned), basis) - (nn(square[0], ones) + nn(square[1], ones))
        return turned.astype(bf16), (jnp.exp(argument) * (1.0 / math.sqrt(samples.shape[0]))).astype(bf16)

    k_turn, k_feat = features(projected[:, width : 2 * width])
    value = projected[:, 2 * width :]
    q_turn, q_feat = features(projected[:, :width])
    qf_o[...], kf_o[...], v_o[...], qt_o[...], kt_o[...] = q_feat, k_feat, value, q_turn, k_turn
    ga_o[...] = nt(cot[...], out_w[...])
    place = info[0] + step * rows + lax.broadcasted_iota(jnp.int32, (rows, 1), 0)
    tail = jnp.where(place >= info[2], 1.0, 0.0).astype(bf16)
    state_s[...] += tn(k_feat * tail, jnp.concatenate([value, jnp.ones_like(value)], axis=1))

    @pl.when(step == pl.num_programs(0) - 1)
    def _():
        state_o[...] = fold_state(state_s[...], head, width)


def project(head, info, normed, w_in, b_in, cs, expand, samples, dct_t, cot, out_w):
    tokens, model = normed.shape
    width = out_w.shape[0]
    row = lambda n: pl.BlockSpec((ROWS, n), lambda i: (i, 0))
    narrow = jax.ShapeDtypeStruct((tokens, width), bf16)

    def body(*refs):
        project_kernel(head, *refs)

    return pl.pallas_call(
        body,
        grid=(tokens // ROWS,),
        in_specs=[
            SMEM,
            row(model),
            whole(*w_in.shape),
            whole(*b_in.shape),
            pl.BlockSpec((cs.shape[0], ROWS), lambda i: (0, i)),
            whole(*expand.shape),
            whole(*samples.shape),
            whole(*dct_t.shape),
            row(model),
            whole(*out_w.shape),
        ],
        out_specs=[row(width)] * 6
        + [whole(*w_in.shape), whole(width, width), whole(width, LANE)],
        out_shape=[narrow] * 5
        + [
            jax.ShapeDtypeStruct((tokens, width), f32),
            jax.ShapeDtypeStruct(w_in.shape, bf16),
            jax.ShapeDtypeStruct((width, width), f32),
            jax.ShapeDtypeStruct((width, LANE), f32),
        ],
        scratch_shapes=[
            pltpu.VMEM(w_in.shape, bf16),
            pltpu.VMEM(b_in.shape, f32),
            pltpu.VMEM((width, width), f32),
            pltpu.VMEM((width, 2 * width), f32),
        ],
        name="project",
        **params(8 * tokens * model * width + 20 * tokens * width * width, 16 * tokens * model, 2 * tokens * width),
    )(info, normed, w_in, b_in, cs, expand, samples, dct_t, cot, out_w)


def turned_grad(grad_feat, feat, turned, basis, tables, head, width):
    weighted = two(grad_feat * feat.astype(f32))
    ones = jnp.where(head_block(head, width, width), 1.0 / math.sqrt(head), 0.0).astype(bf16)
    total = nn(weighted[0], ones) + nn(weighted[1], ones)
    grad = exact3(nt, weighted, basis) - total * turned.astype(f32)
    return turn(grad, tables, -1).astype(bf16)


def attend_kernel(
    head, bit, per_step, info, qf, kf, v, qt, ga, cs, expand, basis_i, state_i, normed, cot,
    mixed_o, gq_o, gk_o, gv_o, back_o, total_o, send_o, keep_o, qb_o, state_s, q_acc, o_acc, total_s,
):
    step = pl.program_id(0)
    width = qf.shape[1]
    heads = width // head

    @pl.when(step == 0)
    def _():
        state_s[...] = unfold_state(state_i[...], head, width)
        q_acc[...] = jnp.zeros_like(q_acc)
        o_acc[...] = jnp.zeros_like(o_acc)
        total_s[...] = jnp.zeros_like(total_s)
        qb_o[...] = jnp.zeros_like(qb_o)

    basis = two(basis_i[...])
    block = head_block(head, width, width)
    both = jnp.concatenate([block, block], axis=1)
    ones = jnp.where(block, 1.0, 0.0).astype(bf16)
    lanes = [jnp.where(head_lanes(head, h, width), 1.0, 0.0).astype(bf16) for h in range(heads)]
    state = state_s[...]
    total = total_s[...]
    for sub in range(per_step):
        at = slice(sub * CHUNK, (sub + 1) * CHUNK)
        begin = info[0] + (step * per_step + sub) * CHUNK
        last = seq_start(info, begin + CHUNK - 1)
        row = lax.broadcasted_iota(jnp.int32, (CHUNK, 1), 0)
        start = seq_start(info, begin + row)
        col = lax.broadcasted_iota(jnp.int32, (CHUNK, CHUNK), 1)
        window = (col <= lax.broadcasted_iota(jnp.int32, (CHUNK, CHUNK), 0)) & (col + begin >= start)
        carried = jnp.where(start < begin, 1.0, 0.0)
        q, k, value = qf[at, :], kf[at, :], v[at, :]
        state_two = two(state)
        from_state = nn(q, state_two[0]) + nn(q, state_two[1])
        sums = carried * from_state
        scores = []
        for h in range(heads):
            score = jnp.where(window, nt(q * lanes[h], k), 0.0).astype(bf16)
            scores.append(score)
            right = jnp.concatenate([value * lanes[h], jnp.broadcast_to(lanes[h], value.shape)], axis=1)
            sums = sums + nn(score, right)
        over = 1.0 / sums[:, width:]
        attended = sums[:, :width] * over
        mixed = attended.astype(bf16)
        mixed_o[at, :] = mixed
        grad_att = ga[at, :]
        g_num = grad_att * over
        product = two(grad_att * attended)
        g_den = -(nn(product[0], ones) + nn(product[1], ones)) * over
        g_low = g_num.astype(bf16)
        g_both = two(jnp.concatenate([g_num, g_den * (1.0 / head)], axis=1))
        grad_fq = carried * exact3(nt, g_both, state_two)
        grad_fk = jnp.zeros((CHUNK, width), f32)
        grad_v = jnp.zeros((CHUNK, width), f32)
        for h in range(heads):
            g_head = g_low * lanes[h]
            mixing = nt(g_head, value) + g_den[:, h * head : h * head + 1]
            mixing = jnp.where(window, mixing, 0.0).astype(bf16)
            grad_fq = grad_fq + nn(mixing, k * lanes[h])
            grad_fk = grad_fk + tn(mixing, q * lanes[h])
            grad_v = grad_v + tn(scores[h], g_head)
        gk_o[at, :] = grad_fk
        gv_o[at, :] = grad_v
        carried_g = (carried * jnp.concatenate([g_num, g_den], axis=1)).astype(bf16)
        back = tn(q, carried_g)
        back_o[sub] = fold_state(back, head, width)
        live = jnp.where(seq_start(info, begin - 1) < info[0], 1.0, 0.0)
        total = total + live * back
        tail = jnp.where(begin + row >= last, 1.0, 0.0).astype(bf16)
        retain = jnp.where(last < begin, 1.0, 0.0)
        added = tn(k * tail, jnp.concatenate([value, jnp.ones_like(value)], axis=1))
        state = retain * state + jnp.where(both, added, 0.0)
        tables = turn_tables(cs[:, at], expand[...], head, width)
        gq = turned_grad(grad_fq, q, qt[at, :], basis, tables, head, width)
        gq_o[at, :] = gq
        qb_o[...] += jnp.sum(gq.astype(f32).reshape(CHUNK // 8, 8, width), axis=0)
        q_acc[...] += tn(normed[at, :], gq)
        o_acc[...] += tn(mixed, cot[at, :])
    state_s[...] = state
    total_s[...] = total

    @pl.when(step == pl.num_programs(0) - 1)
    def _():
        total_o[...] = fold_state(total, head, width)
        mine = info[1]
        for out, side in ((send_o, 1 - mine), (keep_o, mine)):
            for i in range(out.shape[0]):
                spot = pl.multiple_of(block_at(i, bit, side) * LANE, LANE)
                out[i, :width, :] = o_acc[:, pl.ds(spot, LANE)]
                for j in range(width // LANE):
                    out[i, width + j * LANE : width + (j + 1) * LANE, :] = q_acc[
                        pl.ds(spot, LANE), j * LANE : (j + 1) * LANE
                    ]


def attend(head, bit, info, qf, kf, v, qt, ga, cs, expand, basis, state, normed, cot):
    tokens, width = qf.shape
    model = cot.shape[1]
    per_step = 2
    rows = per_step * CHUNK
    chunks = tokens // CHUNK
    row = lambda n: pl.BlockSpec((rows, n), lambda i: (i, 0))
    piece = jax.ShapeDtypeStruct((model // LANE // 2, 2 * width, LANE), f32)

    def body(*refs):
        attend_kernel(head, bit, per_step, *refs)

    return pl.pallas_call(
        body,
        grid=(tokens // rows,),
        in_specs=[
            SMEM,
            *[row(width)] * 5,
            pl.BlockSpec((cs.shape[0], rows), lambda i: (0, i)),
            whole(*expand.shape),
            whole(width, width),
            whole(width, LANE),
            row(model),
            row(model),
        ],
        out_specs=[
            *[row(width)] * 4,
            pl.BlockSpec((per_step, width, LANE), lambda i: (i, 0, 0)),
            whole(width, LANE),
            whole(*piece.shape),
            whole(*piece.shape),
            whole(8, width),
        ],
        out_shape=[
            jax.ShapeDtypeStruct((tokens, width), bf16),
            jax.ShapeDtypeStruct((tokens, width), bf16),
            jax.ShapeDtypeStruct((tokens, width), f32),
            jax.ShapeDtypeStruct((tokens, width), f32),
            jax.ShapeDtypeStruct((chunks, width, LANE), f32),
            jax.ShapeDtypeStruct((width, LANE), f32),
            piece,
            piece,
            jax.ShapeDtypeStruct((8, width), f32),
        ],
        scratch_shapes=[
            pltpu.VMEM((width, 2 * width), f32),
            pltpu.VMEM((model, width), f32),
            pltpu.VMEM((width, model), f32),
            pltpu.VMEM((width, 2 * width), f32),
        ],
        name="attend",
        **params(4 * tokens * model * width + 120 * tokens * width * width, 20 * tokens * width + 4 * tokens * model),
    )(info, qf, kf, v, qt, ga, cs, expand, basis, state, normed, cot)


def keys_kernel(
    head, bit, per_step, info, kf, v, kt, gk, gv, back, cs, expand, basis_i, state_i, normed,
    gkv_o, send_o, keep_o, kvb_o, state_s, acc,
):
    step = pl.program_id(0)
    width = kf.shape[1]

    @pl.when(step == 0)
    def _():
        state_s[...] = unfold_state(state_i[...], head, width)
        acc[...] = jnp.zeros_like(acc)
        kvb_o[...] = jnp.zeros_like(kvb_o)

    basis = two(basis_i[...])
    state = state_s[...]
    for sub in reversed(range(per_step)):
        at = slice(sub * CHUNK, (sub + 1) * CHUNK)
        begin = info[0] + ((pl.num_programs(0) - 1 - step) * per_step + sub) * CHUNK
        last = seq_start(info, begin + CHUNK - 1)
        row = lax.broadcasted_iota(jnp.int32, (CHUNK, 1), 0)
        tail = jnp.where(begin + row >= last, 1.0, 0.0)
        k, value = kf[at, :], v[at, :]
        state_two = two(state)
        right = jnp.concatenate([value, jnp.full(value.shape, 1.0 / head, bf16)], axis=1)
        grad_fk = gk[at, :] + tail * (nt(right, state_two[0]) + nt(right, state_two[1]))
        grad_v = gv[at, :] + tail * (
            nn(k, state_two[0][:, :width]) + nn(k, state_two[1][:, :width])
        )
        retain = jnp.where(last < begin, 1.0, 0.0)
        state = unfold_state(back[sub], head, width) + retain * state
        tables = turn_tables(cs[:, at], expand[...], head, width)
        grad_k = turned_grad(grad_fk, k, kt[at, :], basis, tables, head, width)
        both = jnp.concatenate([grad_k, grad_v.astype(bf16)], axis=1)
        gkv_o[at, :] = both
        kvb_o[...] += jnp.sum(both.astype(f32).reshape(CHUNK // 8, 8, 2 * width), axis=0)
        acc[...] += tn(normed[at, :], both)
    state_s[...] = state

    @pl.when(step == pl.num_programs(0) - 1)
    def _():
        mine = info[1]
        for out, side in ((send_o, 1 - mine), (keep_o, mine)):
            for i in range(out.shape[0]):
                spot = pl.multiple_of(block_at(i, bit, side) * LANE, LANE)
                for j in range(2 * width // LANE):
                    out[i, j * LANE : (j + 1) * LANE, :] = acc[
                        pl.ds(spot, LANE), j * LANE : (j + 1) * LANE
                    ]


def keys(head, bit, info, kf, v, kt, gk, gv, back, cs, expand, basis, state, normed):
    tokens, width = kf.shape
    model = normed.shape[1]
    per_step = 2
    rows = per_step * CHUNK
    steps = tokens // rows
    row = lambda n: pl.BlockSpec((rows, n), lambda i: (steps - 1 - i, 0))
    piece = jax.ShapeDtypeStruct((model // LANE // 2, 2 * width, LANE), f32)

    def body(*refs):
        keys_kernel(head, bit, per_step, *refs)

    return pl.pallas_call(
        body,
        grid=(steps,),
        in_specs=[
            SMEM,
            *[row(width)] * 5,
            pl.BlockSpec((per_step, width, LANE), lambda i: (steps - 1 - i, 0, 0)),
            pl.BlockSpec((cs.shape[0], rows), lambda i: (0, steps - 1 - i)),
            whole(*expand.shape),
            whole(width, width),
            whole(width, LANE),
            row(model),
        ],
        out_specs=[row(2 * width), whole(*piece.shape), whole(*piece.shape), whole(8, 2 * width)],
        out_shape=[
            jax.ShapeDtypeStruct((tokens, 2 * width), bf16),
            piece,
            piece,
            jax.ShapeDtypeStruct((8, 2 * width), f32),
        ],
        scratch_shapes=[pltpu.VMEM((width, 2 * width), f32), pltpu.VMEM((model, 2 * width), f32)],
        name="keys",
        **params(4 * tokens * model * width + 40 * tokens * width * width, 20 * tokens * width + 2 * tokens * model),
    )(info, kf, v, kt, gk, gv, back, cs, expand, basis, state, normed)


def outward_kernel(hidden0, hidden1, mixed, down_w, out_w, out):
    half = hidden0.shape[1]
    out[...] = (
        nn(hidden0[...], down_w[:half, :]) + nn(hidden1[...], down_w[half:, :])
    ) + nn(mixed[...], out_w[...])


def outward(hidden0, hidden1, mixed, down_w, out_w):
    tokens, half = hidden0.shape
    model = down_w.shape[1]
    row = lambda n: pl.BlockSpec((ROWS, n), lambda i: (i, 0))
    return pl.pallas_call(
        outward_kernel,
        grid=(tokens // ROWS,),
        in_specs=[row(half), row(half), row(mixed.shape[1]), whole(*down_w.shape), whole(*out_w.shape)],
        out_specs=row(model),
        out_shape=jax.ShapeDtypeStruct((tokens, model), f32),
        name="outward",
        **params(2 * tokens * model * (2 * half + mixed.shape[1]), 8 * tokens * model),
    )(hidden0, hidden1, mixed, down_w, out_w)


def inward_kernel(gpre0, gpre1, gq, up_w, qkv_w, out):
    half, width = gpre0.shape[1], gq.shape[1]
    out[...] = (
        nt(gpre0[...], up_w[:, :half]) + nt(gpre1[...], up_w[:, half:])
    ) + nt(gq[...], qkv_w[:, :width])


def inward(gpre0, gpre1, gq, up_w, qkv_w):
    tokens, half = gpre0.shape
    model = up_w.shape[0]
    row = lambda n: pl.BlockSpec((ROWS, n), lambda i: (i, 0))
    return pl.pallas_call(
        inward_kernel,
        grid=(tokens // ROWS,),
        in_specs=[row(half), row(half), row(gq.shape[1]), whole(*up_w.shape), whole(*qkv_w.shape)],
        out_specs=row(model),
        out_shape=jax.ShapeDtypeStruct((tokens, model), f32),
        name="inward",
        **params(2 * tokens * model * (2 * half + gq.shape[1]), 8 * tokens * model),
    )(gpre0, gpre1, gq, up_w, qkv_w)


def close_kernel(info, prior, gkv, qkv_w, x, send_o, keep_o, gain_o, shift_o):
    step = pl.program_id(0)
    steps = pl.num_programs(0)
    width = gkv.shape[1] // 2
    rows, model = prior.shape

    @pl.when(step == 0)
    def _():
        gain_o[...] = jnp.zeros_like(gain_o)
        shift_o[...] = jnp.zeros_like(shift_o)

    grad = prior[...] + nt(gkv[...], qkv_w[:, width:])

    @pl.when(step < steps // 2)
    def _():
        send_o[...] = grad

    @pl.when(step >= steps // 2)
    def _():
        keep_o[...] = grad

    xf = x[...].astype(f32)
    centered = xf - jnp.mean(xf, axis=1, keepdims=True)
    unit = centered * lax.rsqrt(jnp.mean(centered * centered, axis=1, keepdims=True) + epsilon)
    gain_o[...] += jnp.sum((grad * unit).reshape(rows // 8, 8, model), axis=0)
    shift_o[...] += jnp.sum(grad.reshape(rows // 8, 8, model), axis=0)


def close(info, prior, gkv, qkv_w, x, shares):
    tokens, model = prior.shape
    per_share = tokens // shares // CHUNK
    half = shares // 2 * per_share

    def rows_of(i, info):
        other = jnp.where(i < half, 1 - info[3], info[3])
        within = i % half
        return (2 * (within // per_share) + other) * per_share + within % per_share, 0

    row = lambda n: pl.BlockSpec((CHUNK, n), rows_of)
    return pl.pallas_call(
        close_kernel,
        grid_spec=pltpu.PrefetchScalarGridSpec(
            num_scalar_prefetch=1,
            grid=(2 * half,),
            in_specs=[row(model), row(gkv.shape[1]), whole(*qkv_w.shape), row(model)],
            out_specs=[
                pl.BlockSpec((CHUNK, model), lambda i, info: (jnp.minimum(i, half - 1), 0)),
                pl.BlockSpec((CHUNK, model), lambda i, info: (jnp.maximum(i - half, 0), 0)),
                whole(8, model),
                whole(8, model),
            ],
        ),
        out_shape=[
            jax.ShapeDtypeStruct((tokens // 2, model), f32),
            jax.ShapeDtypeStruct((tokens // 2, model), f32),
            jax.ShapeDtypeStruct((8, model), f32),
            jax.ShapeDtypeStruct((8, model), f32),
        ],
        name="close",
        **params(2 * tokens * model * gkv.shape[1], 10 * tokens * model),
    )(info, prior, gkv, qkv_w, x)


def swapped(value, axis, distance):
    size = lax.axis_size(axis)
    return lax.ppermute(value, axis, [(i, i ^ distance) for i in range(size)])


def shifted(value, axis, distance):
    size = lax.axis_size(axis)
    pairs = [(i, i + distance) for i in range(size) if 0 <= i + distance < size]
    return lax.ppermute(value, axis, pairs)


def halve(value, bit, mine):
    blocks = value.shape[0]
    split = value.reshape((blocks >> (bit + 1), 2, 1 << bit) + value.shape[1:])
    pick = lambda side: lax.dynamic_index_in_dim(split, side, 1, keepdims=False).reshape(
        (blocks // 2,) + value.shape[1:]
    )
    return pick(1 - mine), pick(mine)


def reduce_blocks(send, keep, order, low):
    index = lax.axis_index("batch") // low
    bits = list(order)
    first = True
    while bits:
        bit = bits.pop(0)
        place = sum(1 for b in [0, 1, 2] if b < bit and b in bits)
        if not first:
            send, keep = halve(keep, place, (index >> bit) & 1)
        first = False
        keep = keep + swapped(send, "batch", low << bit)
    return keep[0]


def finish(part, dim, low):
    if low == 1:
        return part
    size = lax.axis_size("batch")
    groups = [[j * low + i for i in range(low)] for j in range(size // low)]
    return lax.psum_scatter(
        part, "batch", scatter_dimension=dim, axis_index_groups=groups, tiled=True
    )


def entering(local, first_pos, tokens, start_of, size):
    span, total, k = local, None, 1
    here = start_of(first_pos + tokens - 1)
    before = start_of(first_pos - 1)
    while k < size:
        came = shifted(span, "batch", k)
        reach = first_pos - (k - 1) * tokens
        taken = jnp.where(before < reach, came, 0.0)
        total = taken if total is None else total + taken
        if 2 * k < size:
            span = span + jnp.where(here < reach, came, 0.0)
        k *= 2
    return total


def leaving(local, first_pos, tokens, start_of, size):
    span, total, k = local, None, 1
    while k < size:
        came = shifted(span, "batch", -k)
        far = start_of(first_pos + k * tokens - 1)
        taken = jnp.where(far < first_pos + tokens, came, 0.0)
        total = taken if total is None else total + taken
        if 2 * k < size:
            span = span + jnp.where(far < first_pos, came, 0.0)
        k *= 2
    return total


def per_device(
    inputs, ln_gain, ln_shift, qkv_weight, qkv_bias, out_weight, up_weight, up_bias, down_weight,
    out_bias, feature_samples, lengths, cotangent,
):
    tokens, model = inputs.shape
    head = feature_samples.shape[1]
    width = out_weight.shape[0]
    heads = width // head
    batch = lax.axis_size("batch")
    branch = lax.axis_size("branch")
    batch_pos = lax.axis_index("batch")
    branch_pos = lax.axis_index("branch")
    share = tokens // branch
    low = batch // (model // LANE)
    order = (0, 1, 2)
    block_index = batch_pos // low
    first_pos = batch_pos * tokens
    ends = jnp.cumsum(lengths, dtype=jnp.int32)

    def start_of(place):
        return jnp.max(jnp.where(place >= ends, ends, 0))

    info = jnp.concatenate(
        [
            jnp.stack(
                [
                    first_pos,
                    (block_index >> order[0]) & 1,
                    start_of(first_pos + tokens - 1),
                    branch_pos & 1,
                ]
            ).astype(jnp.int32),
            ends,
        ]
    )
    position = first_pos + jnp.arange(tokens, dtype=jnp.int32)
    begun = jnp.max(jnp.where(position[None, :] >= ends[:, None], ends[:, None], 0), axis=0)
    in_seq_place = (position - begun).astype(f32)
    frequency = 10000.0 ** (-2.0 * jnp.arange(ROT // 2, dtype=f32) / ROT)
    angles = in_seq_place[None, :] * frequency[:, None]
    circle = jnp.concatenate([jnp.cos(angles), jnp.sin(angles)], axis=0)
    level0 = lax.reduce_precision(circle, 8, 7)
    level1 = lax.reduce_precision(circle - level0, 8, 7)
    level2 = circle - level0 - level1
    cs = jnp.concatenate([level0, level1, level2], axis=0).astype(bf16)
    expand = jnp.asarray(expand_table(head), bf16)
    dct_t = jnp.asarray(dct_table(head).T)
    gain = ln_gain.reshape(1, model)
    shift = ln_shift.reshape(1, model)
    up_b = up_bias.reshape(1, -1)

    normed, hidden0, gpre0, send0, keep0, ub0, cb = feed(
        0, order[0], info, inputs, gain, shift, up_weight, up_b, down_weight, cotangent
    )
    qf, kf, value, qt, kt, ga, w_perm, basis, local_state = project(
        head, info, normed, qkv_weight, qkv_bias.reshape(1, -1), cs, expand, feature_samples,
        dct_t, cotangent, out_weight,
    )
    in_state = entering(local_state, first_pos, tokens, start_of, batch)
    hidden1, gpre1, send1, keep1, ub1 = feed(
        1, order[0], info, normed, gain, shift, up_weight, up_b, down_weight, cotangent
    )
    mixed, gq, gk, gv, back, back_total, send2, keep2, qb = attend(
        head, order[0], info, qf, kf, value, qt, ga, cs, expand, basis, in_state, normed, cotangent
    )
    out_state = leaving(back_total, first_pos, tokens, start_of, batch)
    branch_part = outward(hidden0, hidden1, mixed, down_weight, out_weight)
    branch_sum = lax.psum_scatter(branch_part, "branch", scatter_dimension=0, tiled=True)
    prior = inward(gpre0, gpre1, gq, up_weight, w_perm)
    gkv, send3, keep3, kvb = keys(
        head, order[0], info, kf, value, kt, gk, gv, back, cs, expand, basis, out_state, normed
    )
    far, near, gain_part, shift_part = close(info, prior, gkv, w_perm, inputs, branch)

    pair = near + swapped(far, "branch", 1)
    pair = pair.reshape(branch // 2, share, model)
    step = 1
    while step < branch // 2:
        side = (branch_pos >> 1) // step & 1
        other, pair = halve(pair, 0, side)
        pair = pair + swapped(other, "branch", 2 * step)
        step *= 2
    grad_normed = pair.reshape(share, model)

    piece0 = reduce_blocks(send0, keep0, order, low)
    piece1 = reduce_blocks(send1, keep1, order, low)
    piece2 = reduce_blocks(send2, keep2, order, low)
    piece3 = reduce_blocks(send3, keep3, order, low)
    half = hidden0.shape[1]

    def columns(rows):
        count = rows.shape[0] // LANE
        return rows.reshape(count, LANE, LANE).transpose(1, 0, 2).reshape(LANE, count * LANE)

    down_sum = finish(jnp.concatenate([piece0[:half], piece1[:half]], axis=0), 1, low)
    up_sum = finish(jnp.concatenate([columns(piece0[half:]), columns(piece1[half:])], axis=1), 0, low)
    out_sum = finish(piece2[:width], 1, low)

    def by_head(parts):
        rows = parts[0].shape[0]
        stacked = jnp.stack([p.reshape(rows, heads, head) for p in parts], axis=2)
        return stacked.reshape(rows, 3 * width)

    kv_columns = columns(piece3)
    qkv_sum = finish(
        by_head([columns(piece2[width:]), kv_columns[:, :width], kv_columns[:, width:]]), 0, low
    )

    cot_part = jnp.sum(cb, axis=0) * jnp.where(branch_pos == 0, 1.0, 0.0)
    kv_part = jnp.sum(kvb, axis=0)[None]
    qkv_part = by_head([jnp.sum(qb, axis=0)[None], kv_part[:, :width], kv_part[:, width:]])[0]
    up_part = jnp.concatenate([jnp.sum(ub0, axis=0), jnp.sum(ub1, axis=0)])

    def spread(part):
        return lax.dynamic_update_slice_in_dim(
            jnp.zeros((part.shape[0] * branch,), f32), part, branch_pos * part.shape[0], 0
        )

    small = jnp.concatenate(
        [jnp.sum(gain_part, axis=0), jnp.sum(shift_part, axis=0), cot_part, spread(qkv_part), spread(up_part)]
    ).reshape(-1, LANE)
    for axis, size in (("branch", branch), ("batch", batch)):
        step = 1
        while step < size:
            small = small + swapped(small, axis, step)
            step *= 2
    small = small.reshape(-1)
    cuts = np.cumsum([model, model, model, 3 * width * branch])
    gain_grad, shift_grad, out_bias_grad, qkv_bias_grad, up_bias_grad = jnp.split(small, cuts)

    row_start = branch_pos * share
    own_inputs = lax.dynamic_slice_in_dim(inputs, row_start, share, 0).astype(f32)
    own_cot = lax.dynamic_slice_in_dim(cotangent, row_start, share, 0).astype(f32)
    output = (own_inputs + branch_sum + out_bias).astype(bf16)
    centered = own_inputs - jnp.mean(own_inputs, axis=1, keepdims=True)
    own_inv = lax.rsqrt(jnp.mean(centered * centered, axis=1, keepdims=True) + epsilon)
    own_unit = centered * own_inv
    grad_unit = grad_normed * ln_gain
    input_grad = (
        own_inv
        * (
            grad_unit
            - jnp.mean(grad_unit, axis=1, keepdims=True)
            - own_unit * jnp.mean(grad_unit * own_unit, axis=1, keepdims=True)
        )
        + own_cot
    )
    return (
        output,
        input_grad,
        gain_grad,
        shift_grad,
        qkv_sum,
        qkv_bias_grad,
        out_sum,
        up_sum,
        up_bias_grad,
        down_sum,
        out_bias_grad,
    )


def solution(mesh):
    placed = (
        P("batch", None),
        P(),
        P(),
        P(None, "branch"),
        P("branch"),
        P("branch", None),
        P(None, "branch"),
        P("branch"),
        P("branch", None),
        P(),
        P(),
        P(),
        P("batch", None),
    )
    return jax.shard_map(
        per_device,
        mesh=mesh,
        in_specs=placed,
        out_specs=(
            P(("batch", "branch"), None),
            P(("batch", "branch"), None),
            P(),
            P(),
            P("batch", "branch"),
            P(),
            P("branch", "batch"),
            P("batch", "branch"),
            P(),
            P("branch", "batch"),
            P(),
        ),
        check_vma=False,
    )
```

time: 1070 us -> 475 us (0.44); the launches traced: 1060 us -> 474 us
  matrix products: 308 us -> 0 us
  blocking collectives: 184 us -> 0 us
  waiting for transfers between devices: 360 us -> 224 us
  Pallas kernels: 0 us -> 129 us
  local copies, waits for them, and re-layouts: 99.3 us -> 17.7 us
  starting transfers between devices: 0.71 us -> 48.1 us
  other arithmetic: 77.5 us -> 34.4 us
    reduce_scatter x6 -> x1, waiting for transfers between devices: 360 us -> 0.02 us  [per_device(): lax.psum_scatter(branch_part, 'branch', scatter_dimension=0, tiled=True)]
    dot_general x42 -> x0, matrix products: 308 us -> none  [the longest x1 23.5 us: per_device(): pre_act = jnp.dot(normed, up_weight, preferred_element_type=f32) + up_bias]
    ppermute x0 -> x25, waiting for transfers between devices: none -> 224 us  [the longest x19 211 us: swapped(): return lax.ppermute(value, axis, [(i, i ^ distance) for i in range(size)])]
    pallas_call x0 -> x8, Pallas kernels: none -> 129 us  [the longest x2 34.3 us: feed(): pl.pallas_call(body, grid=(tokens // ROWS,), in_specs=[SMEM, row(model),...]
    all_gather x4 -> x0, blocking collectives: 122 us -> none  [entering(): everything = jax.tree.map(lambda part: lax.all_gather(part, axis), shard)]
    ppermute x0 -> x25, starting transfers between devices: none -> 48 us  [the longest x19 28.3 us: swapped(): return lax.ppermute(value, axis, [(i, i ^ distance) for i in range(size)])]
    psum x1 -> x0, blocking collectives: 40.6 us -> none  [per_device(): lax.psum((gain_part, shift_part, out_bias_part, qkv_bias_full, up_bias_fu...]
    select_n x32 -> x0, other arithmetic: 28.9 us -> none  [turn(): return jax.tree.map(lambda a, b: jnp.where(reached, a, b), new, before)]
  transfers between devices with their start and end apart: 6 -> 26, of which waited for: 6 -> 14; matrix products, arithmetic and copies ran while one was open for 7% -> 7% of each run, Pallas kernels for 0% -> 11%
where the time goes in v1:
time: 475 us; the launch traced here: 474 us
  waiting for transfers between devices  224 us (47%)
  Pallas kernels  129 us (27%)
  starting transfers between devices  48.1 us (10%)
  other arithmetic  34.4 us (7%)
  between operations  20.2 us (4%)
  local copies, waits for them, and re-layouts  17.7 us (4%)
    ppermute x19, waiting for transfers between devices, swapped(): return lax.ppermute(value, axis, [(i, i ^ distance) for i in range(size)])  211 us
    pallas_call x2, Pallas kernels, feed(): pl.pallas_call(body, grid=(tokens // ROWS,), in_specs=[SMEM, row(model),...  34.3 us
    pallas_call x1, Pallas kernels, attend(): pl.pallas_call(body, grid=(tokens // rows,), in_specs=[SMEM, *[row(width)...  31.4 us
    ppermute x19, starting transfers between devices, swapped(): return lax.ppermute(value, axis, [(i, i ^ distance) for i in range(size)])  28.3 us
    ppermute x6, starting transfers between devices, shifted(): return lax.ppermute(value, axis, pairs)  19.8 us
    pallas_call x1, Pallas kernels, project(): pl.pallas_call(body, grid=(tokens // ROWS,), in_specs=[SMEM, row(model),...  15.3 us
    pallas_call x1, Pallas kernels, keys(): pl.pallas_call(body, grid=(steps,), in_specs=[SMEM, *[row(width)] * 5, pl...  14 us
    pallas_call x1, Pallas kernels, close(): pl.pallas_call(close_kernel, grid_spec=pltpu.PrefetchScalarGridSpec(num_s...  13.5 us
  transfers between devices with their start and end apart: 26, of which 14 were waited for; matrix products, arithmetic and copies ran while one was open for 7% of the time, Pallas kernels for 11%

profile of v1, /device:TPU:0, one launch (start us, length us, event | category | flops | bytes accessed | tf_op | source)
XLA Modules:
  0.0 473.7 jit_solution(16769937624824078838)
XLA Ops:
  12.5 18.3 %feed_forward.2 = (bf16[2048,1024]{1,0:T(8,128)(2,1)}, bf16[2048,512]{1,0:T(8,128)(2,1)}, bf16[2048,512]{1,0:T(8,128)(2,1)}, f32[4,1024,128]{2,1,0:T(8,128)}, f3...) custom-call(s32[12]{0:T(128)} %concatenate.22.refs_0_.info, bf16[2048,1024]{1,0:T(8,128)(2,1)} %x.1, ...), custom_call_target="tpu_custom_call" | custom-call | flops 8589934592 | bytes 33554432 | tf_op jit(solution)/shard_map/feed_forward/pallas_call | solution.py:219
  30.8 15.3 %project.1 = (bf16[2048,256]{1,0:T(8,128)(2,1)}, bf16[2048,256]{1,0:T(8,128)(2,1)}, bf16[2048,256]{1,0:T(8,128)(2,1)}, bf16[2048,256]{1,0:T(8,128)(2,1)}, bf16[2...) custom-call(s32[12]{0:T(128)} %concatenate.22.refs_0_.info, ...), custom_call_target="tpu_custom_call" | custom-call | flops 6979321856 | bytes 33554432 | tf_op jit(solution)/shard_map/project/pallas_call | solution.py:304
  46.1 4.9 %collective-permute-start = (f32[256,128]{1,0:T(8,128)}, f32[256,128]{1,0:T(8,128)S(1)}, u32[]{:S(2)}, u32[]{:S(2)}) collective-permute-start(f32[256,128]{1,0:T(8,128)} %get-tuple-element.58), channel_id=1, source_target_pairs={{0,4},{4,8},{8,12},{12,16},{16,20},{20,24},{24,28},{1,5},{5,9},{9,... | collective-permute-start | bytes 393224 | tf_op jit(solution)/shard_map/ppermute | solution.py:701
  51.6 2.4 collective-permute-done
  55.0 5.2 %collective-permute-start.1 = (f32[256,128]{1,0:T(8,128)S(1)}, f32[256,128]{1,0:T(8,128)S(1)}, u32[]{:S(2)}, u32[]{:S(2)}) collective-permute-start(f32[256,128]{1,0:T(8,128)S(1)} %select_add_fusion.5), channel_id=1, source_target_pairs={{0,8},{4,12},{8,16},{12,20},{16,24},{20,28},{1,9},{5,13},{9,17},{1... | collective-permute-start | bytes 393224 | tf_op jit(solution)/shard_map/ppermute | solution.py:701
  62.7 5.6 %collective-permute-start.2 = (f32[256,128]{1,0:T(8,128)S(1)}, f32[256,128]{1,0:T(8,128)S(1)}, u32[]{:S(2)}, u32[]{:S(2)}) collective-permute-start(f32[256,128]{1,0:T(8,128)S(1)} %select_add_fusion.4), channel_id=1, source_target_pairs={{0,16},{4,20},{8,24},{12,28},{1,17},{5,21},{9,25},{13,29},{2,18},{... | collective-permute-start | bytes 393224 | tf_op jit(solution)/shard_map/ppermute | solution.py:701
  68.3 15.9 %feed_forward.3 = (bf16[2048,512]{1,0:T(8,128)(2,1)}, bf16[2048,512]{1,0:T(8,128)(2,1)}, f32[4,1024,128]{2,1,0:T(8,128)}, f32[4,1024,128]{2,1,0:T(8,128)}, f32[8,512]{1,0:T(8,128)}) custom-call(s32[12]{0:T(128)} %concatenate.22.refs_0_.info, bf16[2048,1024]{1,0:T(8,128)(2,1)} %get-tuple-element.50.refs_1_.refs_10_.refs_11_, f32[1,1024]{1,0:T(1,128)} %bitcast.112, ...), custom_call_target="tpu_custom_call" | custom-call | flops 8589934592 | bytes 33554432 | tf_op jit(solution)/shard_map/feed_forward/pallas_call | solution.py:219
  86.9 31.4 %attend.1 = (bf16[2048,256]{1,0:T(8,128)(2,1)}, bf16[2048,256]{1,0:T(8,128)(2,1)}, f32[2048,256]{1,0:T(8,128)}, f32[2048,256]{1,0:T(8,128)}, f32[8,256,128]{2,1,...) custom-call(s32[12]{0:T(128)} %concatenate.22.refs_0_.info, ...), custom_call_target="tpu_custom_call" | custom-call | flops 18253611008 | bytes 18874368 | tf_op jit(solution)/shard_map/attend/pallas_call | solution.py:455
  118.3 10.3 %outward.1 = f32[2048,1024]{1,0:T(8,128)} custom-call(bf16[2048,512]{1,0:T(8,128)(2,1)} %get-tuple-element.49.hidden0, bf16[2048,512]{1,0:T(8,128)(2,1)} %get-tuple-element.51.hidden1, bf16[2048,256]{1,0:T(8,128)(2,1)} %get-tuple-element.59.mixed, bf16[1024,1024]{1,0:T(8,128)(2,1)} %down_w.1, bf16[256,1024]{1,0:T(8,128)(2,1)} %out_w.1), custom_call_target="tpu_custom_call" | custom-call | flops 5368709120 | bytes 16777216 | tf_op jit(solution)/shard_map/outward/pallas_call | solution.py:597
  130.7 5.6 %collective-permute-done.3 = f32[256,128]{1,0:T(8,128)S(1)} collective-permute-done((f32[256,128]{1,0:T(8,128)S(1)}, f32[256,128]{1,0:T(8,128)S(1)}, u32[]{:S(2)}, u32[]{:S(2)}) %collective-permute-start.3) | collective-permute-done | bytes 131104 | tf_op jit(solution)/shard_map/ppermute | solution.py:701
  140.2 3.0 collective-permute-done.4
  144.7 10.8 %inward.1.prior = f32[2048,1024]{1,0:T(8,128)} custom-call(bf16[2048,512]{1,0:T(8,128)(2,1)} %get-tuple-element.60.gpre0, bf16[2048,512]{1,0:T(8,128)(2,1)} %get-tuple-element.61.gpre1, bf16[2048,256]{1,0:T(8,128)(2,1)} %get-tuple-element.62.gq, bf16[1024,1024]{1,0:T(8,128)(2,1)} %up_w.1, bf16[1024,768]{1,0:T(8,128)(2,1)} %get-tuple-element.63.qkv_w), custom_call_target="tpu_custom_call" | custom-call | flops 5368709120 | bytes 16777216 | tf_op jit(solution)/shard_map/inward/pallas_call | solution.py:619
  156.3 14.0 %keys.1 = (bf16[2048,512]{1,0:T(8,128)(2,1)}, f32[4,512,128]{2,1,0:T(8,128)}, f32[4,512,128]{2,1,0:T(8,128)}, f32[8,512]{1,0:T(8,128)}) custom-call(s32[12]{0:T(128)} %concatenate.22.refs_0_.info, bf16[2048,256]{1,0:T(8,128)(2,1)} %get-tuple-element.53.refs_2_.refs_1_, bf16[2048,256]{1,0:T(8,128)(2,1)} %get-tuple-element.54.refs_3_.refs_2_, ...), custom_call_target="tpu_custom_call" | custom-call | flops 7516192768 | bytes 14680064 | tf_op jit(solution)/shard_map/keys/pallas_call | solution.py:560
  171.3 13.5 %close.1 = (f32[1024,1024]{1,0:T(8,128)}, f32[1024,1024]{1,0:T(8,128)}, f32[8,1024]{1,0:T(8,128)}, f32[8,1024]{1,0:T(8,128)}) custom-call(s32[12]{0:T(128)} %concatenate.22.refs_0_.info, f32[2048,1024]{1,0:T(8,128)} %inward.1.prior, bf16[2048,512]{1,0:T(8,128)(2,1)} %get-tuple-element.69.gkv, bf16[1024,768]{1,0:T(8,128)(2,1)} %get-tuple-element.63.qkv_w, ...), custom_call_target="tpu_custom_call" | custom-call | flops 2147483648 | bytes 20971520 | tf_op jit(solution)/shard_map/close/pallas_call | solution.py:669
  195.2 66.4 %collective-permute-done.10 = f32[80,128]{1,0:T(8,128)S(1)} collective-permute-done((f32[80,128]{1,0:T(8,128)S(1)}, f32[80,128]{1,0:T(8,128)S(1)}, u32[]{:S(2)}, u32[]{:S(2)}) %collective-permute-start.10) | collective-permute-done | bytes 40992 | tf_op jit(solution)/shard_map/ppermute | solution.py:695
  261.6 2.0 collective-permute-start.11
  265.6 3.7 collective-permute-start.12
  269.3 2.0 collective-permute-done.12
  276.5 2.0 collective-permute-start.14
  279.8 48.2 %collective-permute-done.16 = f32[4,512,128]{2,1,0:T(8,128)} collective-permute-done((f32[4,512,128]{2,1,0:T(8,128)}, f32[4,512,128]{2,1,0:T(8,128)}, u32[]{:S(2)}, u32[]{:S(2)}) %collective-permute-start.16) | collective-permute-done | bytes 1048608 | tf_op jit(solution)/shard_map/ppermute | solution.py:695
  329.4 2.1 collective-permute-start.17
  331.5 3.7 collective-permute-start.15
  338.3 1.9 add.235
  341.6 8.3 %collective-permute-done.17 = f32[2,512,128]{2,1,0:T(8,128)S(1)} collective-permute-done((f32[2,512,128]{2,1,0:T(8,128)S(1)}, f32[2,512,128]{2,1,0:T(8,128)S(1)}, u32[]{:S(2)}, u32[]{:S(2)}) %collective-permute-start.17) | collective-permute-done | bytes 524320 | tf_op jit(solution)/shard_map/ppermute | solution.py:695
  350.0 2.5 collective-permute-start.18
  353.3 44.7 %collective-permute-done.18 = f32[1,512,128]{2,1,0:T(8,128)S(1)} collective-permute-done((f32[1,512,128]{2,1,0:T(8,128)S(1)}, f32[1,512,128]{2,1,0:T(8,128)S(1)}, u32[]{:S(2)}, u32[]{:S(2)}) %collective-permute-start.18) | collective-permute-done | bytes 262176 | tf_op jit(solution)/shard_map/ppermute | solution.py:695
  399.9 4.4 add.210
  408.4 3.4 collective-permute-start.21
  415.9 31.5 %collective-permute-done.21 = f32[1,1024,128]{2,1,0:T(8,128)} collective-permute-done((f32[1,1024,128]{2,1,0:T(8,128)}, f32[1,1024,128]{2,1,0:T(8,128)}, u32[]{:S(2)}, u32[]{:S(2)}) %collective-permute-start.21) | collective-permute-done | bytes 524320 | tf_op jit(solution)/shard_map/ppermute | solution.py:695
  448.6 7.2 %collective-permute-done.24 = f32[1,1024,128]{2,1,0:T(8,128)} collective-permute-done((f32[1,1024,128]{2,1,0:T(8,128)}, f32[1,1024,128]{2,1,0:T(8,128)}, u32[]{:S(2)}, u32[]{:S(2)}) %collective-permute-start.24) | collective-permute-done | bytes 524320 | tf_op jit(solution)/shard_map/ppermute | solution.py:695
  459.4 2.8 fusion.16
  462.2 4.7 fusion.7
  (149 shorter events, 56.1 us)
Async XLA Ops:
  7.2 455.0 %reduce-scatter.2.cloned.1.call-start = ((), (), s32[]{:S(2)}) async-start(), calls=%async_computation.1 | async-start | bytes 10485760 | tf_op jit(solution)/shard_map/reduce_scatter | solution.py:832
  46.1 7.9 %collective-permute-start = (f32[256,128]{1,0:T(8,128)}, f32[256,128]{1,0:T(8,128)S(1)}, u32[]{:S(2)}, u32[]{:S(2)}) collective-permute-start(f32[256,128]{1,0:T(8,128)} %get-tuple-element.58), channel_id=1, source_target_pairs={{0,4},{4,8},{8,12},{12,16},{16,20},{20,24},{24,28},{1,5},{5,9},{9,... | collective-permute-start | bytes 393224 | tf_op jit(solution)/shard_map/ppermute | solution.py:701
  55.0 7.7 %collective-permute-start.1 = (f32[256,128]{1,0:T(8,128)S(1)}, f32[256,128]{1,0:T(8,128)S(1)}, u32[]{:S(2)}, u32[]{:S(2)}) collective-permute-start(f32[256,128]{1,0:T(8,128)S(1)} %select_add_fusion.5), channel_id=1, source_target_pairs={{0,8},{4,12},{8,16},{12,20},{16,24},{20,28},{1,9},{5,13},{9,17},{1... | collective-permute-start | bytes 393224 | tf_op jit(solution)/shard_map/ppermute | solution.py:701
  62.7 23.5 %collective-permute-start.2 = (f32[256,128]{1,0:T(8,128)S(1)}, f32[256,128]{1,0:T(8,128)S(1)}, u32[]{:S(2)}, u32[]{:S(2)}) collective-permute-start(f32[256,128]{1,0:T(8,128)S(1)} %select_add_fusion.4), channel_id=1, source_target_pairs={{0,16},{4,20},{8,24},{12,28},{1,17},{5,21},{9,25},{13,29},{2,18},{... | collective-permute-start | bytes 393224 | tf_op jit(solution)/shard_map/ppermute | solution.py:701
  128.5 11.5 %copy-start.11 = (f32[8,512]{1,0:T(8,128)S(1)}, f32[8,512]{1,0:T(8,128)}, u32[]{:S(2)}) copy-start(f32[8,512]{1,0:T(8,128)} %get-tuple-element.77) | copy-start | bytes 49156
  128.5 11.5 %copy-start.10 = (f32[8,1024]{1,0:T(8,128)S(1)}, f32[8,1024]{1,0:T(8,128)}, u32[]{:S(2)}) copy-start(f32[8,1024]{1,0:T(8,128)} %get-tuple-element.74) | copy-start | bytes 98308
  128.5 11.5 %copy-start.12 = (f32[8,512]{1,0:T(8,128)S(1)}, f32[8,512]{1,0:T(8,128)}, u32[]{:S(2)}) copy-start(f32[8,512]{1,0:T(8,128)} %get-tuple-element.78) | copy-start | bytes 49156
  129.4 6.8 %collective-permute-start.3 = (f32[256,128]{1,0:T(8,128)S(1)}, f32[256,128]{1,0:T(8,128)S(1)}, u32[]{:S(2)}, u32[]{:S(2)}) collective-permute-start(f32[256,128]{1,0:T(8,128)S(1)} %copy-done.9), channel_id=1, source_target_pairs={{4,0},{8,4},{12,8},{16,12},{20,16},{24,20},{28,24},{5,1},{9,5},{13... | collective-permute-start | bytes 393224 | tf_op jit(solution)/shard_map/ppermute | solution.py:701
  136.3 6.9 %collective-permute-start.4 = (f32[256,128]{1,0:T(8,128)S(1)}, f32[256,128]{1,0:T(8,128)S(1)}, u32[]{:S(2)}, u32[]{:S(2)}) collective-permute-start(f32[256,128]{1,0:T(8,128)S(1)} %select_add_fusion.2), channel_id=1, source_target_pairs={{8,0},{12,4},{16,8},{20,12},{24,16},{28,20},{9,1},{13,5},{17,9},{2... | collective-permute-start | bytes 393224 | tf_op jit(solution)/shard_map/ppermute | solution.py:701
  143.2 12.4 %collective-permute-start.5 = (f32[256,128]{1,0:T(8,128)S(1)}, f32[256,128]{1,0:T(8,128)S(1)}, u32[]{:S(2)}, u32[]{:S(2)}) collective-permute-start(f32[256,128]{1,0:T(8,128)S(1)} %select_add_fusion.1), channel_id=1, source_target_pairs={{16,0},{20,4},{24,8},{28,12},{17,1},{21,5},{25,9},{29,13},{18,2},{... | collective-permute-start | bytes 393224 | tf_op jit(solution)/shard_map/ppermute | solution.py:701
  184.8 90.3 %copy-start.7 = (f32[4,512,128]{2,1,0:T(8,128)S(1)}, f32[4,512,128]{2,1,0:T(8,128)}, u32[]{:S(2)}) copy-start(f32[4,512,128]{2,1,0:T(8,128)} %get-tuple-element.79) | copy-start | bytes 3145732
  186.8 1.3 collective-permute-start.8
  186.8 213.0 %collective-permute-start.6 = (f32[1024,1024]{1,0:T(8,128)}, f32[1024,1024]{1,0:T(8,128)}, u32[]{:S(2)}, u32[]{:S(2)}) collective-permute-start(f32[1024,1024]{1,0:T(8,128)} %get-tuple-element.71), channel_id=1, source_target_pairs={{0,1},{1,0},{2,3},{3,2},{4,5},{5,4},{6,7},{7,6},{8,9},{9,8},{10,11... | collective-permute-start | bytes 12582920 | tf_op jit(solution)/shard_map/ppermute | solution.py:695
  188.1 5.0 %collective-permute-start.9 = (f32[80,128]{1,0:T(8,128)S(1)}, f32[80,128]{1,0:T(8,128)S(1)}, u32[]{:S(2)}, u32[]{:S(2)}) collective-permute-start(f32[80,128]{1,0:T(8,128)S(1)} %bitcast_add_fusion.5), channel_id=1, source_target_pairs={{0,2},{1,3},{2,0},{3,1},{4,6},{5,7},{6,4},{7,5},{8,10},{9,11},{10,... | collective-permute-start | bytes 122888 | tf_op jit(solution)/shard_map/ppermute | solution.py:695
  189.5 145.8 %collective-permute-start.19 = (f32[4,1024,128]{2,1,0:T(8,128)}, f32[4,1024,128]{2,1,0:T(8,128)S(1)}, u32[]{:S(2)}, u32[]{:S(2)}) collective-permute-start(f32[4,1024,128]{2,1,0:T(8,128)} %get-tuple-element.84), channel_id=1, source_target_pairs={{0,4},{4,0},{8,12},{12,8},{16,20},{20,16},{24,28},{28,24},{1,5},{5... | collective-permute-start | bytes 6291464 | tf_op jit(solution)/shard_map/ppermute | solution.py:695
  191.1 83.9 %collective-permute-start.13 = (f32[4,512,128]{2,1,0:T(8,128)}, f32[4,512,128]{2,1,0:T(8,128)}, u32[]{:S(2)}, u32[]{:S(2)}) collective-permute-start(f32[4,512,128]{2,1,0:T(8,128)} %get-tuple-element.80), channel_id=1, source_target_pairs={{0,4},{4,0},{8,12},{12,8},{16,20},{20,16},{24,28},{28,24},{1,5},{5... | collective-permute-start | bytes 3145736 | tf_op jit(solution)/shard_map/ppermute | solution.py:695
  193.1 68.5 %collective-permute-start.10 = (f32[80,128]{1,0:T(8,128)S(1)}, f32[80,128]{1,0:T(8,128)S(1)}, u32[]{:S(2)}, u32[]{:S(2)}) collective-permute-start(f32[80,128]{1,0:T(8,128)S(1)} %fusion.18), channel_id=1, source_target_pairs={{0,4},{4,0},{8,12},{12,8},{16,20},{20,16},{24,28},{28,24},{1,5},{5... | collective-permute-start | bytes 122888 | tf_op jit(solution)/shard_map/ppermute | solution.py:695
  194.7 142.0 %collective-permute-start.22 = (f32[4,1024,128]{2,1,0:T(8,128)}, f32[4,1024,128]{2,1,0:T(8,128)}, u32[]{:S(2)}, u32[]{:S(2)}) collective-permute-start(f32[4,1024,128]{2,1,0:T(8,128)} %get-tuple-element.86), channel_id=1, source_target_pairs={{0,4},{4,0},{8,12},{12,8},{16,20},{20,16},{24,28},{28,24},{1,5},{5... | collective-permute-start | bytes 6291464 | tf_op jit(solution)/shard_map/ppermute | solution.py:695
  261.6 4.0 collective-permute-start.11
  265.6 5.7 %collective-permute-start.12 = (f32[80,128]{1,0:T(8,128)S(1)}, f32[80,128]{1,0:T(8,128)S(1)}, u32[]{:S(2)}, u32[]{:S(2)}) collective-permute-start(f32[80,128]{1,0:T(8,128)S(1)} %add.220), channel_id=1, source_target_pairs={{0,16},{4,20},{8,24},{12,28},{16,0},{20,4},{24,8},{28,12},{1,17},{... | collective-permute-start | bytes 122888 | tf_op jit(solution)/shard_map/ppermute | solution.py:695
  271.3 56.7 %collective-permute-start.16 = (f32[4,512,128]{2,1,0:T(8,128)}, f32[4,512,128]{2,1,0:T(8,128)}, u32[]{:S(2)}, u32[]{:S(2)}) collective-permute-start(f32[4,512,128]{2,1,0:T(8,128)} %get-tuple-element.82), channel_id=1, source_target_pairs={{0,4},{4,0},{8,12},{12,8},{16,20},{20,16},{24,28},{28,24},{1,5},{5... | collective-permute-start | bytes 3145736 | tf_op jit(solution)/shard_map/ppermute | solution.py:695
  275.1 52.9 %copy-start.8 = (f32[4,512,128]{2,1,0:T(8,128)S(1)}, f32[4,512,128]{2,1,0:T(8,128)}, u32[]{:S(2)}) copy-start(f32[4,512,128]{2,1,0:T(8,128)} %get-tuple-element.81) | copy-start | bytes 3145732
  276.5 54.9 %collective-permute-start.14 = (f32[2,512,128]{2,1,0:T(8,128)S(1)}, f32[2,512,128]{2,1,0:T(8,128)S(1)}, u32[]{:S(2)}, u32[]{:S(2)}) collective-permute-start(f32[2,512,128]{2,1,0:T(8,128)S(1)} %dynamic-slice_bitcast_fusion.4), channel_id=1, source_target_pairs={{0,8},{4,12},{8,0},{12,4},{16,24},{20,28},{24,16},{28,20},{1,9},{5... | collective-permute-start | bytes 1572872 | tf_op jit(solution)/shard_map/ppermute | solution.py:695
  329.4 20.5 %collective-permute-start.17 = (f32[2,512,128]{2,1,0:T(8,128)S(1)}, f32[2,512,128]{2,1,0:T(8,128)S(1)}, u32[]{:S(2)}, u32[]{:S(2)}) collective-permute-start(f32[2,512,128]{2,1,0:T(8,128)S(1)} %dynamic-slice_bitcast_fusion.3), channel_id=1, source_target_pairs={{0,8},{4,12},{8,0},{12,4},{16,24},{20,28},{24,16},{28,20},{1,9},{5... | collective-permute-start | bytes 1572872 | tf_op jit(solution)/shard_map/ppermute | solution.py:695
  331.5 21.0 %collective-permute-start.15 = (f32[1,512,128]{2,1,0:T(8,128)S(1)}, f32[1,512,128]{2,1,0:T(8,128)S(1)}, u32[]{:S(2)}, u32[]{:S(2)}) collective-permute-start(f32[1,512,128]{2,1,0:T(8,128)S(1)} %constant_dynamic-slice_fusion.3), channel_id=1, source_target_pairs={{0,16},{4,20},{8,24},{12,28},{16,0},{20,4},{24,8},{28,12},{1,17},{... | collective-permute-start | bytes 786440 | tf_op jit(solution)/shard_map/ppermute | solution.py:695
  336.6 61.5 %collective-permute-start.20 = (f32[2,1024,128]{2,1,0:T(8,128)}, f32[2,1024,128]{2,1,0:T(8,128)}, u32[]{:S(2)}, u32[]{:S(2)}) collective-permute-start(f32[2,1024,128]{2,1,0:T(8,128)} %dynamic-slice_bitcast_fusion.2), channel_id=1, source_target_pairs={{0,8},{4,12},{8,0},{12,4},{16,24},{20,28},{24,16},{28,20},{1,9},{5... | collective-permute-start | bytes 3145736 | tf_op jit(solution)/shard_map/ppermute | solution.py:695
  341.3 70.5 %collective-permute-start.23 = (f32[2,1024,128]{2,1,0:T(8,128)}, f32[2,1024,128]{2,1,0:T(8,128)}, u32[]{:S(2)}, u32[]{:S(2)}) collective-permute-start(f32[2,1024,128]{2,1,0:T(8,128)} %dynamic-slice_bitcast_fusion.1), channel_id=1, source_target_pairs={{0,8},{4,12},{8,0},{12,4},{16,24},{20,28},{24,16},{28,20},{1,9},{5... | collective-permute-start | bytes 3145736 | tf_op jit(solution)/shard_map/ppermute | solution.py:695
  350.0 48.0 %collective-permute-start.18 = (f32[1,512,128]{2,1,0:T(8,128)S(1)}, f32[1,512,128]{2,1,0:T(8,128)S(1)}, u32[]{:S(2)}, u32[]{:S(2)}) collective-permute-start(f32[1,512,128]{2,1,0:T(8,128)S(1)} %constant_dynamic-slice_fusion.2), channel_id=1, source_target_pairs={{0,16},{4,20},{8,24},{12,28},{16,0},{20,4},{24,8},{28,12},{1,17},{... | collective-permute-start | bytes 786440 | tf_op jit(solution)/shard_map/ppermute | solution.py:695
  406.8 51.8 %collective-permute-start.7 = (f32[1,512,1024]{2,1,0:T(8,128)}, f32[1,512,1024]{2,1,0:T(8,128)}, u32[]{:S(2)}, u32[]{:S(2)}) collective-permute-start(f32[1,512,1024]{2,1,0:T(8,128)} %dynamic-slice_bitcast_fusion), channel_id=1, source_target_pairs={{0,2},{1,3},{2,0},{3,1},{4,6},{5,7},{6,4},{7,5},{8,10},{9,11},{10,... | collective-permute-start | bytes 6291464 | tf_op jit(solution)/shard_map/ppermute | solution.py:695
  408.4 39.0 %collective-permute-start.21 = (f32[1,1024,128]{2,1,0:T(8,128)}, f32[1,1024,128]{2,1,0:T(8,128)}, u32[]{:S(2)}, u32[]{:S(2)}) collective-permute-start(f32[1,1024,128]{2,1,0:T(8,128)} %constant_dynamic-slice_fusion.1), channel_id=1, source_target_pairs={{0,16},{4,20},{8,24},{12,28},{16,0},{20,4},{24,8},{28,12},{1,17},{... | collective-permute-start | bytes 1572872 | tf_op jit(solution)/shard_map/ppermute | solution.py:695
  414.9 40.8 %collective-permute-start.24 = (f32[1,1024,128]{2,1,0:T(8,128)}, f32[1,1024,128]{2,1,0:T(8,128)}, u32[]{:S(2)}, u32[]{:S(2)}) collective-permute-start(f32[1,1024,128]{2,1,0:T(8,128)} %constant_dynamic-slice_fusion), channel_id=1, source_target_pairs={{0,16},{4,20},{8,24},{12,28},{16,0},{20,4},{24,8},{28,12},{1,17},{... | collective-permute-start | bytes 1572872 | tf_op jit(solution)/shard_map/ppermute | solution.py:695
  415.0 40.7 %copy-start.4 = (f32[2,1024,128]{2,1,0:T(8,128)S(1)}, f32[2,1024,128]{2,1,0:T(8,128)}, u32[]{:S(2)}) copy-start(f32[2,1024,128]{2,1,0:T(8,128)} %copy-done.3) | copy-start | bytes 3145732
  (10 other events, 37.3 us)
Sparse Core Ops, SparseCore 0:
  128.7 70.9 reduce-scatter.1

commit v2 on v0

v2 whole, which is shorter than its diff:
```python
import math

import numpy as np

import jax
import jax.numpy as jnp
from jax import lax
from jax.experimental import pallas as pl
from jax.experimental.pallas import tpu as pltpu
from jax.sharding import PartitionSpec as P

ROT = 16
CHUNK = 256
ROWS = 512
LANE = 128
epsilon = 1e-05
f32 = jnp.float32
bf16 = jnp.bfloat16
HALF_ROOT = math.sqrt(0.5)
GAUSS = 1.0 / math.sqrt(2.0 * math.pi)
VMEM_BYTES = 64 * 2**20
LONG = 2**40
SHORT = 2**35
PARTS = ((3, 1), (0, 3))


def nn(a, b):
    return lax.dot_general(a, b, (((1,), (0,)), ((), ())), preferred_element_type=f32)


def nt(a, b):
    return lax.dot_general(a, b, (((1,), (1,)), ((), ())), preferred_element_type=f32)


def tn(a, b):
    return lax.dot_general(a, b, (((0,), (0,)), ((), ())), preferred_element_type=f32)


def two(value):
    high = value.astype(bf16)
    return high, (value - high.astype(f32)).astype(bf16)


def exact3(dot, a, b):
    return dot(a[0], b[0]) + (dot(a[1], b[0]) + dot(a[0], b[1]))


def beside(*parts):
    return jnp.concatenate(parts, axis=1)


def below(*parts):
    return jnp.concatenate(parts, axis=0)


class Order:
    def __init__(self):
        self.last = ()

    def __call__(
        self, body, args, in_specs, out_specs, out_shape, after=(), through=(), flops=0, **rest
    ):
        given, results = len(args), len(out_shape)
        skipped = [*self.last, *after, *through]

        def without(*refs):
            outs = refs[given + len(skipped) :]
            body(*refs[:given], *outs[:results], *outs[results + len(through) :])

        place = pl.BlockSpec(memory_space=pl.ANY)
        first = given + len(skipped) - len(through)
        outs = pl.pallas_call(
            without,
            in_specs=[*in_specs, *[place] * len(skipped)],
            out_specs=[*out_specs, *[place] * len(through)],
            out_shape=[*out_shape, *[shaped(t.shape, t.dtype) for t in through]],
            input_output_aliases={first + i: results + i for i in range(len(through))},
            compiler_params=pltpu.CompilerParams(vmem_limit_bytes=VMEM_BYTES),
            cost_estimate=pl.CostEstimate(flops=flops, bytes_accessed=0, transcendentals=0),
            **rest,
        )(*args, *skipped)
        self.last = (outs[0],)
        return outs


def hold(call, arrays, after=()):
    def body(out):
        out[...] = jnp.zeros_like(out)

    return call(body, (), [], [whole(8, LANE)], [shaped((8, LANE))], after, arrays, grid=(1,), name="hold")[1:]


def shaped(shape, dtype=f32):
    return jax.ShapeDtypeStruct(tuple(shape), dtype)


def whole(*shape):
    return pl.BlockSpec(shape, lambda *ids: (0,) * len(shape))


def rows_at(rows, width):
    return pl.BlockSpec((rows, width), lambda i: (i, 0))


SMEM = pl.BlockSpec(memory_space=pltpu.SMEM)


def dct_table(size):
    row = np.arange(size)[:, None]
    col = np.arange(size)[None, :]
    table = np.cos(math.pi * (col + 0.5) * row / size) * math.sqrt(2.0 / size)
    table[0] *= math.sqrt(0.5)
    return table.astype(np.float32)


def expand_table(head):
    half = ROT // 2
    table = np.zeros((ROT, 3 * LANE), np.float32)
    for lane in range(LANE):
        place = lane % head
        if place < half:
            table[place, lane] = 1.0
            table[half + place, LANE + lane] = -1.0
        elif place < ROT:
            table[place - half, lane] = 1.0
            table[place, 2 * LANE + lane] = 1.0
    return np.concatenate([table] * 3, axis=0)


def ends_of(lengths):
    ends, total = [], jnp.int32(0)
    for j in range(lengths.shape[0]):
        total = total + lengths[j]
        ends.append(total)
    return ends


def seq_start(ends, place):
    start = jnp.zeros_like(place)
    for end in ends:
        start = jnp.where(place >= end, end, start)
    return start


def iota(shape, dim):
    return lax.broadcasted_iota(jnp.int32, shape, dim)


def head_block(head, rows, cols):
    return iota((rows, cols), 0) // head == iota((rows, cols), 1) // head


def turn_tables(cs, expand, head, width):
    wide = tn(cs, expand)
    lane = iota((1, LANE), 1) % head
    cosine = wide[:, :LANE] + jnp.where(lane < ROT, 0.0, 1.0)
    times = width // LANE
    return tuple(
        beside(*[part] * times) for part in (cosine, wide[:, LANE : 2 * LANE], wide[:, 2 * LANE :])
    )


def turn(value, tables, sign):
    cosine, up, down = tables
    width = value.shape[1]
    half = ROT // 2
    moved = pltpu.roll(value, width - half, 1) * up + pltpu.roll(value, half, 1) * down
    return value * cosine + moved if sign > 0 else value * cosine - moved


def fold_state(full, head, width):
    block = head_block(head, width, width)
    s_part = jnp.where(block, full[:, :width], 0.0)
    n_part = jnp.where(block, full[:, width:], 0.0)
    s_fold = sum(s_part[:, i * LANE : (i + 1) * LANE] for i in range(width // LANE))
    n_fold = sum(n_part[:, i * LANE : (i + 1) * LANE] for i in range(width // LANE))
    return s_fold + pltpu.roll(n_fold, LANE // 2, 1)


def unfold_state(packed, head, width):
    block = head_block(head, width, width)
    times = width // LANE
    s_part = beside(*[packed] * times)
    n_part = beside(*[pltpu.roll(packed, LANE // 2, 1)] * times)
    return beside(jnp.where(block, s_part, 0.0), jnp.where(block, n_part, 0.0))


def deal(outs, order, low, write):
    mine = lax.axis_index("batch") // low
    first, second, third = (1 << bit for bit in order)
    wanted = [base + i * third for base in (first + second, first, second, 0) for i in range(2)]
    slots = [(out, i) for out in outs for i in range(out.shape[0])]
    for (out, i), block in zip(slots, wanted):
        write(out, i, pl.multiple_of((mine ^ block) * LANE, LANE))


def feed_step(normed, c, up_w, up_b, down_w, hidden_o, gpre_o, ub_o, down_acc, up_acc):
    rows, width = hidden_o.shape
    pre = nn(normed, up_w[...]) + up_b[...]
    grad_hidden = nt(c, down_w[...])
    phi = 0.5 + 0.5 * lax.erf(pre * HALF_ROOT)
    hidden = (pre * phi).astype(bf16)
    hidden_o[...] = hidden
    down_acc[...] += tn(hidden, c)
    slope = phi + pre * jnp.exp(-0.5 * pre * pre) * GAUSS
    gpre = (grad_hidden * slope).astype(bf16)
    gpre_o[...] = gpre
    up_acc[...] += tn(normed, gpre)
    ub_o[...] += jnp.sum(gpre.astype(f32).reshape(rows // 8, 8, width), axis=0)


def clear(*refs):
    for ref in refs:
        ref[...] = jnp.zeros_like(ref)


def write_down(out, i, at, down_acc):
    out[i, : down_acc.shape[0], :] = down_acc[:, pl.ds(at, LANE)]


def write_up(out, i, at, up_acc):
    width = up_acc.shape[1]
    first = out.shape[1] - width
    for j in range(0, width, LANE):
        out[i, first + j : first + j + LANE, :] = up_acc[pl.ds(at, LANE), j : j + LANE]


def feed_specs(tokens, model, units, part):
    first, quarters = PARTS[part]
    width = units // 4 * quarters
    part = first // quarters
    ins = [
        pl.BlockSpec((model, width), lambda i: (0, part)),
        pl.BlockSpec((1, width), lambda i: (0, part)),
        pl.BlockSpec((width, model), lambda i: (part, 0)),
        rows_at(ROWS, model),
    ]
    outs = [rows_at(ROWS, width)] * 2 + [whole(8, width)]
    shapes = [shaped((tokens, width), bf16)] * 2 + [shaped((8, width))]
    scratch = [pltpu.VMEM((width, model), f32), pltpu.VMEM((model, width), f32)]
    return width, ins, outs, shapes, scratch


def feed(call, orders, low, normed, up_w, up_b, down_w, cot, **rest):
    tokens, model = cot.shape
    width, ins, outs, shapes, scratch = feed_specs(tokens, model, up_w.shape[1], 1)
    firsts, piece = shaped((4, width, LANE)), shaped((2, width, LANE))
    pieces_out = [firsts, piece, piece] * 2

    def body(normed, up_w, up_b, down_w, cot, hidden_o, gpre_o, ub_o, *refs):
        *pieces, down_acc, up_acc = refs
        step = pl.program_id(0)

        @pl.when(step == 0)
        def _():
            clear(down_acc, up_acc, ub_o)

        feed_step(
            normed[...], cot[...], up_w, up_b, down_w, hidden_o, gpre_o, ub_o, down_acc, up_acc
        )

        @pl.when(step == pl.num_programs(0) - 1)
        def _():
            deal(pieces[:3], orders[0], low, lambda *at: write_down(*at, down_acc))
            deal(pieces[3:], orders[1], low, lambda *at: write_up(*at, up_acc))

    return call(
        body,
        (normed, up_w, up_b, down_w, cot),
        [rows_at(ROWS, model), *ins],
        outs + [whole(*a.shape) for a in pieces_out],
        shapes + pieces_out,
        **rest,
        grid=(tokens // ROWS,),
        scratch_shapes=scratch,
        name="feed_forward",
    )


def take_columns(w_in, head, heads, part):
    return beside(*[w_in[:, (3 * h + part) * head : (3 * h + part + 1) * head] for h in range(heads)])


def features(part, tables, basis, head, feats):
    width = part.shape[1]
    turned = turn(part.astype(f32), tables, 1)
    square = two(turned * turned)
    ones = jnp.where(head_block(head, width, width), 1.0 / (2.0 * math.sqrt(head)), 0.0).astype(bf16)
    argument = exact3(nn, two(turned), basis) - (nn(square[0], ones) + nn(square[1], ones))
    return turned.astype(bf16), (jnp.exp(argument) * (1.0 / math.sqrt(feats))).astype(bf16)


def rotary_table(ends, first_pos, rows, tokens, out):
    half = ROT // 2
    order = iota((half, rows), 0)
    frequency = jnp.zeros((half, rows), f32)
    for j in range(half):
        value = float(np.float32(10000.0) ** np.float32(-2.0 * j / ROT))
        frequency = jnp.where(order == j, value, frequency)
    for i in range(tokens // rows):
        place = first_pos + i * rows + iota((half, rows), 1)
        angle = (place - seq_start(ends, place)).astype(f32) * frequency
        circle = below(jnp.cos(angle), jnp.sin(angle))
        high, rest = two(circle)
        middle, lowest = two(circle - high.astype(f32))
        out[i] = below(high, middle, lowest)


def front(
    call, head, lengths, x, gain, shift, up_w, up_b, down_w, cot, qkv_w, qkv_b, expand,
    samples, dct_t,
):
    tokens, model = x.shape
    width = qkv_w.shape[1] // 3
    heads = width // head
    feats = samples.shape[0]
    blocks = tokens // ROWS
    table = (blocks, expand.shape[0], ROWS)
    part, ins, outs, shapes, scratch = feed_specs(tokens, model, up_w.shape[1], 0)
    piece = shaped((model // LANE, 2 * part, LANE))

    def body(
        lengths, x, gain, shift, up_w, up_b, down_w, cot, qkv_w, qkv_b, expand, samples, dct_t,
        normed_o, cb_o, kf_o, v_o, kt_o, w_o, basis_o, cs_o, state_o, hidden_o, gpre_o, ub_o, piece_o,
        down_acc, up_acc, w_s, b_s, basis_s, cs_s, state_s,
    ):
        step = pl.program_id(0)
        ends = ends_of(lengths)
        first_pos = lax.axis_index("batch") * tokens
        start_last = seq_start(ends, first_pos + tokens - 1)

        @pl.when(step == 0)
        def _():
            clear(down_acc, up_acc, ub_o, cb_o, state_s)
            for part in (1, 2):
                to = slice((part - 1) * width, part * width)
                w_s[:, to] = take_columns(qkv_w, head, heads, part)
                b_s[:, to] = take_columns(qkv_b, head, heads, part)
            basis = lax.dot_general(
                dct_t[...], samples[...], (((1,), (1,)), ((), ())),
                preferred_element_type=f32, precision=lax.Precision.HIGHEST,
            )
            basis = basis * (1.0 / head**0.25)
            wide = below(*[beside(*[basis] * heads)] * heads)
            basis_s[...] = jnp.where(head_block(head, width, width), wide, 0.0)
            basis_o[...] = basis_s[...]
            w_o[...] = w_s[...]
            rotary_table(ends, first_pos, ROWS, tokens, cs_s)
            cs_o[...] = cs_s[...]

        xf = x[...].astype(f32)
        centered = xf - jnp.mean(xf, axis=1, keepdims=True)
        inv = lax.rsqrt(jnp.mean(centered * centered, axis=1, keepdims=True) + epsilon)
        normed = (centered * inv * gain[...] + shift[...]).astype(bf16)
        normed_o[...] = normed
        c = cot[...]
        cb_o[...] += jnp.sum(c.astype(f32).reshape(ROWS // 8, 8, model), axis=0)
        feed_step(normed, c, up_w, up_b, down_w, hidden_o, gpre_o, ub_o, down_acc, up_acc)

        projected = (nn(normed, w_s[...]) + b_s[...]).astype(bf16)
        tables = turn_tables(cs_s[step], expand[...], head, width)
        k_turn, k_feat = features(projected[:, :width], tables, two(basis_s[...]), head, feats)
        value = projected[:, width:]
        kf_o[...], v_o[...], kt_o[...] = k_feat, value, k_turn
        place = first_pos + step * ROWS + iota((ROWS, 1), 0)
        tail = jnp.where(place >= start_last, 1.0, 0.0).astype(bf16)
        state_s[...] += tn(k_feat * tail, beside(value, jnp.ones_like(value)))

        @pl.when(step == pl.num_programs(0) - 1)
        def _():
            state_o[...] = fold_state(state_s[...], head, width)
            for i in range(piece.shape[0]):
                write_down(piece_o, i, i * LANE, down_acc)
                write_up(piece_o, i, i * LANE, up_acc)

    narrow = shaped((tokens, width), bf16)
    return call(
        body,
        (lengths, x, gain, shift, up_w, up_b, down_w, cot, qkv_w, qkv_b, expand, samples, dct_t),
        [SMEM, rows_at(ROWS, model), whole(1, model), whole(1, model), *ins]
        + [whole(*a.shape) for a in (qkv_w, qkv_b, expand, samples, dct_t)],
        [rows_at(ROWS, model), whole(8, model), *[rows_at(ROWS, width)] * 3]
        + [whole(model, 2 * width), whole(width, width), whole(*table), whole(width, LANE), *outs]
        + [whole(*piece.shape)],
        [shaped((tokens, model), bf16), shaped((8, model)), *[narrow] * 3]
        + [shaped((model, 2 * width), bf16), shaped((width, width)), shaped(table, bf16)]
        + [shaped((width, LANE)), *shapes, piece],
        grid=(blocks,),
        scratch_shapes=[
            *scratch,
            pltpu.VMEM((model, 2 * width), bf16),
            pltpu.VMEM((1, 2 * width), f32),
            pltpu.VMEM((width, width), f32),
            pltpu.VMEM(table, bf16),
            pltpu.VMEM((width, 2 * width), f32),
        ],
        name="front",
    )


def project_queries_kernel(
    head, feats, normed, w_in, b_in, expand, basis, cs, cot, out_w, qf_o, qt_o, ga_o, w_o, w_s, b_s
):
    width = out_w.shape[0]
    heads = width // head

    @pl.when(pl.program_id(0) == 0)
    def _():
        w_s[...] = take_columns(w_in, head, heads, 0)
        b_s[...] = take_columns(b_in, head, heads, 0)
        w_o[...] = w_s[...]

    projected = (nn(normed[...], w_s[...]) + b_s[...]).astype(bf16)
    ga_o[...] = nt(cot[...], out_w[...])
    tables = turn_tables(cs[0], expand[...], head, width)
    qt_o[...], qf_o[...] = features(projected, tables, two(basis[...]), head, feats)


def project_queries(call, head, feats, normed, w_in, b_in, expand, basis, cs, cot, out_w):
    tokens, model = normed.shape
    width = out_w.shape[0]

    def body(*refs):
        project_queries_kernel(head, feats, *refs)

    return call(
        body,
        (normed, w_in, b_in, expand, basis, cs, cot, out_w),
        [
            rows_at(ROWS, model),
            whole(*w_in.shape),
            whole(*b_in.shape),
            whole(*expand.shape),
            whole(*basis.shape),
            pl.BlockSpec((1,) + cs.shape[1:], lambda i: (i, 0, 0)),
            rows_at(ROWS, model),
            whole(*out_w.shape),
        ],
        [rows_at(ROWS, width)] * 3 + [whole(model, width)],
        [
            shaped((tokens, width), bf16),
            shaped((tokens, width), bf16),
            shaped((tokens, width)),
            shaped((model, width), bf16),
        ],
        grid=(tokens // ROWS,),
        scratch_shapes=[pltpu.VMEM((model, width), bf16), pltpu.VMEM((1, width), f32)],
        name="project_queries",
    )


def swapped(value, axis, distance):
    size = lax.axis_size(axis)
    return lax.ppermute(value, axis, [(i, i ^ distance) for i in range(size)])


def joined(forward, lengths, tokens, base, entered, own, came):
    ends = ends_of(lengths)
    here = lax.axis_index("batch")
    count, size = 1, 2
    group = (here >> (base + count)) << (base + count)
    mine = (here >> base) & (size - 1)
    group_end = (group + (size << base)) * tokens
    total = jnp.zeros_like(own)
    entered = total if entered is None else entered
    for m in range(size):
        part = came if m else own
        other = mine ^ m
        if forward:
            edge = (group + ((other + 1) << base)) * tokens
            enters = (other < mine) & (seq_start(ends, here * tokens - 1) < edge)
            counts = seq_start(ends, group_end - 1) < edge
        else:
            start = seq_start(ends, (group + (other << base)) * tokens - 1)
            enters = (other > mine) & (start < (here + 1) * tokens)
            counts = start < group * tokens
        if m:
            entered = entered + jnp.where(enters, part, 0.0)
        total = total + jnp.where(counts, part, 0.0)
    return entered, total


def join_states(call, forward, tokens, base, lengths, entered, own, came, **rest):
    given = [own, came] if entered is None else [entered, own, came]

    def body(lengths, *refs):
        *ins, entered_o, total_o = refs
        values = [r[...] for r in ins]
        if entered is None:
            values = [None, *values]
        entered_o[...], total_o[...] = joined(
            forward, lengths, tokens, base, *values
        )

    spec = whole(*own.shape)
    return call(
        body,
        (lengths, *given),
        [SMEM] + [spec] * len(given),
        [spec, spec],
        [shaped(own.shape)] * 2,
        **rest,
        grid=(1,),
        name="join_states",
    )


def turned_grad(grad_feat, feat, turned, basis, tables, head, width):
    weighted = two(grad_feat * feat.astype(f32))
    ones = jnp.where(head_block(head, width, width), 1.0 / math.sqrt(head), 0.0).astype(bf16)
    total = nn(weighted[0], ones) + nn(weighted[1], ones)
    grad = exact3(nt, weighted, basis) - total * turned.astype(f32)
    return turn(grad, tables, -1).astype(bf16)


def attend_kernel(
    head, order, low, tokens, per_step, base, lengths, qf, kf, v, qt, ga, cs, expand, basis_i,
    normed, cot, hidden0, hidden1, down_w, out_w, entered_i, own_i, came_i,
    gq_o, gk_o, gv_o, back_o, total_o, qb_o, send_o, keep_o, *refs,
):
    *piece, state_s, q_acc, o_acc, total_s = refs
    step = pl.program_id(0)
    width = qf.shape[1]
    heads = width // head
    ends = ends_of(lengths)
    first_pos = lax.axis_index("batch") * tokens

    @pl.when(step == 0)
    def _():
        entered, _ = joined(
            True, lengths, tokens, base, entered_i[...], own_i[...], came_i[...]
        )
        state_s[...] = unfold_state(entered, head, width)
        q_acc[...] = jnp.zeros_like(q_acc)
        o_acc[...] = jnp.zeros_like(o_acc)
        total_s[...] = jnp.zeros_like(total_s)
        qb_o[...] = jnp.zeros_like(qb_o)

    basis = two(basis_i[...])
    block = head_block(head, width, width)
    both = beside(block, block)
    ones = jnp.where(block, 1.0, 0.0).astype(bf16)
    lanes = [jnp.where(iota((1, width), 1) // head == h, 1.0, 0.0).astype(bf16) for h in range(heads)]
    state = state_s[...]
    total = total_s[...]
    part = hidden0.shape[1]
    outward = nn(hidden1[...], down_w[:-part]) + nn(hidden0[...], down_w[-part:])
    mixes = []
    for sub in range(per_step):
        at = slice(sub * CHUNK, (sub + 1) * CHUNK)
        begin = first_pos + (step * per_step + sub) * CHUNK
        last = seq_start(ends, begin + CHUNK - 1)
        row = iota((CHUNK, 1), 0)
        start = seq_start(ends, begin + row)
        col = iota((CHUNK, CHUNK), 1)
        window = (col <= iota((CHUNK, CHUNK), 0)) & (col + begin >= start)
        carried = jnp.where(start < begin, 1.0, 0.0)
        q, k, value = qf[at, :], kf[at, :], v[at, :]
        q_carried = q * carried.astype(bf16)
        state_two = two(state)
        scores = [jnp.where(window, nt(q * lanes[h], k), 0.0).astype(bf16) for h in range(heads)]
        right = [beside(value * lane, jnp.broadcast_to(lane, value.shape)) for lane in lanes]
        sums = nn(beside(*scores, q_carried, q_carried), below(*right, *state_two))
        over = 1.0 / sums[:, width:]
        attended = sums[:, :width] * over
        mixed = attended.astype(bf16)
        mixes.append(mixed)
        grad_att = ga[at, :]
        g_num = grad_att * over
        product = two(grad_att * attended)
        g_den = -nn(beside(*product), below(ones, ones)) * over
        g_low = g_num.astype(bf16)
        g_both = two(beside(g_num, g_den * (1.0 / head)))
        from_state = nt(
            beside(g_both[0], g_both[0], g_both[1]), beside(state_two[0], state_two[1], state_two[0])
        )
        g_heads = [g_low * lane for lane in lanes]
        mixing = [
            jnp.where(window, nt(g_heads[h], value) + g_den[:, h * head : h * head + 1], 0.0).astype(bf16)
            for h in range(heads)
        ]
        grad_fq = carried * from_state + nn(beside(*mixing), below(*[k * lane for lane in lanes]))
        gk_o[at, :] = tn(below(*mixing), below(*[q * lane for lane in lanes]))
        gv_o[at, :] = tn(below(*scores), below(*g_heads))
        back = tn(q_carried, beside(g_num, g_den).astype(bf16))
        back_o[sub] = fold_state(back, head, width)
        live = jnp.where(seq_start(ends, begin - 1) < first_pos, 1.0, 0.0)
        total = total + live * back
        tail = jnp.where(begin + row >= last, 1.0, 0.0).astype(bf16)
        retain = jnp.where(last < begin, 1.0, 0.0)
        added = tn(k * tail, beside(value, jnp.ones_like(value)))
        state = retain * state + jnp.where(both, added, 0.0)
        tables = turn_tables(cs[0, :, at], expand[...], head, width)
        gq = turned_grad(grad_fq, q, qt[at, :], basis, tables, head, width)
        gq_o[at, :] = gq
        qb_o[...] += jnp.sum(gq.astype(f32).reshape(CHUNK // 8, 8, width), axis=0)
        q_acc[...] += tn(normed[at, :], gq)
        o_acc[...] += tn(mixed, cot[at, :])
    state_s[...] = state
    total_s[...] = total
    outward = outward + nn(below(*mixes), out_w[...])
    by_core(step & 1, send_o, keep_o, outward)

    @pl.when(step == pl.num_programs(0) - 1)
    def _():
        total_o[...] = fold_state(total, head, width)

        def write(out, i, spot):
            out[i, :width, :] = o_acc[:, pl.ds(spot, LANE)]
            for j in range(width // LANE):
                out[i, width + j * LANE : width + (j + 1) * LANE, :] = q_acc[
                    pl.ds(spot, LANE), j * LANE : (j + 1) * LANE
                ]

        deal(piece, order, low, write)


def by_core(core, send, keep, value):
    mine = lax.axis_index("branch") & 1

    @pl.when(core != mine)
    def _():
        send[0] = value

    @pl.when(core == mine)
    def _():
        keep[0] = value


def attend(
    call, head, order, low, base, lengths, qf, kf, v, qt, ga, cs, expand, basis, normed, cot,
    hidden0, hidden1, down_w, out_w, entered, own, came, **rest,
):
    tokens, width = qf.shape
    model = cot.shape[1]
    per_step = ROWS // CHUNK
    chunks = tokens // CHUNK
    part = hidden0.shape[1]
    firsts, piece = shaped((4, 2 * width, LANE)), shaped((2, 2 * width, LANE))
    chip = pl.BlockSpec((1, ROWS, model), lambda i: (i >> 1, 0, 0))
    row = rows_at(ROWS, width)
    packed = whole(width, LANE)

    def body(*refs):
        attend_kernel(head, order, low, tokens, per_step, base, *refs)

    return call(
        body,
        (lengths, qf, kf, v, qt, ga, cs, expand, basis, normed, cot, hidden0, hidden1, down_w, out_w)
        + (entered, own, came),
        [
            SMEM,
            *[row] * 5,
            pl.BlockSpec((1,) + cs.shape[1:], lambda i: (i, 0, 0)),
            whole(*expand.shape),
            whole(width, width),
            rows_at(ROWS, model),
            rows_at(ROWS, model),
            rows_at(ROWS, part),
            rows_at(ROWS, hidden1.shape[1]),
            whole(*down_w.shape),
            whole(*out_w.shape),
            *[packed] * 3,
        ],
        [
            *[row] * 3,
            pl.BlockSpec((per_step, width, LANE), lambda i: (i, 0, 0)),
            packed,
            whole(8, width),
            chip,
            chip,
            *[whole(*a.shape) for a in (firsts, piece, piece)],
        ],
        [
            shaped((tokens, width), bf16),
            shaped((tokens, width)),
            shaped((tokens, width)),
            shaped((chunks, width, LANE)),
            shaped((width, LANE)),
            shaped((8, width)),
            *[shaped((tokens // ROWS // 2, ROWS, model))] * 2,
            firsts,
            piece,
            piece,
        ],
        **rest,
        grid=(tokens // ROWS,),
        scratch_shapes=[
            pltpu.VMEM((width, 2 * width), f32),
            pltpu.VMEM((model, width), f32),
            pltpu.VMEM((width, model), f32),
            pltpu.VMEM((width, 2 * width), f32),
        ],
        name="attend",
        flops=LONG,
    )


def branch_place():
    here = lax.axis_index("branch")
    return here & 1, here >> 1


def share_at(i):
    core, chip = branch_place()
    return 2 * jnp.where(i < 2, 1 - chip, chip) + jnp.where(i & 1, core, 1 - core)


def backward(
    call, head, order, low, base, lengths, kf, v, kt, gk, gv, back, cs, expand, basis, normed, x,
    gpre0, gpre1, gq, up_w, q_w, kv_w, entered, own, came, **rest,
):
    tokens, width = kf.shape
    model = normed.shape[1]
    part = gpre0.shape[1]
    chunks, per_step = tokens // CHUNK, ROWS // CHUNK
    row = lambda n: pl.BlockSpec((ROWS, n), lambda i: (share_at(i), 0))
    packed = whole(width, LANE)
    firsts, piece = shaped((4, 2 * width, LANE)), shaped((2, 2 * width, LANE))
    acc_shape = (model, 2 * width)

    def body(
        lengths, kf, v, kt, gk, gv, back, cs, expand, basis_i, normed, x, gpre0, gpre1, gq, up_w,
        q_w, kv_w, entered_i, own_i, came_i, keep_o, far0_o, far1_o, near_o, kvb_o, gain_o, shift_o,
        *refs,
    ):
        *pieces, acc, state_s = refs
        step = pl.program_id(0)
        ends = ends_of(lengths)
        first_pos = lax.axis_index("batch") * tokens

        @pl.when(step == 0)
        def _():
            clear(kvb_o, gain_o, shift_o, acc)
            state, _ = joined(
                False, lengths, tokens, base, entered_i[...], own_i[...], came_i[...]
            )
            for chunk in reversed(range(chunks)):
                state_s[chunk] = state
                begin = first_pos + chunk * CHUNK
                last = seq_start(ends, begin + CHUNK - 1)
                state = back[chunk] + jnp.where(last < begin, state, 0.0)

        grad = nt(gpre1[...], up_w[:, :-part]) + nt(gpre0[...], up_w[:, -part:])
        basis = two(basis_i[...])
        tables = turn_tables(cs[0], expand[...], head, width)
        grads = []
        for sub in range(per_step):
            here = slice(sub * CHUNK, (sub + 1) * CHUNK)
            chunk = share_at(step) * per_step + sub
            begin = first_pos + chunk * CHUNK
            last = seq_start(ends, begin + CHUNK - 1)
            tail = jnp.where(begin + iota((CHUNK, 1), 0) >= last, 1.0, 0.0)
            k, value = kf[here, :], v[here, :]
            state = two(unfold_state(state_s[chunk], head, width))
            right = beside(value, jnp.full(value.shape, 1.0 / head, bf16))
            grad_fk = gk[here, :] + tail * nt(beside(right, right), beside(*state))
            grad_v = gv[here, :] + tail * nn(
                beside(k, k), below(state[0][:, :width], state[1][:, :width])
            )
            turned = tuple(t[here, :] for t in tables)
            grad_k = turned_grad(grad_fk, k, kt[here, :], basis, turned, head, width)
            grads.append(beside(grad_k, grad_v.astype(bf16)))
        both = below(*grads)
        kvb_o[...] += jnp.sum(both.astype(f32).reshape(ROWS // 8, 8, 2 * width), axis=0)
        grad = grad + nt(beside(gq[...], both), beside(q_w[...], kv_w[...]))
        acc[...] += tn(normed[...], both)

        @pl.when(step == 0)
        def _():
            far0_o[...] = grad[: ROWS // 2]
            far1_o[...] = grad[ROWS // 2 :]

        @pl.when(step == 2)
        def _():
            near_o[...] = grad

        @pl.when(step & 1 == 1)
        def _():
            keep_o[0] = grad

        xf = x[...].astype(f32)
        centered = xf - jnp.mean(xf, axis=1, keepdims=True)
        unit = centered * lax.rsqrt(jnp.mean(centered * centered, axis=1, keepdims=True) + epsilon)
        gain_o[...] += jnp.sum((grad * unit).reshape(ROWS // 8, 8, model), axis=0)
        shift_o[...] += jnp.sum(grad.reshape(ROWS // 8, 8, model), axis=0)

        @pl.when(step == pl.num_programs(0) - 1)
        def _():
            deal(pieces, order, low, lambda *spot: write_up(*spot, acc))

    chip = pl.BlockSpec((1, ROWS, model), lambda i: (i >> 1, 0, 0))
    sums = [shaped((8, 2 * width)), shaped((8, model)), shaped((8, model))]
    pieces = [firsts, piece, piece]
    sent = [shaped((ROWS // 2, model)), shaped((ROWS // 2, model)), shaped((ROWS, model))]
    return call(
        body,
        (lengths, kf, v, kt, gk, gv, back, cs, expand, basis, normed, x, gpre0, gpre1, gq, up_w)
        + (q_w, kv_w, entered, own, came),
        [SMEM, *[row(width)] * 5, whole(*back.shape)]
        + [pl.BlockSpec((1,) + cs.shape[1:], lambda i: (share_at(i), 0, 0)), whole(*expand.shape)]
        + [whole(width, width), row(model), row(model), row(part), row(gpre1.shape[1]), row(width)]
        + [whole(*up_w.shape), whole(*q_w.shape), whole(*kv_w.shape), *[packed] * 3],
        [chip] + [whole(*a.shape) for a in (*sent, *sums, *pieces)],
        [shaped((tokens // ROWS // 2, ROWS, model)), *sent, *sums, *pieces],
        **rest,
        grid=(tokens // ROWS,),
        scratch_shapes=[pltpu.VMEM(acc_shape, f32), pltpu.VMEM((chunks, width, LANE), f32)],
        flops=LONG,
        name="backward",
    )


def finish_small(call, one, other, sizes):
    shapes = [shaped((size // LANE, LANE)) for size in sizes]

    def body(one, other, *outs):
        row = 0
        for out in outs:
            out[...] = one[row : row + out.shape[0], :] + other[row : row + out.shape[0], :]
            row += out.shape[0]

    parts = call(
        body,
        (one, other),
        [whole(*one.shape)] * 2,
        [whole(*a.shape) for a in shapes],
        shapes,
        grid=(1,),
        name="finish_small",
    )
    return [part.reshape(-1) for part in parts]


def block_of(array, count, at):
    shape = (count,) + array.shape[1:]
    return pl.BlockSpec(shape, lambda i: (at() if callable(at) else at,) + (0,) * (len(shape) - 1))


def sums_of(call, *jobs, **rest):
    arrays, specs, outs, shapes = [], [], [], []
    for job in jobs:
        for array, count, at in job:
            arrays.append(array)
            specs.append(block_of(array, count, at))
        shapes.append(shaped((count,) + array.shape[1:]))
        outs.append(whole(*shapes[-1].shape))

    def body(*refs):
        ins, results = refs[: len(arrays)], refs[len(arrays) :]
        for job, out in zip(jobs, results):
            mine, ins = ins[: len(job)], ins[len(job) :]
            out[...] = sum(r[...] for r in mine[1:]) + mine[0][...]

    return call(body, arrays, specs, outs, shapes, grid=(1,), name="sums", **rest)


def whole_of(array):
    return array, array.shape[0], 0


def finish_feed(call, one, down, up, **rest):
    args, specs = [one], [block_of(one, 1, 0)]
    for piece, first, two_came, three_came in (down, up):
        args += [piece[2], first, two_came, three_came]
        specs += [block_of(a, 1, at) for a, at in zip(args[-4:], (0, 2, 0, 0))]
    widths = [down[0][2].shape[1], one.shape[1] // 2]

    def body(one, *refs):
        down_o, up_o = refs[-2:]
        values = []
        for a, b, c, d in (refs[:4], refs[4:8]):
            values.append((a[0] + b[0]) + (c[0] + d[0]))
        downs = (values[0], one[0, : widths[1]])
        ups = (values[1], one[0, widths[1] :])
        for down, up, start, width in zip(downs, ups, (0, widths[0]), widths):
            down_o[start : start + width, :] = down
            for j in range(0, width, LANE):
                up_o[:, start + j : start + j + LANE] = up[j : j + LANE, :]

    shapes = [shaped((sum(widths), LANE)), shaped((LANE, sum(widths)))]
    return call(
        body, args, specs, [whole(*a.shape) for a in shapes], shapes, grid=(1,), name="finish_feed", **rest
    )


def finish_heads(call, head, out_q, key_val, **rest):
    args, specs = [], []
    for piece, first, two_came, three_came in (out_q, key_val):
        args += [piece[2], first, two_came, three_came]
        specs += [block_of(a, 1, at) for a, at in zip(args[-4:], (0, 2, 0, 0))]
    width = key_val[0][2].shape[1] // 2
    heads = width // head

    def body(*refs):
        out_o, qkv_o = refs[-2:]
        values = []
        for n in range(2):
            a, b, c, d = refs[4 * n : 4 * n + 4]
            values.append((a[0] + b[0]) + (c[0] + d[0]))
        out_o[...] = values[0][:width]
        columns = []
        for rows in (values[0][width:], values[1][:width], values[1][width:]):
            columns.append(beside(*[rows[j * LANE : (j + 1) * LANE] for j in range(width // LANE)]))
        qkv_o[...] = beside(*[p[:, h * head : (h + 1) * head] for h in range(heads) for p in columns])

    shapes = [shaped((width, LANE)), shaped((LANE, 3 * width))]
    return call(
        body, args, specs, [whole(*a.shape) for a in shapes], shapes, grid=(1,), name="finish_heads", **rest
    )


def far_sums(call, keep, came, far, **rest):
    rows, model = CHUNK, keep.shape[2]
    steps = keep.shape[1] // rows
    spec = pl.BlockSpec((1, rows, model), lambda i: (far(), i, 0))
    parts = isinstance(came, tuple)

    def body(keep, *refs):
        *came, out = refs
        if parts:
            step = pl.program_id(0)
            out[...] = keep[0] + jnp.where(step == 0, came[0][...], came[1][...])
        else:
            out[...] = keep[0] + came[0][0]

    return call(
        body,
        (keep, *came) if parts else (keep, came),
        [spec, *([whole(rows, model)] * 2 if parts else [spec])],
        [rows_at(rows, model)],
        [shaped(keep.shape[1:])],
        grid=(steps,),
        name="far_sums",
        **rest,
    )


def finish_specs(keep, near):
    share, model = keep.shape[1:]
    steps = share // CHUNK
    own = pl.BlockSpec((CHUNK, model), lambda i: (lax.axis_index("branch") * steps + i, 0))
    return own, pl.BlockSpec((1, CHUNK, model), lambda i: (near(), i, 0)), rows_at(CHUNK, model), steps


def finish_output(call, x, keep, came_core, came_chip, bias, near):
    share, model = came_chip.shape
    own, part, row, steps = finish_specs(keep, near)

    def body(x, keep, core, chip, bias, out):
        total = (keep[0] + core[0]) + chip[...]
        out[...] = (x[...].astype(f32) + total + bias[...]).astype(bf16)

    return call(
        body,
        (x, keep, came_core, came_chip, bias),
        [own, part, part, row, whole(1, model)],
        [row],
        [shaped((share, model), bf16)],
        grid=(steps,),
        name="finish_output",
    )[0]


def finish_input(call, x, cot, gain, keep, came_core, came_chip, near):
    share, model = came_chip.shape
    own, part, row, steps = finish_specs(keep, near)


    def body(x, cot, gain, keep, core, chip, out):
        xf = x[...].astype(f32)
        centered = xf - jnp.mean(xf, axis=1, keepdims=True)
        inv = lax.rsqrt(jnp.mean(centered * centered, axis=1, keepdims=True) + epsilon)
        unit = centered * inv
        g = ((keep[0] + core[...]) + chip[...]) * gain[...]
        inner = g - jnp.mean(g, axis=1, keepdims=True) - unit * jnp.mean(g * unit, axis=1, keepdims=True)
        out[...] = inv * inner + cot[...].astype(f32)

    return call(
        body,
        (x, cot, gain, keep, came_core, came_chip),
        [own, own, whole(1, model), part, row, row],
        [row],
        [shaped((share, model))],
        grid=(steps,),
        name="finish_input",
    )[0]


def pack_small(call, head, branch, gain, shift, cot, qb, kvb, ubs, **rest):
    model = cot.shape[1]
    width = qb.shape[1]
    heads = width // head
    up_width = sum(u.shape[1] for u in ubs)
    qkv_rows, up_rows = 3 * width // LANE, up_width // LANE
    starts = [0, model // LANE, 2 * model // LANE, 3 * model // LANE]
    starts.append(starts[3] + qkv_rows * branch)
    total = starts[4] + up_rows * branch

    def body(gain, shift, cot, qb, kvb, ub0, ub1, out):
        out[...] = jnp.zeros_like(out)
        here = lax.axis_index("branch")

        def summed(value):
            return jnp.sum(value, axis=0, keepdims=True)

        def place(row, value):
            for j in range(value.shape[1] // LANE):
                out[pl.ds(row + j, 1), :] = value[:, j * LANE : (j + 1) * LANE]

        place(starts[0], summed(gain[...]))
        place(starts[1], summed(shift[...]))
        place(starts[2], summed(cot[...]) * jnp.where(here == 0, 1.0, 0.0))
        q, kv = summed(qb[...]), summed(kvb[...])
        parts = (q, kv[:, :width], kv[:, width:])
        place(
            starts[3] + here * qkv_rows,
            beside(*[p[:, h * head : (h + 1) * head] for h in range(heads) for p in parts]),
        )
        place(starts[4] + here * up_rows, beside(summed(ub1[...]), summed(ub0[...])))

    args = (gain, shift, cot, qb, kvb, *ubs)
    return call(
        body,
        args,
        [whole(*a.shape) for a in args],
        [whole(total, LANE)],
        [shaped((total, LANE))],
        grid=(1,),
        name="pack_small",
        **rest,
    )


def finish(part, dim, low):
    if low == 1:
        return part
    size = lax.axis_size("batch")
    groups = [[j * low + i for i in range(low)] for j in range(size // low)]
    return lax.psum_scatter(
        part, "batch", scatter_dimension=dim, axis_index_groups=groups, tiled=True
    )


def per_device(
    inputs, ln_gain, ln_shift, qkv_weight, qkv_bias, out_weight, up_weight, up_bias, down_weight,
    out_bias, feature_samples, lengths, cotangent,
):
    tokens, model = inputs.shape
    feats, head = feature_samples.shape
    width = out_weight.shape[0]
    batch = lax.axis_size("batch")
    branch = lax.axis_size("branch")
    low = batch // (model // LANE)
    y_first, z_first = (0, 1, 2), (1, 0, 2)
    bits = [1 << b for b in range(batch.bit_length() - 1)]
    expand = jnp.asarray(expand_table(head), bf16)
    dct_t = jnp.asarray(dct_table(head).T)
    gain = ln_gain.reshape(1, model)
    shift = ln_shift.reshape(1, model)
    up_b = up_bias.reshape(1, -1)
    qkv_b = qkv_bias.reshape(1, -1)
    call = Order()

    def send(value, order, step):
        return swapped(value, "batch", low << order[step])

    def enter(forward, own, came):
        entered = None
        for i, bit in enumerate(bits[1:]):
            entered, own = join_states(call, forward, tokens, i, lengths, entered, own, came)
            came = swapped(own, "batch", bit)
        return entered, own, came

    normed, cb, kf, value, kt, kv_w, basis, cs, state, hidden0, gpre0, ub0, piece0 = front(
        call, head, lengths, inputs, gain, shift, up_weight, up_b, down_weight, cotangent, qkv_weight,
        qkv_b, expand, feature_samples, dct_t,
    )
    groups = [[j * low + i for j in range(batch // low)] for i in range(low)] if low > 1 else None
    sum0 = lax.psum_scatter(
        piece0, "batch", scatter_dimension=0, axis_index_groups=groups, tiled=True
    )
    came = swapped(state, "batch", 1)
    qf, qt, ga, q_w = project_queries(
        call, head, feats, normed, qkv_weight, qkv_b, expand, basis, cs, cotangent, out_weight
    )
    states = enter(True, state, came)
    hidden1, gpre1, ub1, *pieces = feed(
        call, (y_first, z_first), low, normed, up_weight, up_b, down_weight, cotangent
    )
    down, up = pieces[:3], pieces[3:]
    down_first, up_first = send(down[0], y_first, 0), send(up[0], z_first, 0)
    gq, gk, gv, back, state, qb, out_send, out_keep, *oq = attend(
        call, head, y_first, low, len(bits) - 1, lengths, qf, kf, value, qt, ga, cs, expand, basis,
        normed, cotangent, hidden0, hidden1, down_weight, out_weight, *states,
    )
    came = swapped(state, "batch", 1)
    out_core = swapped(out_send, "branch", 1)
    far_chip = lambda: 1 - branch_place()[1]
    near_chip = lambda: branch_place()[1]
    down_2, up_2 = sums_of(
        call, [whole_of(down[1]), (down_first, 2, 0)], [whole_of(up[1]), (up_first, 2, 0)]
    )
    entered, state, oq_first = join_states(
        call, False, tokens, 0, lengths, None, state, came, through=(oq[0],), flops=LONG
    )
    came = swapped(state, "batch", bits[1])
    oq_first = send(oq_first, y_first, 0)
    (out_far,) = far_sums(call, out_keep, out_core, far_chip)
    out_chip = swapped(out_far, "branch", 2)
    for i in range(1, len(bits) - 1):
        entered, state = join_states(call, False, tokens, i, lengths, entered, state, came)
        came = swapped(state, "batch", bits[i + 1])
    down_2, up_2 = hold(call, (down_2, up_2))
    down_2, up_2 = send(down_2, y_first, 1), send(up_2, z_first, 1)
    grad_keep, far0, far1, near, kvb, gain_part, shift_part, *kv = backward(
        call, head, y_first, low, len(bits) - 1, lengths, kf, value, kt, gk, gv, back, cs,
        expand, basis, normed, inputs, gpre0, gpre1, gq, up_weight, q_w, kv_w, entered, state, came,
    )
    far_core = (swapped(far0, "branch", 1), swapped(far1, "branch", 1))
    down_3, up_3, oq_2, near, kv_first = sums_of(
        call, [(down[2], 1, 1), (down_first, 1, 3), (down_2, 1, 1)],
        [(up[2], 1, 1), (up_first, 1, 3), (up_2, 1, 1)], [whole_of(oq[1]), (oq_first, 2, 0)],
        through=(near, kv[0]),
    )
    grad_core = swapped(near, "branch", 1)
    kv_first = send(kv_first, y_first, 0)
    down_3, up_3 = send(down_3, y_first, 2), send(up_3, z_first, 2)
    oq_2 = send(oq_2, y_first, 1)
    (small,) = pack_small(
        call, head, branch, gain_part, shift_part, cb, qb, kvb, (ub0, ub1), flops=SHORT
    )
    came = swapped(small, "branch", 1)
    (grad_far,) = far_sums(call, grad_keep, far_core, lambda: 0)
    grad_chip = swapped(grad_far, "branch", 2)
    output = finish_output(
        call, inputs, out_keep, out_core, out_chip, out_bias.reshape(1, model), near_chip
    )
    (small,) = sums_of(call, [whole_of(small), whole_of(came)], after=(grad_core,))
    came = swapped(small, "batch", 1)
    (kv_2,) = sums_of(call, [whole_of(kv[1]), (kv_first, 2, 0)])
    kv_2 = send(kv_2, y_first, 1)
    (small,) = sums_of(call, [whole_of(small), whole_of(came)])
    came = swapped(small, "batch", bits[1])
    (oq_3,) = sums_of(call, [(oq[2], 1, 1), (oq_first, 1, 3), (oq_2, 1, 1)])
    oq_3 = send(oq_3, y_first, 2)
    for bit in bits[2:]:
        (small,) = sums_of(call, [whole_of(small), whole_of(came)])
        came = swapped(small, "batch", bit)
    (kv_3,) = sums_of(call, [(kv[2], 1, 1), (kv_first, 1, 3), (kv_2, 1, 1)])
    kv_3 = send(kv_3, y_first, 2)
    (small,) = sums_of(call, [whole_of(small), whole_of(came)])
    came = swapped(small, "branch", 2)
    down_sum, up_sum = finish_feed(
        call, sum0, (down, down_first, down_2, down_3), (up, up_first, up_2, up_3)
    )
    out_sum, qkv_sum = finish_heads(
        call, head, (oq, oq_first, oq_2, oq_3), (kv, kv_first, kv_2, kv_3)
    )
    small = finish_small(call, small, came, [model, model, model, 3 * width * branch, up_bias.size * branch])
    input_grad = finish_input(
        call, inputs, cotangent, gain, grad_keep, grad_core, grad_chip, lambda: 1
    )
    down_sum, out_sum = finish(down_sum, 1, low), finish(out_sum, 1, low)
    up_sum, qkv_sum = finish(up_sum, 0, low), finish(qkv_sum, 0, low)

    gain_grad, shift_grad, out_bias_grad, qkv_bias_grad, up_bias_grad = small
    return (
        output,
        input_grad,
        gain_grad,
        shift_grad,
        qkv_sum,
        qkv_bias_grad,
        out_sum,
        up_sum,
        up_bias_grad,
        down_sum,
        out_bias_grad,
    )


def solution(mesh):
    placed = (
        P("batch", None),
        P(),
        P(),
        P(None, "branch"),
        P("branch"),
        P("branch", None),
        P(None, "branch"),
        P("branch"),
        P("branch", None),
        P(),
        P(),
        P(),
        P("batch", None),
    )
    return jax.shard_map(
        per_device,
        mesh=mesh,
        in_specs=placed,
        out_specs=(
            P(("batch", "branch"), None),
            P(("batch", "branch"), None),
            P(),
            P(),
            P("batch", "branch"),
            P(),
            P("branch", "batch"),
            P("batch", "branch"),
            P(),
            P("branch", "batch"),
            P(),
        ),
        check_vma=False,
    )
```

time: 1070 us -> 298 us (0.28); the launches traced: 1060 us -> 297 us
  matrix products: 308 us -> 0 us
  waiting for transfers between devices: 360 us -> 85.3 us
  blocking collectives: 184 us -> 0 us
  Pallas kernels: 0 us -> 164 us
  local copies, waits for them, and re-layouts: 99.3 us -> 1.27 us
  other arithmetic: 77.5 us -> 0 us
  starting transfers between devices: 0.71 us -> 32 us
    reduce_scatter x6 -> x1, waiting for transfers between devices: 360 us -> 0.01 us  [per_device(): lax.psum_scatter(piece0, 'batch', scatter_dimension=0, axis_index_groups=...]
    dot_general x42 -> x0, matrix products: 308 us -> none  [the longest x1 23.5 us: per_device(): pre_act = jnp.dot(normed, up_weight, preferred_element_type=f32) + up_bias]
    pallas_call x0 -> x27, Pallas kernels: none -> 164 us  [__call__(): pl.pallas_call(without, in_specs=[*in_specs, *[place] * len(skipped)], ou...]
    all_gather x4 -> x0, blocking collectives: 122 us -> none  [entering(): everything = jax.tree.map(lambda part: lax.all_gather(part, axis), shard)]
    ppermute x0 -> x29, waiting for transfers between devices: none -> 85.3 us  [swapped(): return lax.ppermute(value, axis, [(i, i ^ distance) for i in range(size)])]
    psum x1 -> x0, blocking collectives: 40.6 us -> none  [per_device(): lax.psum((gain_part, shift_part, out_bias_part, qkv_bias_full, up_bias_fu...]
    ppermute x0 -> x29, starting transfers between devices: none -> 32 us  [swapped(): return lax.ppermute(value, axis, [(i, i ^ distance) for i in range(size)])]
    select_n x32 -> x0, other arithmetic: 28.9 us -> none  [turn(): return jax.tree.map(lambda a, b: jnp.where(reached, a, b), new, before)]
  transfers between devices with their start and end apart: 6 -> 30, of which waited for: 6 -> 13; matrix products, arithmetic and copies ran while one was open for 7% -> 0% of each run, Pallas kernels for 0% -> 45%
where the time goes in v2:
time: 298 us; the launch traced here: 297 us
  Pallas kernels  164 us (55%)
  waiting for transfers between devices  85.3 us (29%)
  starting transfers between devices  32 us (11%)
  between operations  14.1 us (5%)
    pallas_call x27, Pallas kernels, __call__(): pl.pallas_call(without, in_specs=[*in_specs, *[place] * len(skipped)], ou...  164 us
    ppermute x29, waiting for transfers between devices, swapped(): return lax.ppermute(value, axis, [(i, i ^ distance) for i in range(size)])  85.3 us
    ppermute x29, starting transfers between devices, swapped(): return lax.ppermute(value, axis, [(i, i ^ distance) for i in range(size)])  32 us
  transfers between devices with their start and end apart: 30, of which 13 were waited for; matrix products, arithmetic and copies ran while one was open for 0% of the time, Pallas kernels for 45%

profile of v2, /device:TPU:0, one launch (start us, length us, event | category | flops | bytes accessed | tf_op | source)
XLA Modules:
  0.0 297.2 jit_solution(885702703454572163)
XLA Ops:
  8.5 20.8 %front.1 = (bf16[2048,1024]{1,0:T(8,128)(2,1)}, f32[8,1024]{1,0:T(8,128)}, bf16[2048,256]{1,0:T(8,128)(2,1)}, bf16[2048,256]{1,0:T(8,128)(2,1)}, bf16[2048,256]{...) custom-call(s32[8]{0:T(128)} %refs_0_.15, ...), custom_call_target="tpu_custom_call" | custom-call | tf_op jit(solution)/shard_map/front/pallas_call | solution.py:72
  29.3 3.0 %collective-permute-start = (f32[256,128]{1,0:T(8,128)}, f32[256,128]{1,0:T(8,128)}, u32[]{:S(2)}, u32[]{:S(2)}) collective-permute-start(f32[256,128]{1,0:T(8,128)} %get-tuple-element.95.refs_1_), channel_id=1, source_target_pairs={{0,4},{4,0},{8,12},{12,8},{16,20},{20,16},{24,28},{28,24},{1,5},{5... | collective-permute-start | bytes 393224 | tf_op jit(solution)/shard_map/ppermute | solution.py:454
  32.3 9.2 %project_queries.1 = (bf16[2048,256]{1,0:T(8,128)(2,1)}, bf16[2048,256]{1,0:T(8,128)(2,1)}, f32[2048,256]{1,0:T(8,128)}, bf16[1024,256]{1,0:T(8,128)(2,1)}) custom-call(bf16[2048,1024]{1,0:T(8,128)(2,1)} %get-tuple-element.86.refs_0_.refs_8_.refs_9_.refs_10_, bf16[1024,768]{1,0:T(8,128)(2,1)} %refs_1_.5, f32[1,768]{1,0:T(1,128)} %reshape.55.refs_9_.refs_2_, ...), custom_call_target="tpu_custom_call" | custom-call | tf_op jit(solution)/shard_map/project_queries/pallas_call | solution.py:72
  44.8 3.7 %collective-permute-done.1.refs_3_ = f32[256,128]{1,0:T(8,128)} collective-permute-done((f32[256,128]{1,0:T(8,128)}, f32[256,128]{1,0:T(8,128)}, u32[]{:S(2)}, u32[]{:S(2)}) %collective-permute-start.1) | collective-permute-done | bytes 131104 | tf_op jit(solution)/shard_map/ppermute | solution.py:454
  50.3 2.6 collective-permute-start.2
  52.9 21.1 %feed_forward.1 = (bf16[2048,768]{1,0:T(8,128)(2,1)}, bf16[2048,768]{1,0:T(8,128)(2,1)}, f32[8,768]{1,0:T(8,128)}, f32[4,768,128]{2,1,0:T(8,128)}, f32[2,768,128...) custom-call(bf16[2048,1024]{1,0:T(8,128)(2,1)} %get-tuple-element.86, ...), custom_call_target="tpu_custom_call" | custom-call | tf_op jit(solution)/shard_map/feed_forward/pallas_call | solution.py:72
  76.2 35.9 %attend.1 = (bf16[2048,256]{1,0:T(8,128)(2,1)}, f32[2048,256]{1,0:T(8,128)}, f32[2048,256]{1,0:T(8,128)}, f32[8,256,128]{2,1,0:T(8,128)}, f32[256,128]{1,0:T(8,1...) custom-call(s32[8]{0:T(128)} %refs_0_.15, ...), custom_call_target="tpu_custom_call" | custom-call | flops 1099511627776 | tf_op jit(solution)/shard_map/attend/pallas_call | solution.py:72
  113.7 3.1 %sums.9 = (f32[2,768,128]{2,1,0:T(8,128)}, f32[2,768,128]{2,1,0:T(8,128)}) custom-call(f32[2,768,128]{2,1,0:T(8,128)} %get-tuple-element.104.refs_0_, f32[4,768,128]{2,1,0:T(8,128)} %collective-permute-done.5.refs_1_.refs_2_, f32[2,768,128]{2,1,0:T(8,128)} %get-tuple-element.106.refs_2_, f32[4,768,128]{2,1,0:T(8,128)} %collective-permute-done.6.refs_3_.refs_4_.refs_6_, ...), custom_call_target="tpu_custom_call" | custom-call | tf_op jit(solution)/shard_map/sums/pallas_call | solution.py:72
  121.1 3.3 %far_sums.2.refs_4_ = f32[512,1024]{1,0:T(8,128)} custom-call(f32[2,512,1024]{2,1,0:T(8,128)} %get-tuple-element.101.refs_0_.refs_1_, f32[2,512,1024]{2,1,0:T(8,128)} %collective-permute-done.3.refs_1_.refs_2_, f32[256,128]{1,0:T(8,128)} %get-tuple-element.111.refs_2_.refs_1_), custom_call_target="tpu_custom_call" | custom-call | tf_op jit(solution)/shard_map/far_sums/pallas_call | solution.py:72
  124.7 1.8 join_states.7
  131.4 4.3 %collective-permute-done.9.refs_20_ = f32[256,128]{1,0:T(8,128)} collective-permute-done((f32[256,128]{1,0:T(8,128)}, f32[256,128]{1,0:T(8,128)}, u32[]{:S(2)}, u32[]{:S(2)}) %collective-permute-start.9) | collective-permute-done | bytes 131104 | tf_op jit(solution)/shard_map/ppermute | solution.py:454
  135.8 27.9 %backward.1 = (f32[2,512,1024]{2,1,0:T(8,128)}, f32[256,1024]{1,0:T(8,128)}, f32[256,1024]{1,0:T(8,128)}, f32[512,1024]{1,0:T(8,128)}, f32[8,512]{1,0:T(8,128)},...) custom-call(s32[8]{0:T(128)} %refs_0_.15, ...), custom_call_target="tpu_custom_call" | custom-call | flops 1099511627776 | tf_op jit(solution)/shard_map/backward/pallas_call | solution.py:72
  164.3 3.6 %collective-permute-done.12.refs_2_.refs_3_ = f32[2,768,128]{2,1,0:T(8,128)} collective-permute-done((f32[2,768,128]{2,1,0:T(8,128)}, f32[2,768,128]{2,1,0:T(8,128)}, u32[]{:S(2)}, u32[]{:S(2)}) %collective-permute-start.12) | collective-permute-done | bytes 786464 | tf_op jit(solution)/shard_map/ppermute | solution.py:454
  167.9 10.5 %collective-permute-done.13.refs_5_.refs_7_ = f32[2,768,128]{2,1,0:T(8,128)} collective-permute-done((f32[2,768,128]{2,1,0:T(8,128)}, f32[2,768,128]{2,1,0:T(8,128)}, u32[]{:S(2)}, u32[]{:S(2)}) %collective-permute-start.13) | collective-permute-done | bytes 786464 | tf_op jit(solution)/shard_map/ppermute | solution.py:454
  178.4 3.0 %sums.10 = (f32[1,768,128]{2,1,0:T(8,128)}, f32[1,768,128]{2,1,0:T(8,128)}, f32[2,512,128]{2,1,0:T(8,128)}, f32[512,1024]{1,0:T(8,128)}, f32[4,512,128]{2,1,0:T(8,128)}) custom-call(f32[2,768,128]{2,1,0:T(8,128)} %get-tuple-element.135.refs_0_.refs_1_, ...), custom_call_target="tpu_custom_call", output_to_operand_aliasing={{3}: (9, {}), {4}: (10, {})} | custom-call | tf_op jit(solution)/shard_map/sums/pallas_call | solution.py:72
  183.0 3.4 %far_sums.3.refs_5_ = f32[512,1024]{1,0:T(8,128)} custom-call(f32[2,512,1024]{2,1,0:T(8,128)} %get-tuple-element.125.refs_8_.refs_0_.refs_3_, f32[256,1024]{1,0:T(8,128)} %collective-permute-done.10.refs_1_, f32[256,1024]{1,0:T(8,128)} %collective-permute-done.11.refs_2_, f32[80,128]{1,0:T(8,128)} %pack_small.1.refs_3_.refs_0_), custom_call_target="tpu_custom_call" | custom-call | tf_op jit(solution)/shard_map/far_sums/pallas_call | solution.py:72
  186.4 2.3 collective-permute-start.16
  189.0 4.2 %finish_output.1.refs_2_ = bf16[512,1024]{1,0:T(8,128)(2,1)} custom-call(bf16[2048,1024]{1,0:T(8,128)(2,1)} %refs_0_.17, f32[2,512,1024]{2,1,0:T(8,128)} %get-tuple-element.101.refs_0_.refs_1_, f32[2,512,1024]{2,1,0:T(8,128)} %collective-permute-done.3.refs_1_.refs_2_, f32[512,1024]{1,0:T(8,128)} %collective-permute-done.7.refs_3_, f32[1,1024]{1,0:T(1,128)} %bitcast.13, ...), custom_call_target="tpu_custom_call" | custom-call | tf_op jit(solution)/shard_map/finish_output/pallas_call | solution.py:72
  194.6 22.4 %collective-permute-done.19.refs_1_.refs_5_ = f32[4,512,128]{2,1,0:T(8,128)} collective-permute-done((f32[4,512,128]{2,1,0:T(8,128)}, f32[4,512,128]{2,1,0:T(8,128)}, u32[]{:S(2)}, u32[]{:S(2)}) %collective-permute-start.19) | collective-permute-done | bytes 1048608 | tf_op jit(solution)/shard_map/ppermute | solution.py:454
  217.0 2.0 sums.12.refs_2_
  219.3 3.6 %collective-permute-start.28 = (f32[1,768,128]{2,1,0:T(8,128)}, f32[1,768,128]{2,1,0:T(8,128)}, u32[]{:S(2)}, u32[]{:S(2)}) collective-permute-start(f32[1,768,128]{2,1,0:T(8,128)} %get-tuple-element.151), channel_id=1, source_target_pairs={{0,16},{4,20},{8,24},{12,28},{16,0},{20,4},{24,8},{28,12},{1,17},{... | collective-permute-start | bytes 1179656 | tf_op jit(solution)/shard_map/ppermute | solution.py:454
  223.3 3.7 %collective-permute-start.27 = (f32[1,768,128]{2,1,0:T(8,128)}, f32[1,768,128]{2,1,0:T(8,128)}, u32[]{:S(2)}, u32[]{:S(2)}) collective-permute-start(f32[1,768,128]{2,1,0:T(8,128)} %get-tuple-element.143.refs_7_), channel_id=1, source_target_pairs={{0,16},{4,20},{8,24},{12,28},{16,0},{20,4},{24,8},{28,12},{1,17},{... | collective-permute-start | bytes 1179656 | tf_op jit(solution)/shard_map/ppermute | solution.py:454
  229.2 1.9 sums.14.refs_2_
  231.0 17.7 %collective-permute-done.20.refs_1_ = f32[80,128]{1,0:T(8,128)} collective-permute-done((f32[80,128]{1,0:T(8,128)}, f32[80,128]{1,0:T(8,128)}, u32[]{:S(2)}, u32[]{:S(2)}) %collective-permute-start.20) | collective-permute-done | bytes 40992 | tf_op jit(solution)/shard_map/ppermute | solution.py:454
  250.1 4.4 %collective-permute-start.22 = (f32[80,128]{1,0:T(8,128)}, f32[80,128]{1,0:T(8,128)}, u32[]{:S(2)}, u32[]{:S(2)}) collective-permute-start(f32[80,128]{1,0:T(8,128)} %sums.15.refs_3_.refs_0_), channel_id=1, source_target_pairs={{0,16},{4,20},{8,24},{12,28},{16,0},{20,4},{24,8},{28,12},{1,17},{... | collective-permute-start | bytes 122888 | tf_op jit(solution)/shard_map/ppermute | solution.py:454
  254.6 1.8 sums.16.refs_2_
  256.5 9.5 %collective-permute-done.22.refs_1_ = f32[80,128]{1,0:T(8,128)} collective-permute-done((f32[80,128]{1,0:T(8,128)}, f32[80,128]{1,0:T(8,128)}, u32[]{:S(2)}, u32[]{:S(2)}) %collective-permute-start.22) | collective-permute-done | bytes 40992 | tf_op jit(solution)/shard_map/ppermute | solution.py:454
  267.6 3.0 %finish_feed.1 = (f32[1024,128]{1,0:T(8,128)}, f32[128,1024]{1,0:T(8,128)}) custom-call(f32[1,512,128]{2,1,0:T(8,128)} %reduce-scatter.2.cloned.1.call-done.refs_0_, f32[2,768,128]{2,1,0:T(8,128)} %get-tuple-element.135.refs_0_.refs_1_, f32[4,768,128]{2,1,0:T(8,128)} %collective-permute-done.5.refs_1_.refs_2_, ...), custom_call_target="tpu_custom_call" | custom-call | tf_op jit(solution)/shard_map/finish_feed/pallas_call | solution.py:72
  270.7 3.7 %collective-permute-done.25.refs_3_ = f32[1,512,128]{2,1,0:T(8,128)} collective-permute-done((f32[1,512,128]{2,1,0:T(8,128)}, f32[1,512,128]{2,1,0:T(8,128)}, u32[]{:S(2)}, u32[]{:S(2)}) %collective-permute-start.25) | collective-permute-done | bytes 262176 | tf_op jit(solution)/shard_map/ppermute | solution.py:454
  274.4 7.0 %collective-permute-done.26.refs_7_ = f32[1,512,128]{2,1,0:T(8,128)} collective-permute-done((f32[1,512,128]{2,1,0:T(8,128)}, f32[1,512,128]{2,1,0:T(8,128)}, u32[]{:S(2)}, u32[]{:S(2)}) %collective-permute-start.26) | collective-permute-done | bytes 262176 | tf_op jit(solution)/shard_map/ppermute | solution.py:454
  281.4 2.4 finish_heads.1
  285.2 5.1 %finish_input.1 = f32[512,1024]{1,0:T(8,128)} custom-call(bf16[2048,1024]{1,0:T(8,128)(2,1)} %refs_0_.17, bf16[2048,1024]{1,0:T(8,128)(2,1)} %refs_1_.7, f32[1,1024]{1,0:T(1,128)} %bitcast.12, f32[2,512,1024]{2,1,0:T(8,128)} %get-tuple-element.125.refs_8_.refs_0_.refs_3_, f32[512,1024]{1,0:T(8,128)} %collective-permute-done.15.refs_3_.refs_4_, ...), custom_call_target="tpu_custom_call" | custom-call | tf_op jit(solution)/shard_map/finish_input/pallas_call | solution.py:72
  (57 shorter events, 31.1 us)
Async XLA Ops:
  7.2 260.5 %reduce-scatter.2.cloned.1.call-start = ((), (), s32[]{:S(2)}) async-start(), calls=%async_computation.1 | async-start | bytes 2359296 | tf_op jit(solution)/shard_map/reduce_scatter | solution.py:1080
  29.3 12.2 %collective-permute-start = (f32[256,128]{1,0:T(8,128)}, f32[256,128]{1,0:T(8,128)}, u32[]{:S(2)}, u32[]{:S(2)}) collective-permute-start(f32[256,128]{1,0:T(8,128)} %get-tuple-element.95.refs_1_), channel_id=1, source_target_pairs={{0,4},{4,0},{8,12},{12,8},{16,20},{20,16},{24,28},{28,24},{1,5},{5... | collective-permute-start | bytes 393224 | tf_op jit(solution)/shard_map/ppermute | solution.py:454
  43.2 5.3 %collective-permute-start.1 = (f32[256,128]{1,0:T(8,128)}, f32[256,128]{1,0:T(8,128)}, u32[]{:S(2)}, u32[]{:S(2)}) collective-permute-start(f32[256,128]{1,0:T(8,128)} %get-tuple-element.97.refs_2_), channel_id=1, source_target_pairs={{0,8},{4,12},{8,0},{12,4},{16,24},{20,28},{24,16},{28,20},{1,9},{5... | collective-permute-start | bytes 393224 | tf_op jit(solution)/shard_map/ppermute | solution.py:454
  50.3 25.9 %collective-permute-start.2 = (f32[256,128]{1,0:T(8,128)}, f32[256,128]{1,0:T(8,128)}, u32[]{:S(2)}, u32[]{:S(2)}) collective-permute-start(f32[256,128]{1,0:T(8,128)} %get-tuple-element.100.refs_16_), channel_id=1, source_target_pairs={{0,16},{4,20},{8,24},{12,28},{16,0},{20,4},{24,8},{28,12},{1,17},{... | collective-permute-start | bytes 393224 | tf_op jit(solution)/shard_map/ppermute | solution.py:454
  74.0 39.6 %collective-permute-start.5 = (f32[4,768,128]{2,1,0:T(8,128)}, f32[4,768,128]{2,1,0:T(8,128)}, u32[]{:S(2)}, u32[]{:S(2)}) collective-permute-start(f32[4,768,128]{2,1,0:T(8,128)} %get-tuple-element.105), channel_id=1, source_target_pairs={{0,4},{4,0},{8,12},{12,8},{16,20},{20,16},{24,28},{28,24},{1,5},{5... | collective-permute-start | bytes 4718600 | tf_op jit(solution)/shard_map/ppermute | solution.py:454
  74.6 39.1 %collective-permute-start.6 = (f32[4,768,128]{2,1,0:T(8,128)}, f32[4,768,128]{2,1,0:T(8,128)}, u32[]{:S(2)}, u32[]{:S(2)}) collective-permute-start(f32[4,768,128]{2,1,0:T(8,128)} %get-tuple-element.107), channel_id=1, source_target_pairs={{0,8},{4,12},{8,0},{12,4},{16,24},{20,28},{24,16},{28,20},{1,9},{5... | collective-permute-start | bytes 4718600 | tf_op jit(solution)/shard_map/ppermute | solution.py:454
  112.1 5.3 %collective-permute-start.4 = (f32[256,128]{1,0:T(8,128)}, f32[256,128]{1,0:T(8,128)}, u32[]{:S(2)}, u32[]{:S(2)}) collective-permute-start(f32[256,128]{1,0:T(8,128)} %get-tuple-element.103.refs_1_), channel_id=1, source_target_pairs={{0,4},{4,0},{8,12},{12,8},{16,20},{20,16},{24,28},{28,24},{1,5},{5... | collective-permute-start | bytes 393224 | tf_op jit(solution)/shard_map/ppermute | solution.py:454
  113.6 7.5 %collective-permute-start.3 = (f32[2,512,1024]{2,1,0:T(8,128)}, f32[2,512,1024]{2,1,0:T(8,128)}, u32[]{:S(2)}, u32[]{:S(2)}) collective-permute-start(f32[2,512,1024]{2,1,0:T(8,128)} %get-tuple-element.102), channel_id=1, source_target_pairs={{0,1},{1,0},{2,3},{3,2},{4,5},{5,4},{6,7},{7,6},{8,9},{9,8},{10,11... | collective-permute-start | bytes 12582920 | tf_op jit(solution)/shard_map/ppermute | solution.py:454
  119.1 5.5 %collective-permute-start.8 = (f32[256,128]{1,0:T(8,128)}, f32[256,128]{1,0:T(8,128)}, u32[]{:S(2)}, u32[]{:S(2)}) collective-permute-start(f32[256,128]{1,0:T(8,128)} %get-tuple-element.120.refs_2_), channel_id=1, source_target_pairs={{0,8},{4,12},{8,0},{12,4},{16,24},{20,28},{24,16},{28,20},{1,9},{5... | collective-permute-start | bytes 393224 | tf_op jit(solution)/shard_map/ppermute | solution.py:454
  126.5 9.3 %collective-permute-start.9 = (f32[256,128]{1,0:T(8,128)}, f32[256,128]{1,0:T(8,128)}, u32[]{:S(2)}, u32[]{:S(2)}) collective-permute-start(f32[256,128]{1,0:T(8,128)} %get-tuple-element.122.refs_19_), channel_id=1, source_target_pairs={{0,16},{4,20},{8,24},{12,28},{16,0},{20,4},{24,8},{28,12},{1,17},{... | collective-permute-start | bytes 393224 | tf_op jit(solution)/shard_map/ppermute | solution.py:454
  126.8 37.0 %collective-permute-start.14 = (f32[4,512,128]{2,1,0:T(8,128)}, f32[4,512,128]{2,1,0:T(8,128)}, u32[]{:S(2)}, u32[]{:S(2)}) collective-permute-start(f32[4,512,128]{2,1,0:T(8,128)} %get-tuple-element.140), channel_id=1, source_target_pairs={{0,4},{4,0},{8,12},{12,8},{16,20},{20,16},{24,28},{28,24},{1,5},{5... | collective-permute-start | bytes 3145736 | tf_op jit(solution)/shard_map/ppermute | solution.py:454
  128.1 60.5 %collective-permute-start.7 = (f32[512,1024]{1,0:T(8,128)}, f32[512,1024]{1,0:T(8,128)}, u32[]{:S(2)}, u32[]{:S(2)}) collective-permute-start(f32[512,1024]{1,0:T(8,128)} %far_sums.2.refs_4_), channel_id=1, source_target_pairs={{0,2},{1,3},{2,0},{3,1},{4,6},{5,7},{6,4},{7,5},{8,10},{9,11},{10,... | collective-permute-start | bytes 6291464 | tf_op jit(solution)/shard_map/ppermute | solution.py:454
  130.2 37.6 %collective-permute-start.12 = (f32[2,768,128]{2,1,0:T(8,128)}, f32[2,768,128]{2,1,0:T(8,128)}, u32[]{:S(2)}, u32[]{:S(2)}) collective-permute-start(f32[2,768,128]{2,1,0:T(8,128)} %get-tuple-element.136), channel_id=1, source_target_pairs={{0,8},{4,12},{8,0},{12,4},{16,24},{20,28},{24,16},{28,20},{1,9},{5... | collective-permute-start | bytes 2359304 | tf_op jit(solution)/shard_map/ppermute | solution.py:454
  130.7 47.7 %collective-permute-start.13 = (f32[2,768,128]{2,1,0:T(8,128)}, f32[2,768,128]{2,1,0:T(8,128)}, u32[]{:S(2)}, u32[]{:S(2)}) collective-permute-start(f32[2,768,128]{2,1,0:T(8,128)} %get-tuple-element.138), channel_id=1, source_target_pairs={{0,4},{4,0},{8,12},{12,8},{16,20},{20,16},{24,28},{28,24},{1,5},{5... | collective-permute-start | bytes 2359304 | tf_op jit(solution)/shard_map/ppermute | solution.py:454
  163.7 19.3 %collective-permute-start.10 = (f32[256,1024]{1,0:T(8,128)}, f32[256,1024]{1,0:T(8,128)}, u32[]{:S(2)}, u32[]{:S(2)}) collective-permute-start(f32[256,1024]{1,0:T(8,128)} %get-tuple-element.126), channel_id=1, source_target_pairs={{0,1},{1,0},{2,3},{3,2},{4,5},{5,4},{6,7},{7,6},{8,9},{9,8},{10,11... | collective-permute-start | bytes 3145736 | tf_op jit(solution)/shard_map/ppermute | solution.py:454
  163.8 19.2 %collective-permute-start.11 = (f32[256,1024]{1,0:T(8,128)}, f32[256,1024]{1,0:T(8,128)}, u32[]{:S(2)}, u32[]{:S(2)}) collective-permute-start(f32[256,1024]{1,0:T(8,128)} %get-tuple-element.127), channel_id=1, source_target_pairs={{0,1},{1,0},{2,3},{3,2},{4,5},{5,4},{6,7},{7,6},{8,9},{9,8},{10,11... | collective-permute-start | bytes 3145736 | tf_op jit(solution)/shard_map/ppermute | solution.py:454
  181.4 11.7 %collective-permute-start.15 = (f32[512,1024]{1,0:T(8,128)}, f32[512,1024]{1,0:T(8,128)}, u32[]{:S(2)}, u32[]{:S(2)}) collective-permute-start(f32[512,1024]{1,0:T(8,128)} %get-tuple-element.144), channel_id=1, source_target_pairs={{0,1},{1,0},{2,3},{3,2},{4,5},{5,4},{6,7},{7,6},{8,9},{9,8},{10,11... | collective-permute-start | bytes 6291464 | tf_op jit(solution)/shard_map/ppermute | solution.py:454
  186.4 98.8 %collective-permute-start.16 = (f32[512,1024]{1,0:T(8,128)}, f32[512,1024]{1,0:T(8,128)}, u32[]{:S(2)}, u32[]{:S(2)}) collective-permute-start(f32[512,1024]{1,0:T(8,128)} %far_sums.3.refs_5_), channel_id=1, source_target_pairs={{0,2},{1,3},{2,0},{3,1},{4,6},{5,7},{6,4},{7,5},{8,10},{9,11},{10,... | collective-permute-start | bytes 6291464 | tf_op jit(solution)/shard_map/ppermute | solution.py:454
  188.7 28.3 %collective-permute-start.19 = (f32[4,512,128]{2,1,0:T(8,128)}, f32[4,512,128]{2,1,0:T(8,128)}, u32[]{:S(2)}, u32[]{:S(2)}) collective-permute-start(f32[4,512,128]{2,1,0:T(8,128)} %get-tuple-element.146), channel_id=1, source_target_pairs={{0,4},{4,0},{8,12},{12,8},{16,20},{20,16},{24,28},{28,24},{1,5},{5... | collective-permute-start | bytes 3145736 | tf_op jit(solution)/shard_map/ppermute | solution.py:454
  188.7 39.7 %collective-permute-start.21 = (f32[2,512,128]{2,1,0:T(8,128)}, f32[2,512,128]{2,1,0:T(8,128)}, u32[]{:S(2)}, u32[]{:S(2)}) collective-permute-start(f32[2,512,128]{2,1,0:T(8,128)} %get-tuple-element.148), channel_id=1, source_target_pairs={{0,8},{4,12},{8,0},{12,4},{16,24},{20,28},{24,16},{28,20},{1,9},{5... | collective-permute-start | bytes 1572872 | tf_op jit(solution)/shard_map/ppermute | solution.py:454
  188.7 4.5 %collective-permute-start.17 = (f32[80,128]{1,0:T(8,128)}, f32[80,128]{1,0:T(8,128)}, u32[]{:S(2)}, u32[]{:S(2)}) collective-permute-start(f32[80,128]{1,0:T(8,128)} %pack_small.1.refs_3_.refs_0_), channel_id=1, source_target_pairs={{0,1},{1,0},{2,3},{3,2},{4,5},{5,4},{6,7},{7,6},{8,9},{9,8},{10,11... | collective-permute-start | bytes 122888 | tf_op jit(solution)/shard_map/ppermute | solution.py:454
  219.0 35.6 %collective-permute-start.23 = (f32[2,512,128]{2,1,0:T(8,128)}, f32[2,512,128]{2,1,0:T(8,128)}, u32[]{:S(2)}, u32[]{:S(2)}) collective-permute-start(f32[2,512,128]{2,1,0:T(8,128)} %sums.12.refs_2_), channel_id=1, source_target_pairs={{0,8},{4,12},{8,0},{12,4},{16,24},{20,28},{24,16},{28,20},{1,9},{5... | collective-permute-start | bytes 1572872 | tf_op jit(solution)/shard_map/ppermute | solution.py:454
  219.0 4.3 %collective-permute-start.18 = (f32[80,128]{1,0:T(8,128)}, f32[80,128]{1,0:T(8,128)}, u32[]{:S(2)}, u32[]{:S(2)}) collective-permute-start(f32[80,128]{1,0:T(8,128)} %sums.11.refs_2_.refs_0_), channel_id=1, source_target_pairs={{0,4},{4,0},{8,12},{12,8},{16,20},{20,16},{24,28},{28,24},{1,5},{5... | collective-permute-start | bytes 122888 | tf_op jit(solution)/shard_map/ppermute | solution.py:454
  219.3 48.0 %collective-permute-start.28 = (f32[1,768,128]{2,1,0:T(8,128)}, f32[1,768,128]{2,1,0:T(8,128)}, u32[]{:S(2)}, u32[]{:S(2)}) collective-permute-start(f32[1,768,128]{2,1,0:T(8,128)} %get-tuple-element.151), channel_id=1, source_target_pairs={{0,16},{4,20},{8,24},{12,28},{16,0},{20,4},{24,8},{28,12},{1,17},{... | collective-permute-start | bytes 1179656 | tf_op jit(solution)/shard_map/ppermute | solution.py:454
  223.3 44.3 %collective-permute-start.27 = (f32[1,768,128]{2,1,0:T(8,128)}, f32[1,768,128]{2,1,0:T(8,128)}, u32[]{:S(2)}, u32[]{:S(2)}) collective-permute-start(f32[1,768,128]{2,1,0:T(8,128)} %get-tuple-element.143.refs_7_), channel_id=1, source_target_pairs={{0,16},{4,20},{8,24},{12,28},{16,0},{20,4},{24,8},{28,12},{1,17},{... | collective-permute-start | bytes 1179656 | tf_op jit(solution)/shard_map/ppermute | solution.py:454
  228.4 20.3 %collective-permute-start.20 = (f32[80,128]{1,0:T(8,128)}, f32[80,128]{1,0:T(8,128)}, u32[]{:S(2)}, u32[]{:S(2)}) collective-permute-start(f32[80,128]{1,0:T(8,128)} %sums.13.refs_3_.refs_0_), channel_id=1, source_target_pairs={{0,8},{4,12},{8,0},{12,4},{16,24},{20,28},{24,16},{28,20},{1,9},{5... | collective-permute-start | bytes 122888 | tf_op jit(solution)/shard_map/ppermute | solution.py:454
  250.1 15.8 %collective-permute-start.22 = (f32[80,128]{1,0:T(8,128)}, f32[80,128]{1,0:T(8,128)}, u32[]{:S(2)}, u32[]{:S(2)}) collective-permute-start(f32[80,128]{1,0:T(8,128)} %sums.15.refs_3_.refs_0_), channel_id=1, source_target_pairs={{0,16},{4,20},{8,24},{12,28},{16,0},{20,4},{24,8},{28,12},{1,17},{... | collective-permute-start | bytes 122888 | tf_op jit(solution)/shard_map/ppermute | solution.py:454
  254.6 19.8 %collective-permute-start.25 = (f32[1,512,128]{2,1,0:T(8,128)}, f32[1,512,128]{2,1,0:T(8,128)}, u32[]{:S(2)}, u32[]{:S(2)}) collective-permute-start(f32[1,512,128]{2,1,0:T(8,128)} %sums.14.refs_2_), channel_id=1, source_target_pairs={{0,16},{4,20},{8,24},{12,28},{16,0},{20,4},{24,8},{28,12},{1,17},{... | collective-permute-start | bytes 786440 | tf_op jit(solution)/shard_map/ppermute | solution.py:454
  265.9 15.5 %collective-permute-start.26 = (f32[1,512,128]{2,1,0:T(8,128)}, f32[1,512,128]{2,1,0:T(8,128)}, u32[]{:S(2)}, u32[]{:S(2)}) collective-permute-start(f32[1,512,128]{2,1,0:T(8,128)} %sums.16.refs_2_), channel_id=1, source_target_pairs={{0,16},{4,20},{8,24},{12,28},{16,0},{20,4},{24,8},{28,12},{1,17},{... | collective-permute-start | bytes 786440 | tf_op jit(solution)/shard_map/ppermute | solution.py:454
  267.4 16.4 %collective-permute-start.24 = (f32[80,128]{1,0:T(8,128)}, f32[80,128]{1,0:T(8,128)}, u32[]{:S(2)}, u32[]{:S(2)}) collective-permute-start(f32[80,128]{1,0:T(8,128)} %sums.17.refs_9_.refs_0_), channel_id=1, source_target_pairs={{0,2},{1,3},{2,0},{3,1},{4,6},{5,7},{6,4},{7,5},{8,10},{9,11},{10,... | collective-permute-start | bytes 122888 | tf_op jit(solution)/shard_map/ppermute | solution.py:454
Sparse Core Ops, SparseCore 0:
  126.9 80.9 reduce-scatter.1

commit v3 on v2

--- a/solution.py
+++ b/solution.py
@@ -19,8 +19,12 @@
 HALF_ROOT = math.sqrt(0.5)
 GAUSS = 1.0 / math.sqrt(2.0 * math.pi)
 VMEM_BYTES = 64 * 2**20
-LONG = 2**40
-SHORT = 2**35
+STEP = 2**30
+COST_FAR = 13 * STEP
+COST_NEAR = 0
+COST_END = 10 * STEP
+COST_ATTEND = 16 * STEP
+COST_KEYS = 50 * STEP
 PARTS = ((3, 1), (0, 3))
 
 
@@ -168,21 +172,32 @@
     return value * cosine + moved if sign > 0 else value * cosine - moved
 
 
-def fold_state(full, head, width):
-    block = head_block(head, width, width)
-    s_part = jnp.where(block, full[:, :width], 0.0)
-    n_part = jnp.where(block, full[:, width:], 0.0)
-    s_fold = sum(s_part[:, i * LANE : (i + 1) * LANE] for i in range(width // LANE))
-    n_fold = sum(n_part[:, i * LANE : (i + 1) * LANE] for i in range(width // LANE))
-    return s_fold + pltpu.roll(n_fold, LANE // 2, 1)
-
-
-def unfold_state(packed, head, width):
-    block = head_block(head, width, width)
-    times = width // LANE
-    s_part = beside(*[packed] * times)
-    n_part = beside(*[pltpu.roll(packed, LANE // 2, 1)] * times)
-    return beside(jnp.where(block, s_part, 0.0), jnp.where(block, n_part, 0.0))
+def own_half(head, rows):
+    return iota((rows, LANE), 1) // head == iota((rows, LANE), 0) // head % 2
+
+
+def pairs_of(width):
+    return [slice(p, p + LANE) for p in range(0, width, LANE)]
+
+
+def outer_pairs(left, right, other):
+    return below(
+        *[tn(left[:, p], beside(right[:, p], other[:, p])) for p in pairs_of(left.shape[1])]
+    )
+
+
+def masked_state(full, head):
+    half = own_half(head, full.shape[0])
+    return jnp.where(beside(half, half), full, 0.0)
+
+
+def fold_state(full, head):
+    full = masked_state(full, head)
+    return full[:, :LANE] + pltpu.roll(full[:, LANE:], LANE // 2, 1)
+
+
+def unfold_state(packed, head):
+    return masked_state(beside(packed, pltpu.roll(packed, LANE // 2, 1)), head)
 
 
 def deal(outs, order, low, write):
@@ -284,9 +299,9 @@
 def features(part, tables, basis, head, feats):
     width = part.shape[1]
     turned = turn(part.astype(f32), tables, 1)
-    square = two(turned * turned)
+    square = (turned * turned).astype(bf16)
     ones = jnp.where(head_block(head, width, width), 1.0 / (2.0 * math.sqrt(head)), 0.0).astype(bf16)
-    argument = exact3(nn, two(turned), basis) - (nn(square[0], ones) + nn(square[1], ones))
+    argument = exact3(nn, two(turned), basis) - nn(square, ones)
     return turned.astype(bf16), (jnp.exp(argument) * (1.0 / math.sqrt(feats))).astype(bf16)
 
 
@@ -321,7 +336,7 @@
 
     def body(
         lengths, x, gain, shift, up_w, up_b, down_w, cot, qkv_w, qkv_b, expand, samples, dct_t,
-        normed_o, cb_o, kf_o, v_o, kt_o, w_o, basis_o, cs_o, state_o, hidden_o, gpre_o, ub_o, piece_o,
+        normed_o, cb_o, kf_o, v_o, kt_o, w_o, b_o, basis_o, cs_o, state_o, hidden_o, gpre_o, ub_o, piece_o,
         down_acc, up_acc, w_s, b_s, basis_s, cs_s, state_s,
     ):
         step = pl.program_id(0)
@@ -332,8 +347,8 @@
         @pl.when(step == 0)
         def _():
             clear(down_acc, up_acc, ub_o, cb_o, state_s)
-            for part in (1, 2):
-                to = slice((part - 1) * width, part * width)
+            for part in range(3):
+                to = slice(part * width, (part + 1) * width)
                 w_s[:, to] = take_columns(qkv_w, head, heads, part)
                 b_s[:, to] = take_columns(qkv_b, head, heads, part)
             basis = lax.dot_general(
@@ -345,6 +360,7 @@
             basis_s[...] = jnp.where(head_block(head, width, width), wide, 0.0)
             basis_o[...] = basis_s[...]
             w_o[...] = w_s[...]
+            b_o[...] = b_s[...]
             rotary_table(ends, first_pos, ROWS, tokens, cs_s)
             cs_o[...] = cs_s[...]
 
@@ -357,18 +373,18 @@
         cb_o[...] += jnp.sum(c.astype(f32).reshape(ROWS // 8, 8, model), axis=0)
         feed_step(normed, c, up_w, up_b, down_w, hidden_o, gpre_o, ub_o, down_acc, up_acc)
 
-        projected = (nn(normed, w_s[...]) + b_s[...]).astype(bf16)
+        projected = (nn(normed, w_s[:, width:]) + b_s[:, width:]).astype(bf16)
         tables = turn_tables(cs_s[step], expand[...], head, width)
         k_turn, k_feat = features(projected[:, :width], tables, two(basis_s[...]), head, feats)
         value = projected[:, width:]
         kf_o[...], v_o[...], kt_o[...] = k_feat, value, k_turn
         place = first_pos + step * ROWS + iota((ROWS, 1), 0)
         tail = jnp.where(place >= start_last, 1.0, 0.0).astype(bf16)
-        state_s[...] += tn(k_feat * tail, beside(value, jnp.ones_like(value)))
+        state_s[...] += outer_pairs(k_feat * tail, value, jnp.ones_like(value))
 
         @pl.when(step == pl.num_programs(0) - 1)
         def _():
-            state_o[...] = fold_state(state_s[...], head, width)
+            state_o[...] = fold_state(state_s[...], head)
             for i in range(piece.shape[0]):
                 write_down(piece_o, i, i * LANE, down_acc)
                 write_up(piece_o, i, i * LANE, up_acc)
@@ -380,71 +396,52 @@
         [SMEM, rows_at(ROWS, model), whole(1, model), whole(1, model), *ins]
         + [whole(*a.shape) for a in (qkv_w, qkv_b, expand, samples, dct_t)],
         [rows_at(ROWS, model), whole(8, model), *[rows_at(ROWS, width)] * 3]
-        + [whole(model, 2 * width), whole(width, width), whole(*table), whole(width, LANE), *outs]
+        + [whole(model, 3 * width), whole(1, 3 * width), whole(width, width), whole(*table)]
+        + [whole(width, LANE), *outs]
         + [whole(*piece.shape)],
         [shaped((tokens, model), bf16), shaped((8, model)), *[narrow] * 3]
-        + [shaped((model, 2 * width), bf16), shaped((width, width)), shaped(table, bf16)]
+        + [shaped((model, 3 * width), bf16), shaped((1, 3 * width)), shaped((width, width))]
+        + [shaped(table, bf16)]
         + [shaped((width, LANE)), *shapes, piece],
         grid=(blocks,),
         scratch_shapes=[
             *scratch,
-            pltpu.VMEM((model, 2 * width), bf16),
-            pltpu.VMEM((1, 2 * width), f32),
+            pltpu.VMEM((model, 3 * width), bf16),
+            pltpu.VMEM((1, 3 * width), f32),
             pltpu.VMEM((width, width), f32),
             pltpu.VMEM(table, bf16),
-            pltpu.VMEM((width, 2 * width), f32),
+            pltpu.VMEM((width, 2 * LANE), f32),
         ],
         name="front",
     )
 
 
-def project_queries_kernel(
-    head, feats, normed, w_in, b_in, expand, basis, cs, cot, out_w, qf_o, qt_o, ga_o, w_o, w_s, b_s
-):
-    width = out_w.shape[0]
-    heads = width // head
-
-    @pl.when(pl.program_id(0) == 0)
-    def _():
-        w_s[...] = take_columns(w_in, head, heads, 0)
-        b_s[...] = take_columns(b_in, head, heads, 0)
-        w_o[...] = w_s[...]
-
-    projected = (nn(normed[...], w_s[...]) + b_s[...]).astype(bf16)
-    ga_o[...] = nt(cot[...], out_w[...])
-    tables = turn_tables(cs[0], expand[...], head, width)
-    qt_o[...], qf_o[...] = features(projected, tables, two(basis[...]), head, feats)
-
-
-def project_queries(call, head, feats, normed, w_in, b_in, expand, basis, cs, cot, out_w):
+def project_queries(call, head, feats, normed, w, b, expand, basis, cs, cot, out_w):
     tokens, model = normed.shape
     width = out_w.shape[0]
 
-    def body(*refs):
-        project_queries_kernel(head, feats, *refs)
+    def body(normed, w, b, expand, basis, cs, cot, out_w, qf_o, qt_o, ga_o):
+        projected = (nn(normed[...], w[...]) + b[...]).astype(bf16)
+        ga_o[...] = nt(cot[...], out_w[...])
+        tables = turn_tables(cs[0], expand[...], head, width)
+        qt_o[...], qf_o[...] = features(projected, tables, two(basis[...]), head, feats)
 
     return call(
         body,
-        (normed, w_in, b_in, expand, basis, cs, cot, out_w),
+        (normed, w, b, expand, basis, cs, cot, out_w),
         [
             rows_at(ROWS, model),
-            whole(*w_in.shape),
-            whole(*b_in.shape),
+            whole(model, width),
+            whole(1, width),
             whole(*expand.shape),
             whole(*basis.shape),
             pl.BlockSpec((1,) + cs.shape[1:], lambda i: (i, 0, 0)),
             rows_at(ROWS, model),
             whole(*out_w.shape),
         ],
-        [rows_at(ROWS, width)] * 3 + [whole(model, width)],
-        [
-            shaped((tokens, width), bf16),
-            shaped((tokens, width), bf16),
-            shaped((tokens, width)),
-            shaped((model, width), bf16),
-        ],
+        [rows_at(ROWS, width)] * 3,
+        [shaped((tokens, width), bf16), shaped((tokens, width), bf16), shaped((tokens, width))],
         grid=(tokens // ROWS,),
-        scratch_shapes=[pltpu.VMEM((model, width), bf16), pltpu.VMEM((1, width), f32)],
         name="project_queries",
     )
 
@@ -506,19 +503,18 @@
 
 
 def turned_grad(grad_feat, feat, turned, basis, tables, head, width):
-    weighted = two(grad_feat * feat.astype(f32))
+    weighted = (grad_feat * feat.astype(f32)).astype(bf16)
     ones = jnp.where(head_block(head, width, width), 1.0 / math.sqrt(head), 0.0).astype(bf16)
-    total = nn(weighted[0], ones) + nn(weighted[1], ones)
-    grad = exact3(nt, weighted, basis) - total * turned.astype(f32)
+    grad = nt(beside(weighted, weighted), beside(*basis)) - nn(weighted, ones) * turned.astype(f32)
     return turn(grad, tables, -1).astype(bf16)
 
 
 def attend_kernel(
-    head, order, low, tokens, per_step, base, lengths, qf, kf, v, qt, ga, cs, expand, basis_i,
+    head, tokens, per_step, base, lengths, qf, kf, v, qt, ga, cs, expand, basis_i,
     normed, cot, hidden0, hidden1, down_w, out_w, entered_i, own_i, came_i,
     gq_o, gk_o, gv_o, back_o, total_o, qb_o, send_o, keep_o, *refs,
 ):
-    *piece, state_s, q_acc, o_acc, total_s = refs
+    piece_o, state_s, q_acc, o_acc, total_s = refs
     step = pl.program_id(0)
     width = qf.shape[1]
     heads = width // head
@@ -530,7 +526,7 @@
         entered, _ = joined(
             True, lengths, tokens, base, entered_i[...], own_i[...], came_i[...]
         )
-        state_s[...] = unfold_state(entered, head, width)
+        state_s[...] = unfold_state(entered, head)
         q_acc[...] = jnp.zeros_like(q_acc)
         o_acc[...] = jnp.zeros_like(o_acc)
         total_s[...] = jnp.zeros_like(total_s)
@@ -538,64 +534,99 @@
 
     basis = two(basis_i[...])
     block = head_block(head, width, width)
-    both = beside(block, block)
     ones = jnp.where(block, 1.0, 0.0).astype(bf16)
     lanes = [jnp.where(iota((1, width), 1) // head == h, 1.0, 0.0).astype(bf16) for h in range(heads)]
     state = state_s[...]
     total = total_s[...]
     part = hidden0.shape[1]
-    outward = nn(hidden1[...], down_w[:-part]) + nn(hidden0[...], down_w[-part:])
-    mixes = []
-    for sub in range(per_step):
-        at = slice(sub * CHUNK, (sub + 1) * CHUNK)
+    subs = range(per_step)
+    ats = [slice(sub * CHUNK, (sub + 1) * CHUNK) for sub in subs]
+    row = iota((CHUNK, 1), 0)
+    col = iota((CHUNK, CHUNK), 1)
+    causal = col <= iota((CHUNK, CHUNK), 0)
+    windows, carries, states, live = [], [], [], []
+    for sub, at in zip(subs, ats):
         begin = first_pos + (step * per_step + sub) * CHUNK
         last = seq_start(ends, begin + CHUNK - 1)
-        row = iota((CHUNK, 1), 0)
         start = seq_start(ends, begin + row)
-        col = iota((CHUNK, CHUNK), 1)
-        window = (col <= iota((CHUNK, CHUNK), 0)) & (col + begin >= start)
-        carried = jnp.where(start < begin, 1.0, 0.0)
-        q, k, value = qf[at, :], kf[at, :], v[at, :]
-        q_carried = q * carried.astype(bf16)
-        state_two = two(state)
-        scores = [jnp.where(window, nt(q * lanes[h], k), 0.0).astype(bf16) for h in range(heads)]
-        right = [beside(value * lane, jnp.broadcast_to(lane, value.shape)) for lane in lanes]
-        sums = nn(beside(*scores, q_carried, q_carried), below(*right, *state_two))
-        over = 1.0 / sums[:, width:]
-        attended = sums[:, :width] * over
-        mixed = attended.astype(bf16)
-        mixes.append(mixed)
-        grad_att = ga[at, :]
-        g_num = grad_att * over
-        product = two(grad_att * attended)
-        g_den = -nn(beside(*product), below(ones, ones)) * over
-        g_low = g_num.astype(bf16)
-        g_both = two(beside(g_num, g_den * (1.0 / head)))
-        from_state = nt(
-            beside(g_both[0], g_both[0], g_both[1]), beside(state_two[0], state_two[1], state_two[0])
-        )
-        g_heads = [g_low * lane for lane in lanes]
-        mixing = [
-            jnp.where(window, nt(g_heads[h], value) + g_den[:, h * head : h * head + 1], 0.0).astype(bf16)
+        windows.append(causal & (col + begin >= start))
+        carries.append(jnp.where(start < begin, 1.0, 0.0))
+        live.append(jnp.where(seq_start(ends, begin - 1) < first_pos, 1.0, 0.0))
+        states.append(two(state))
+        tail = jnp.where(begin + row >= last, 1.0, 0.0).astype(bf16)
+        retain = jnp.where(last < begin, 1.0, 0.0)
+        value = v[at, :]
+        added = outer_pairs(kf[at, :] * tail, value, jnp.ones_like(value))
+        state = retain * state + masked_state(added, head)
+    scores = [
+        [jnp.where(window, nt(qf[at, :] * lane, kf[at, :]), 0.0).astype(bf16) for lane in lanes]
+        for at, window in zip(ats, windows)
+    ]
+    outward = nn(hidden1[...], down_w[:-part]) + nn(hidden0[...], down_w[-part:])
+    q_carries = [qf[at, :] * c.astype(bf16) for at, c in zip(ats, carries)]
+    attends, overs, mixes = [], [], []
+    for sub, at in zip(subs, ats):
+        nums, dens = [], []
+        for p, pair in enumerate(pairs_of(width)):
+            mine = range(p * LANE // head, (p + 1) * LANE // head)
+            right = [
+                beside(v[at, pair] * lanes[h][:, pair], jnp.broadcast_to(lanes[h][:, pair], (CHUNK, LANE)))
+                for h in mine
+            ]
+            carry = q_carries[sub][:, pair]
+            sums = nn(
+                beside(*[scores[sub][h] for h in mine], carry, carry),
+                below(*right, states[sub][0][pair, :], states[sub][1][pair, :]),
+            )
+            nums.append(sums[:, :LANE])
+            dens.append(sums[:, LANE:])
+        overs.append(1.0 / beside(*dens))
+        attends.append(beside(*nums) * overs[sub])
+        mixes.append(attends[sub].astype(bf16))
+    g_nums = [(ga[at, :] * over).astype(bf16) for at, over in zip(ats, overs)]
+    g_dens = []
+    for g_num, attended in zip(g_nums, attends):
+        product = two(g_num.astype(f32) * attended)
+        g_dens.append(-nn(beside(*product), below(ones, ones)))
+    g_heads = [[g_num * lane for lane in lanes] for g_num in g_nums]
+    mixing = [
+        [
+            jnp.where(
+                windows[sub], nt(g_heads[sub][h], v[at, :]) + g_dens[sub][:, h * head : h * head + 1], 0.0
+            ).astype(bf16)
             for h in range(heads)
         ]
-        grad_fq = carried * from_state + nn(beside(*mixing), below(*[k * lane for lane in lanes]))
-        gk_o[at, :] = tn(below(*mixing), below(*[q * lane for lane in lanes]))
-        gv_o[at, :] = tn(below(*scores), below(*g_heads))
-        back = tn(q_carried, beside(g_num, g_den).astype(bf16))
-        back_o[sub] = fold_state(back, head, width)
-        live = jnp.where(seq_start(ends, begin - 1) < first_pos, 1.0, 0.0)
-        total = total + live * back
-        tail = jnp.where(begin + row >= last, 1.0, 0.0).astype(bf16)
-        retain = jnp.where(last < begin, 1.0, 0.0)
-        added = tn(k * tail, beside(value, jnp.ones_like(value)))
-        state = retain * state + jnp.where(both, added, 0.0)
+        for sub, at in zip(subs, ats)
+    ]
+    grad_fqs = []
+    for sub, at in zip(subs, ats):
+        den_two = two(g_dens[sub] * (2.0 / head))
+        den_both = jnp.where(iota((1, width), 1) % head < head // 2, den_two[0], den_two[1])
+        from_state = []
+        for pair in pairs_of(width):
+            left = beside(g_nums[sub][:, pair], den_both[:, pair])
+            from_state.append(
+                nt(beside(left, left), beside(states[sub][0][pair, :], states[sub][1][pair, :]))
+            )
+        grad_fqs.append(
+            carries[sub] * beside(*from_state)
+            + nn(beside(*mixing[sub]), below(*[kf[at, :] * lane for lane in lanes]))
+        )
+    gqs = []
+    for sub, at in zip(subs, ats):
         tables = turn_tables(cs[0, :, at], expand[...], head, width)
-        gq = turned_grad(grad_fq, q, qt[at, :], basis, tables, head, width)
-        gq_o[at, :] = gq
-        qb_o[...] += jnp.sum(gq.astype(f32).reshape(CHUNK // 8, 8, width), axis=0)
-        q_acc[...] += tn(normed[at, :], gq)
-        o_acc[...] += tn(mixed, cot[at, :])
+        gqs.append(turned_grad(grad_fqs[sub], qf[at, :], qt[at, :], basis, tables, head, width))
+    for sub, at in zip(subs, ats):
+        gk_o[at, :] = tn(below(*mixing[sub]), below(*[qf[at, :] * lane for lane in lanes]))
+        gv_o[at, :] = tn(below(*scores[sub]), below(*g_heads[sub]))
+        back = fold_state(outer_pairs(q_carries[sub], g_nums[sub], g_dens[sub].astype(bf16)), head)
+        back_o[sub] = back
+        total = total + live[sub] * back
+    gq = below(*gqs)
+    gq_o[...] = gq
+    qb_o[...] += jnp.sum(gq.astype(f32).reshape(per_step * CHUNK // 8, 8, width), axis=0)
+    q_acc[...] += tn(normed[...], gq)
+    o_acc[...] += tn(below(*mixes), cot[...])
     state_s[...] = state
     total_s[...] = total
     outward = outward + nn(below(*mixes), out_w[...])
@@ -603,16 +634,11 @@
 
     @pl.when(step == pl.num_programs(0) - 1)
     def _():
-        total_o[...] = fold_state(total, head, width)
-
-        def write(out, i, spot):
-            out[i, :width, :] = o_acc[:, pl.ds(spot, LANE)]
-            for j in range(width // LANE):
-                out[i, width + j * LANE : width + (j + 1) * LANE, :] = q_acc[
-                    pl.ds(spot, LANE), j * LANE : (j + 1) * LANE
-                ]
-
-        deal(piece, order, low, write)
+        total_o[...] = total
+
+        for i in range(piece_o.shape[0]):
+            write_down(piece_o, i, i * LANE, o_acc)
+            write_up(piece_o, i, i * LANE, q_acc)
 
 
 def by_core(core, send, keep, value):
@@ -628,7 +654,7 @@
 
 
 def attend(
-    call, head, order, low, base, lengths, qf, kf, v, qt, ga, cs, expand, basis, normed, cot,
+    call, head, base, lengths, qf, kf, v, qt, ga, cs, expand, basis, normed, cot,
     hidden0, hidden1, down_w, out_w, entered, own, came, **rest,
 ):
     tokens, width = qf.shape
@@ -636,13 +662,13 @@
     per_step = ROWS // CHUNK
     chunks = tokens // CHUNK
     part = hidden0.shape[1]
-    firsts, piece = shaped((4, 2 * width, LANE)), shaped((2, 2 * width, LANE))
+    piece = shaped((model // LANE, 2 * width, LANE))
     chip = pl.BlockSpec((1, ROWS, model), lambda i: (i >> 1, 0, 0))
     row = rows_at(ROWS, width)
     packed = whole(width, LANE)
 
     def body(*refs):
-        attend_kernel(head, order, low, tokens, per_step, base, *refs)
+        attend_kernel(head, tokens, per_step, base, *refs)
 
     return call(
         body,
@@ -669,7 +695,7 @@
             whole(8, width),
             chip,
             chip,
-            *[whole(*a.shape) for a in (firsts, piece, piece)],
+            whole(*piece.shape),
         ],
         [
             shaped((tokens, width), bf16),
@@ -679,20 +705,18 @@
             shaped((width, LANE)),
             shaped((8, width)),
             *[shaped((tokens // ROWS // 2, ROWS, model))] * 2,
-            firsts,
-            piece,
             piece,
         ],
         **rest,
         grid=(tokens // ROWS,),
         scratch_shapes=[
-            pltpu.VMEM((width, 2 * width), f32),
+            pltpu.VMEM((width, 2 * LANE), f32),
             pltpu.VMEM((model, width), f32),
             pltpu.VMEM((width, model), f32),
-            pltpu.VMEM((width, 2 * width), f32),
+            pltpu.VMEM((width, LANE), f32),
         ],
         name="attend",
-        flops=LONG,
+        flops=COST_ATTEND,
     )
 
 
@@ -701,28 +725,21 @@
     return here & 1, here >> 1
 
 
-def share_at(i):
-    core, chip = branch_place()
-    return 2 * jnp.where(i < 2, 1 - chip, chip) + jnp.where(i & 1, core, 1 - core)
-
-
-def backward(
-    call, head, order, low, base, lengths, kf, v, kt, gk, gv, back, cs, expand, basis, normed, x,
-    gpre0, gpre1, gq, up_w, q_w, kv_w, entered, own, came, **rest,
+def keys(
+    call, head, order, low, base, lengths, kf, v, kt, gk, gv, back, cs, expand, basis, normed,
+    entered, own, came, **rest,
 ):
     tokens, width = kf.shape
     model = normed.shape[1]
-    part = gpre0.shape[1]
     chunks, per_step = tokens // CHUNK, ROWS // CHUNK
-    row = lambda n: pl.BlockSpec((ROWS, n), lambda i: (share_at(i), 0))
+    row = lambda n: rows_at(ROWS, n)
     packed = whole(width, LANE)
     firsts, piece = shaped((4, 2 * width, LANE)), shaped((2, 2 * width, LANE))
     acc_shape = (model, 2 * width)
 
     def body(
-        lengths, kf, v, kt, gk, gv, back, cs, expand, basis_i, normed, x, gpre0, gpre1, gq, up_w,
-        q_w, kv_w, entered_i, own_i, came_i, keep_o, far0_o, far1_o, near_o, kvb_o, gain_o, shift_o,
-        *refs,
+        lengths, kf, v, kt, gk, gv, back, cs, expand, basis_i, normed, entered_i, own_i, came_i,
+        gkv_o, kvb_o, *refs,
     ):
         *pieces, acc, state_s = refs
         step = pl.program_id(0)
@@ -731,7 +748,7 @@
 
         @pl.when(step == 0)
         def _():
-            clear(kvb_o, gain_o, shift_o, acc)
+            clear(kvb_o, acc)
             state, _ = joined(
                 False, lengths, tokens, base, entered_i[...], own_i[...], came_i[...]
             )
@@ -741,43 +758,88 @@
                 last = seq_start(ends, begin + CHUNK - 1)
                 state = back[chunk] + jnp.where(last < begin, state, 0.0)
 
-        grad = nt(gpre1[...], up_w[:, :-part]) + nt(gpre0[...], up_w[:, -part:])
         basis = two(basis_i[...])
         tables = turn_tables(cs[0], expand[...], head, width)
-        grads = []
+        share = jnp.full((CHUNK, LANE), 1.0 / head, bf16)
+        heres = [slice(sub * CHUNK, (sub + 1) * CHUNK) for sub in range(per_step)]
+        tails, states = [], []
         for sub in range(per_step):
-            here = slice(sub * CHUNK, (sub + 1) * CHUNK)
-            chunk = share_at(step) * per_step + sub
-            begin = first_pos + chunk * CHUNK
+            begin = first_pos + (step * per_step + sub) * CHUNK
             last = seq_start(ends, begin + CHUNK - 1)
-            tail = jnp.where(begin + iota((CHUNK, 1), 0) >= last, 1.0, 0.0)
-            k, value = kf[here, :], v[here, :]
-            state = two(unfold_state(state_s[chunk], head, width))
-            right = beside(value, jnp.full(value.shape, 1.0 / head, bf16))
-            grad_fk = gk[here, :] + tail * nt(beside(right, right), beside(*state))
-            grad_v = gv[here, :] + tail * nn(
-                beside(k, k), below(state[0][:, :width], state[1][:, :width])
-            )
-            turned = tuple(t[here, :] for t in tables)
-            grad_k = turned_grad(grad_fk, k, kt[here, :], basis, turned, head, width)
-            grads.append(beside(grad_k, grad_v.astype(bf16)))
+            tails.append(jnp.where(begin + iota((CHUNK, 1), 0) >= last, 1.0, 0.0))
+            states.append(two(unfold_state(state_s[step * per_step + sub], head)))
+        grad_fks, grad_vs = [], []
+        for here, tail, state in zip(heres, tails, states):
+            to_k, to_v = [], []
+            for pair in pairs_of(width):
+                high, low_ = state[0][pair, :], state[1][pair, :]
+                left = beside(v[here, pair], share)
+                to_k.append(nt(beside(left, left), beside(high, low_)))
+                to_v.append(
+                    nn(beside(kf[here, pair], kf[here, pair]), below(high[:, :LANE], low_[:, :LANE]))
+                )
+            grad_fks.append(gk[here, :] + tail * beside(*to_k))
+            grad_vs.append((gv[here, :] + tail * beside(*to_v)).astype(bf16))
+        grad_k = turned_grad(below(*grad_fks), kf[...], kt[...], basis, tables, head, width)
+        grads = [beside(grad_k, below(*grad_vs))]
         both = below(*grads)
+        gkv_o[...] = both
         kvb_o[...] += jnp.sum(both.astype(f32).reshape(ROWS // 8, 8, 2 * width), axis=0)
-        grad = grad + nt(beside(gq[...], both), beside(q_w[...], kv_w[...]))
         acc[...] += tn(normed[...], both)
+
+        @pl.when(step == pl.num_programs(0) - 1)
+        def _():
+            deal(pieces, order, low, lambda *spot: write_up(*spot, acc))
+
+    pieces = [firsts, piece, piece]
+    return call(
+        body,
+        (lengths, kf, v, kt, gk, gv, back, cs, expand, basis, normed, entered, own, came),
+        [SMEM, *[row(width)] * 5]
+        + [whole(*back.shape)]
+        + [pl.BlockSpec((1,) + cs.shape[1:], lambda i: (i, 0, 0)), whole(*expand.shape)]
+        + [whole(width, width), row(model), *[packed] * 3],
+        [row(2 * width), whole(8, 2 * width), *[whole(*a.shape) for a in pieces]],
+        [shaped((tokens, 2 * width), bf16), shaped((8, 2 * width)), *pieces],
+        **rest,
+        grid=(tokens // ROWS,),
+        scratch_shapes=[pltpu.VMEM(acc_shape, f32), pltpu.VMEM((chunks, width, LANE), f32)],
+        name="keys",
+    )
+
+
+def inward(call, far, x, gpre0, gpre1, gq, gkv, up_w, qkv_w, **rest):
+    tokens, model = x.shape
+    part = gpre0.shape[1]
+
+    def at(i):
+        core, chip = branch_place()
+        return 2 * (1 - chip) + i if far else 2 * chip + (i ^ (1 - core))
+
+    row = lambda a: pl.BlockSpec((ROWS, a.shape[1]), lambda i: (at(i), 0))
+
+    def body(x, gpre0, gpre1, gq, gkv, up_w, qkv_w, *refs):
+        *outs, gain_o, shift_o = refs
+        step = pl.program_id(0)
 
         @pl.when(step == 0)
         def _():
-            far0_o[...] = grad[: ROWS // 2]
-            far1_o[...] = grad[ROWS // 2 :]
-
-        @pl.when(step == 2)
-        def _():
-            near_o[...] = grad
-
-        @pl.when(step & 1 == 1)
-        def _():
-            keep_o[0] = grad
+            clear(gain_o, shift_o)
+
+        grad = nt(gpre1[...], up_w[:, :-part]) + nt(gpre0[...], up_w[:, -part:])
+        grad = grad + nt(beside(gq[...], gkv[...]), qkv_w[...])
+        if far:
+            outs[0][0] = grad
+        else:
+
+            @pl.when(step == 0)
+            def _():
+                outs[0][...] = grad[: ROWS // 2]
+                outs[1][...] = grad[ROWS // 2 :]
+
+            @pl.when(step == 1)
+            def _():
+                outs[2][...] = grad
 
         xf = x[...].astype(f32)
         centered = xf - jnp.mean(xf, axis=1, keepdims=True)
@@ -785,29 +847,21 @@
         gain_o[...] += jnp.sum((grad * unit).reshape(ROWS // 8, 8, model), axis=0)
         shift_o[...] += jnp.sum(grad.reshape(ROWS // 8, 8, model), axis=0)
 
-        @pl.when(step == pl.num_programs(0) - 1)
-        def _():
-            deal(pieces, order, low, lambda *spot: write_up(*spot, acc))
-
-    chip = pl.BlockSpec((1, ROWS, model), lambda i: (i >> 1, 0, 0))
-    sums = [shaped((8, 2 * width)), shaped((8, model)), shaped((8, model))]
-    pieces = [firsts, piece, piece]
-    sent = [shaped((ROWS // 2, model)), shaped((ROWS // 2, model)), shaped((ROWS, model))]
+    if far:
+        specs = [pl.BlockSpec((1, ROWS, model), lambda i: (i, 0, 0))]
+        shapes = [shaped((2, ROWS, model))]
+    else:
+        shapes = [shaped((rows, model)) for rows in (ROWS // 2, ROWS // 2, ROWS)]
+        specs = [whole(*a.shape) for a in shapes]
     return call(
         body,
-        (lengths, kf, v, kt, gk, gv, back, cs, expand, basis, normed, x, gpre0, gpre1, gq, up_w)
-        + (q_w, kv_w, entered, own, came),
-        [SMEM, *[row(width)] * 5, whole(*back.shape)]
-        + [pl.BlockSpec((1,) + cs.shape[1:], lambda i: (share_at(i), 0, 0)), whole(*expand.shape)]
-        + [whole(width, width), row(model), row(model), row(part), row(gpre1.shape[1]), row(width)]
-        + [whole(*up_w.shape), whole(*q_w.shape), whole(*kv_w.shape), *[packed] * 3],
-        [chip] + [whole(*a.shape) for a in (*sent, *sums, *pieces)],
-        [shaped((tokens // ROWS // 2, ROWS, model)), *sent, *sums, *pieces],
+        (x, gpre0, gpre1, gq, gkv, up_w, qkv_w),
+        [row(a) for a in (x, gpre0, gpre1, gq, gkv)] + [whole(*up_w.shape), whole(*qkv_w.shape)],
+        specs + [whole(8, model)] * 2,
+        shapes + [shaped((8, model))] * 2,
         **rest,
-        grid=(tokens // ROWS,),
-        scratch_shapes=[pltpu.VMEM(acc_shape, f32), pltpu.VMEM((chunks, width, LANE), f32)],
-        flops=LONG,
-        name="backward",
+        grid=(2,),
+        name="inward",
     )
 
 
@@ -837,20 +891,29 @@
     return pl.BlockSpec(shape, lambda i: (at() if callable(at) else at,) + (0,) * (len(shape) - 1))
 
 
-def sums_of(call, *jobs, **rest):
-    arrays, specs, outs, shapes = [], [], [], []
+def sums_of(call, *jobs, stack=False, **rest):
+    arrays, specs, shapes = [], [], []
     for job in jobs:
         for array, count, at in job:
             arrays.append(array)
             specs.append(block_of(array, count, at))
         shapes.append(shaped((count,) + array.shape[1:]))
-        outs.append(whole(*shapes[-1].shape))
+    counts = [a.shape[0] for a in shapes]
+    if stack:
+        shapes = [shaped((sum(counts),) + shapes[0].shape[1:])]
+    outs = [whole(*a.shape) for a in shapes]
 
     def body(*refs):
         ins, results = refs[: len(arrays)], refs[len(arrays) :]
-        for job, out in zip(jobs, results):
+        start = 0
+        for i, job in enumerate(jobs):
             mine, ins = ins[: len(job)], ins[len(job) :]
-            out[...] = sum(r[...] for r in mine[1:]) + mine[0][...]
+            value = sum(r[...] for r in mine[1:]) + mine[0][...]
+            if stack:
+                results[0][start : start + counts[i]] = value
+                start += counts[i]
+            else:
+                results[i][...] = value
 
     return call(body, arrays, specs, outs, shapes, grid=(1,), name="sums", **rest)
 
@@ -861,9 +924,9 @@
 
 def finish_feed(call, one, down, up, **rest):
     args, specs = [one], [block_of(one, 1, 0)]
-    for piece, first, two_came, three_came in (down, up):
+    for piece, first, two_came, (three_came, which) in (down, up):
         args += [piece[2], first, two_came, three_came]
-        specs += [block_of(a, 1, at) for a, at in zip(args[-4:], (0, 2, 0, 0))]
+        specs += [block_of(a, 1, at) for a, at in zip(args[-4:], (0, 2, 0, which))]
     widths = [down[0][2].shape[1], one.shape[1] // 2]
 
     def body(one, *refs):
@@ -884,23 +947,18 @@
     )
 
 
-def finish_heads(call, head, out_q, key_val, **rest):
-    args, specs = [], []
-    for piece, first, two_came, three_came in (out_q, key_val):
-        args += [piece[2], first, two_came, three_came]
-        specs += [block_of(a, 1, at) for a, at in zip(args[-4:], (0, 2, 0, 0))]
-    width = key_val[0][2].shape[1] // 2
+def finish_heads(call, head, one, key_val, **rest):
+    piece, first, two_came, three_came = key_val
+    args = [one, piece[2], first, two_came, three_came]
+    specs = [block_of(a, 1, at) for a, at in zip(args, (0, 0, 2, 0, 0))]
+    width = one.shape[1] // 2
     heads = width // head
 
-    def body(*refs):
-        out_o, qkv_o = refs[-2:]
-        values = []
-        for n in range(2):
-            a, b, c, d = refs[4 * n : 4 * n + 4]
-            values.append((a[0] + b[0]) + (c[0] + d[0]))
-        out_o[...] = values[0][:width]
+    def body(one, a, b, c, d, out_o, qkv_o):
+        value = (a[0] + b[0]) + (c[0] + d[0])
+        out_o[...] = one[0, :width]
         columns = []
-        for rows in (values[0][width:], values[1][:width], values[1][width:]):
+        for rows in (one[0, width:], value[:width], value[width:]):
             columns.append(beside(*[rows[j * LANE : (j + 1) * LANE] for j in range(width // LANE)]))
         qkv_o[...] = beside(*[p[:, h * head : (h + 1) * head] for h in range(heads) for p in columns])
 
@@ -910,42 +968,35 @@
     )
 
 
-def far_sums(call, keep, came, far, **rest):
-    rows, model = CHUNK, keep.shape[2]
-    steps = keep.shape[1] // rows
-    spec = pl.BlockSpec((1, rows, model), lambda i: (far(), i, 0))
-    parts = isinstance(came, tuple)
-
-    def body(keep, *refs):
-        *came, out = refs
-        if parts:
-            step = pl.program_id(0)
-            out[...] = keep[0] + jnp.where(step == 0, came[0][...], came[1][...])
-        else:
-            out[...] = keep[0] + came[0][0]
+def far_sums(call, one, other, far=(lambda: 0, lambda: 0), **rest):
+    rows, model = CHUNK, one.shape[2]
+    specs = [pl.BlockSpec((1, rows, model), lambda i, at=at: (at(), i, 0)) for at in far]
+
+    def body(one, other, out):
+        out[...] = one[0] + other[0]
 
     return call(
         body,
-        (keep, *came) if parts else (keep, came),
-        [spec, *([whole(rows, model)] * 2 if parts else [spec])],
+        (one, other),
+        specs,
         [rows_at(rows, model)],
-        [shaped(keep.shape[1:])],
-        grid=(steps,),
+        [shaped(one.shape[1:])],
+        grid=(one.shape[1] // rows,),
         name="far_sums",
         **rest,
     )
 
 
-def finish_specs(keep, near):
-    share, model = keep.shape[1:]
+def finish_specs(share, model):
     steps = share // CHUNK
     own = pl.BlockSpec((CHUNK, model), lambda i: (lax.axis_index("branch") * steps + i, 0))
-    return own, pl.BlockSpec((1, CHUNK, model), lambda i: (near(), i, 0)), rows_at(CHUNK, model), steps
+    return own, rows_at(CHUNK, model), steps
 
 
 def finish_output(call, x, keep, came_core, came_chip, bias, near):
     share, model = came_chip.shape
-    own, part, row, steps = finish_specs(keep, near)
+    own, row, steps = finish_specs(share, model)
+    part = pl.BlockSpec((1, CHUNK, model), lambda i: (near(), i, 0))
 
     def body(x, keep, core, chip, bias, out):
         total = (keep[0] + core[0]) + chip[...]
@@ -962,32 +1013,34 @@
     )[0]
 
 
-def finish_input(call, x, cot, gain, keep, came_core, came_chip, near):
+def finish_input(call, x, cot, gain, keep, came_core, came_chip, **rest):
     share, model = came_chip.shape
-    own, part, row, steps = finish_specs(keep, near)
-
-
-    def body(x, cot, gain, keep, core, chip, out):
+    own, row, steps = finish_specs(share, model)
+
+
+    def body(x, cot, gain, keep, core0, core1, chip, out):
+        core = jnp.where(pl.program_id(0) == 0, core0[...], core1[...])
         xf = x[...].astype(f32)
         centered = xf - jnp.mean(xf, axis=1, keepdims=True)
         inv = lax.rsqrt(jnp.mean(centered * centered, axis=1, keepdims=True) + epsilon)
         unit = centered * inv
-        g = ((keep[0] + core[...]) + chip[...]) * gain[...]
+        g = ((keep[...] + core) + chip[...]) * gain[...]
         inner = g - jnp.mean(g, axis=1, keepdims=True) - unit * jnp.mean(g * unit, axis=1, keepdims=True)
         out[...] = inv * inner + cot[...].astype(f32)
 
     return call(
         body,
-        (x, cot, gain, keep, came_core, came_chip),
-        [own, own, whole(1, model), part, row, row],
+        (x, cot, gain, keep, *came_core, came_chip),
+        [own, own, whole(1, model), row, *[whole(CHUNK, model)] * 2, row],
         [row],
         [shaped((share, model))],
+        **rest,
         grid=(steps,),
         name="finish_input",
     )[0]
 
 
-def pack_small(call, head, branch, gain, shift, cot, qb, kvb, ubs, **rest):
+def pack_small(call, head, branch, gains, shifts, cot, qb, kvb, ubs, **rest):
     model = cot.shape[1]
     width = qb.shape[1]
     heads = width // head
@@ -997,7 +1050,7 @@
     starts.append(starts[3] + qkv_rows * branch)
     total = starts[4] + up_rows * branch
 
-    def body(gain, shift, cot, qb, kvb, ub0, ub1, out):
+    def body(gain0, gain1, shift0, shift1, cot, qb, kvb, ub0, ub1, out):
         out[...] = jnp.zeros_like(out)
         here = lax.axis_index("branch")
 
@@ -1008,8 +1061,8 @@
             for j in range(value.shape[1] // LANE):
                 out[pl.ds(row + j, 1), :] = value[:, j * LANE : (j + 1) * LANE]
 
-        place(starts[0], summed(gain[...]))
-        place(starts[1], summed(shift[...]))
+        place(starts[0], summed(gain0[...] + gain1[...]))
+        place(starts[1], summed(shift0[...] + shift1[...]))
         place(starts[2], summed(cot[...]) * jnp.where(here == 0, 1.0, 0.0))
         q, kv = summed(qb[...]), summed(kvb[...])
         parts = (q, kv[:, :width], kv[:, width:])
@@ -1019,7 +1072,7 @@
         )
         place(starts[4] + here * up_rows, beside(summed(ub1[...]), summed(ub0[...])))
 
-    args = (gain, shift, cot, qb, kvb, *ubs)
+    args = (*gains, *shifts, cot, qb, kvb, *ubs)
     return call(
         body,
         args,
@@ -1052,7 +1105,7 @@
     batch = lax.axis_size("batch")
     branch = lax.axis_size("branch")
     low = batch // (model // LANE)
-    y_first, z_first = (0, 1, 2), (1, 0, 2)
+    y_first, z_first = (0, 1, 2), (1, 2, 0)
     bits = [1 << b for b in range(batch.bit_length() - 1)]
     expand = jnp.asarray(expand_table(head), bf16)
     dct_t = jnp.asarray(dct_table(head).T)
@@ -1072,17 +1125,21 @@
             came = swapped(own, "batch", bit)
         return entered, own, came
 
-    normed, cb, kf, value, kt, kv_w, basis, cs, state, hidden0, gpre0, ub0, piece0 = front(
+    normed, cb, kf, value, kt, w_perm, b_perm, basis, cs, state, hidden0, gpre0, ub0, piece0 = front(
         call, head, lengths, inputs, gain, shift, up_weight, up_b, down_weight, cotangent, qkv_weight,
         qkv_b, expand, feature_samples, dct_t,
     )
     groups = [[j * low + i for j in range(batch // low)] for i in range(low)] if low > 1 else None
-    sum0 = lax.psum_scatter(
-        piece0, "batch", scatter_dimension=0, axis_index_groups=groups, tiled=True
-    )
+
+    def scattered(piece):
+        return lax.psum_scatter(
+            piece, "batch", scatter_dimension=0, axis_index_groups=groups, tiled=True
+        )
+
+    sum0 = scattered(piece0)
     came = swapped(state, "batch", 1)
-    qf, qt, ga, q_w = project_queries(
-        call, head, feats, normed, qkv_weight, qkv_b, expand, basis, cs, cotangent, out_weight
+    qf, qt, ga = project_queries(
+        call, head, feats, normed, w_perm, b_perm, expand, basis, cs, cotangent, out_weight
     )
     states = enter(True, state, came)
     hidden1, gpre1, ub1, *pieces = feed(
@@ -1090,8 +1147,8 @@
     )
     down, up = pieces[:3], pieces[3:]
     down_first, up_first = send(down[0], y_first, 0), send(up[0], z_first, 0)
-    gq, gk, gv, back, state, qb, out_send, out_keep, *oq = attend(
-        call, head, y_first, low, len(bits) - 1, lengths, qf, kf, value, qt, ga, cs, expand, basis,
+    gq, gk, gv, back, state, qb, out_send, out_keep, oq = attend(
+        call, head, len(bits) - 1, lengths, qf, kf, value, qt, ga, cs, expand, basis,
         normed, cotangent, hidden0, hidden1, down_weight, out_weight, *states,
     )
     came = swapped(state, "batch", 1)
@@ -1099,68 +1156,67 @@
     far_chip = lambda: 1 - branch_place()[1]
     near_chip = lambda: branch_place()[1]
     down_2, up_2 = sums_of(
-        call, [whole_of(down[1]), (down_first, 2, 0)], [whole_of(up[1]), (up_first, 2, 0)]
-    )
-    entered, state, oq_first = join_states(
-        call, False, tokens, 0, lengths, None, state, came, through=(oq[0],), flops=LONG
+        call, [whole_of(down[1]), (down_first, 2, 0)], [whole_of(up[1]), (up_first, 2, 0)],
+        after=(sum0,),
+    )
+    entered, state = join_states(
+        call, False, tokens, 0, lengths, None, state, came, flops=50 * STEP
     )
     came = swapped(state, "batch", bits[1])
-    oq_first = send(oq_first, y_first, 0)
-    (out_far,) = far_sums(call, out_keep, out_core, far_chip)
+    (out_far,) = far_sums(call, out_keep, out_core, (far_chip, far_chip))
     out_chip = swapped(out_far, "branch", 2)
     for i in range(1, len(bits) - 1):
         entered, state = join_states(call, False, tokens, i, lengths, entered, state, came)
         came = swapped(state, "batch", bits[i + 1])
-    down_2, up_2 = hold(call, (down_2, up_2))
+    down_2, up_2, oq = hold(call, (down_2, up_2, oq))
+    sum_oq = scattered(oq)
     down_2, up_2 = send(down_2, y_first, 1), send(up_2, z_first, 1)
-    grad_keep, far0, far1, near, kvb, gain_part, shift_part, *kv = backward(
-        call, head, y_first, low, len(bits) - 1, lengths, kf, value, kt, gk, gv, back, cs,
-        expand, basis, normed, inputs, gpre0, gpre1, gq, up_weight, q_w, kv_w, entered, state, came,
-    )
-    far_core = (swapped(far0, "branch", 1), swapped(far1, "branch", 1))
-    down_3, up_3, oq_2, near, kv_first = sums_of(
-        call, [(down[2], 1, 1), (down_first, 1, 3), (down_2, 1, 1)],
-        [(up[2], 1, 1), (up_first, 1, 3), (up_2, 1, 1)], [whole_of(oq[1]), (oq_first, 2, 0)],
-        through=(near, kv[0]),
-    )
-    grad_core = swapped(near, "branch", 1)
-    kv_first = send(kv_first, y_first, 0)
-    down_3, up_3 = send(down_3, y_first, 2), send(up_3, z_first, 2)
-    oq_2 = send(oq_2, y_first, 1)
+    gkv, kvb, *kv = keys(
+        call, head, y_first, low, len(bits) - 1, lengths, kf, value, kt, gk, gv, back, cs, expand,
+        basis, normed, entered, state, came, flops=COST_KEYS,
+    )
+    kv_first = send(kv[0], y_first, 0)
+    in_args = (inputs, gpre0, gpre1, gq, gkv, up_weight, w_perm)
+    far, gain0, shift0 = inward(call, True, *in_args, flops=COST_FAR)
+    cores = [[i, i + 1] for i in range(0, branch, 2)]
+    far = lax.all_to_all(far, "branch", 0, 0, axis_index_groups=cores, tiled=True)
+    (grad_far,) = far_sums(call, far, far, (lambda: 0, lambda: 1))
+    grad_chip = swapped(grad_far, "branch", 2)
+    kv_2, down_3, up_3 = sums_of(
+        call, [whole_of(kv[1]), (kv_first, 2, 0)],
+        [(down[2], 1, 1), (down_first, 1, 3), (down_2, 1, 1)],
+        [(up[2], 1, 1), (up_first, 1, 3), (up_2, 1, 1)],
+    )
+    kv_2, down_3, up_3 = send(kv_2, y_first, 1), send(down_3, y_first, 2), send(up_3, z_first, 2)
+    near0, near1, grad_keep, gain1, shift1 = inward(call, False, *in_args, flops=COST_NEAR)
     (small,) = pack_small(
-        call, head, branch, gain_part, shift_part, cb, qb, kvb, (ub0, ub1), flops=SHORT
-    )
-    came = swapped(small, "branch", 1)
-    (grad_far,) = far_sums(call, grad_keep, far_core, lambda: 0)
-    grad_chip = swapped(grad_far, "branch", 2)
+        call, head, branch, (gain0, gain1), (shift0, shift1), cb, qb, kvb, (ub0, ub1),
+        after=(out_chip,),
+    )
+    came = swapped(small, "batch", 1)
+    grad_core = swapped(near0, "branch", 1), swapped(near1, "branch", 1)
     output = finish_output(
         call, inputs, out_keep, out_core, out_chip, out_bias.reshape(1, model), near_chip
     )
-    (small,) = sums_of(call, [whole_of(small), whole_of(came)], after=(grad_core,))
-    came = swapped(small, "batch", 1)
-    (kv_2,) = sums_of(call, [whole_of(kv[1]), (kv_first, 2, 0)])
-    kv_2 = send(kv_2, y_first, 1)
     (small,) = sums_of(call, [whole_of(small), whole_of(came)])
     came = swapped(small, "batch", bits[1])
-    (oq_3,) = sums_of(call, [(oq[2], 1, 1), (oq_first, 1, 3), (oq_2, 1, 1)])
-    oq_3 = send(oq_3, y_first, 2)
+    down_sum, up_sum = finish_feed(
+        call, sum0, (down, down_first, down_2, (down_3, 0)), (up, up_first, up_2, (up_3, 0))
+    )
     for bit in bits[2:]:
         (small,) = sums_of(call, [whole_of(small), whole_of(came)])
         came = swapped(small, "batch", bit)
+    (small,) = sums_of(call, [whole_of(small), whole_of(came)])
+    came = swapped(small, "branch", 1)
     (kv_3,) = sums_of(call, [(kv[2], 1, 1), (kv_first, 1, 3), (kv_2, 1, 1)])
     kv_3 = send(kv_3, y_first, 2)
-    (small,) = sums_of(call, [whole_of(small), whole_of(came)])
+    (small,) = sums_of(call, [whole_of(small), whole_of(came)], flops=COST_END)
     came = swapped(small, "branch", 2)
-    down_sum, up_sum = finish_feed(
-        call, sum0, (down, down_first, down_2, down_3), (up, up_first, up_2, up_3)
-    )
-    out_sum, qkv_sum = finish_heads(
-        call, head, (oq, oq_first, oq_2, oq_3), (kv, kv_first, kv_2, kv_3)
-    )
     small = finish_small(call, small, came, [model, model, model, 3 * width * branch, up_bias.size * branch])
     input_grad = finish_input(
-        call, inputs, cotangent, gain, grad_keep, grad_core, grad_chip, lambda: 1
-    )
+        call, inputs, cotangent, gain, grad_keep, grad_core, grad_chip, after=(sum_oq,)
+    )
+    out_sum, qkv_sum = finish_heads(call, head, sum_oq, (kv, kv_first, kv_2, kv_3))
     down_sum, out_sum = finish(down_sum, 1, low), finish(out_sum, 1, low)
     up_sum, qkv_sum = finish(up_sum, 0, low), finish(qkv_sum, 0, low)
 

time: 298 us -> 259 us (0.87)
  waiting for transfers between devices: 85.3 us -> 45.4 us
  blocking collectives: 0 us -> 11.9 us
  Pallas kernels: 164 us -> 157 us
  starting transfers between devices: 32 us -> 28.7 us
    ppermute x29 -> x25, waiting for transfers between devices: 85.3 us -> 45.3 us  [swapped(): return lax.ppermute(value, axis, [(i, i ^ distance) for i in range(size)])]
    all_to_all x0 -> x1, blocking collectives: none -> 11.9 us  [per_device(): lax.all_to_all(far, 'branch', 0, 0, axis_index_groups=cores, tiled=True)]
    pallas_call x27, Pallas kernels: 164 us -> 157 us  [__call__(): pl.pallas_call(without, in_specs=[*in_specs, *[place] * len(skipped)], ou...]
    ppermute x29 -> x25, starting transfers between devices: 32 us -> 28.4 us  [swapped(): return lax.ppermute(value, axis, [(i, i ^ distance) for i in range(size)])]
  transfers between devices with their start and end apart: 30 -> 27, of which waited for: 13 -> 11; matrix products, arithmetic and copies ran while one was open for 0% -> 0% of each run, Pallas kernels for 45% -> 51%
where the time goes in v3:
time: 259 us; the launch traced here: 258 us
  Pallas kernels  157 us (61%)
  waiting for transfers between devices  45.4 us (18%)
  starting transfers between devices  28.7 us (11%)
  between operations  14.1 us (5%)
  blocking collectives  11.9 us (5%)
    pallas_call x27, Pallas kernels, __call__(): pl.pallas_call(without, in_specs=[*in_specs, *[place] * len(skipped)], ou...  157 us
    ppermute x25, waiting for transfers between devices, swapped(): return lax.ppermute(value, axis, [(i, i ^ distance) for i in range(size)])  45.3 us
    ppermute x25, starting transfers between devices, swapped(): return lax.ppermute(value, axis, [(i, i ^ distance) for i in range(size)])  28.4 us
    all_to_all x1, blocking collectives, per_device(): lax.all_to_all(far, 'branch', 0, 0, axis_index_groups=cores, tiled=True)  11.9 us
  transfers between devices with their start and end apart: 27, of which 11 were waited for; matrix products, arithmetic and copies ran while one was open for 0% of the time, Pallas kernels for 51%

profile of v3, /device:TPU:0, one launch (start us, length us, event | category | flops | bytes accessed | tf_op | source)
XLA Modules:
  0.0 258.0 jit_solution(1889177884402827233)
XLA Ops:
  8.5 20.4 %front.1 = (bf16[2048,1024]{1,0:T(8,128)(2,1)}, f32[8,1024]{1,0:T(8,128)}, bf16[2048,256]{1,0:T(8,128)(2,1)}, bf16[2048,256]{1,0:T(8,128)(2,1)}, bf16[2048,256]{...) custom-call(s32[8]{0:T(128)} %refs_0_.17, ...), custom_call_target="tpu_custom_call" | custom-call | tf_op jit(solution)/shard_map/front/pallas_call | solution.py:76
  29.1 3.0 %collective-permute-start = (f32[256,128]{1,0:T(8,128)}, f32[256,128]{1,0:T(8,128)}, u32[]{:S(2)}, u32[]{:S(2)}) collective-permute-start(f32[256,128]{1,0:T(8,128)} %get-tuple-element.96.refs_1_), channel_id=1, source_target_pairs={{0,4},{4,0},{8,12},{12,8},{16,20},{20,16},{24,28},{28,24},{1,5},{5... | collective-permute-start | bytes 393224 | tf_op jit(solution)/shard_map/ppermute | solution.py:451
  32.2 8.8 %project_queries.1 = (bf16[2048,256]{1,0:T(8,128)(2,1)}, bf16[2048,256]{1,0:T(8,128)(2,1)}, f32[2048,256]{1,0:T(8,128)}) custom-call(bf16[2048,1024]{1,0:T(8,128)(2,1)} %get-tuple-element.85.refs_0_.refs_8_.refs_9_.refs_10_, bf16[1024,768]{1,0:T(8,128)(2,1)} %get-tuple-element.86.refs_1_.refs_6_, f32[1,768]{1,0:T(1,128)} %get-tuple-element.87.refs_2_, ...), custom_call_target="tpu_custom_call" | custom-call | tf_op jit(solution)/shard_map/project_queries/pallas_call | solution.py:76
  44.2 8.8 %collective-permute-done.1.refs_3_ = f32[256,128]{1,0:T(8,128)} collective-permute-done((f32[256,128]{1,0:T(8,128)}, f32[256,128]{1,0:T(8,128)}, u32[]{:S(2)}, u32[]{:S(2)}) %collective-permute-start.1) | collective-permute-done | bytes 131104 | tf_op jit(solution)/shard_map/ppermute | solution.py:451
  56.0 21.2 %feed_forward.1 = (bf16[2048,768]{1,0:T(8,128)(2,1)}, bf16[2048,768]{1,0:T(8,128)(2,1)}, f32[8,768]{1,0:T(8,128)}, f32[4,768,128]{2,1,0:T(8,128)}, f32[2,768,128...) custom-call(bf16[2048,1024]{1,0:T(8,128)(2,1)} %get-tuple-element.85, ...), custom_call_target="tpu_custom_call" | custom-call | tf_op jit(solution)/shard_map/feed_forward/pallas_call | solution.py:76
  78.2 2.7 %collective-permute-start.6 = (f32[4,768,128]{2,1,0:T(8,128)}, f32[4,768,128]{2,1,0:T(8,128)}, u32[]{:S(2)}, u32[]{:S(2)}) collective-permute-start(f32[4,768,128]{2,1,0:T(8,128)} %get-tuple-element.108), channel_id=1, source_target_pairs={{0,8},{4,12},{8,0},{12,4},{16,24},{20,28},{24,16},{28,20},{1,9},{5... | collective-permute-start | bytes 4718600 | tf_op jit(solution)/shard_map/ppermute | solution.py:451
  80.9 29.5 %attend.1 = (bf16[2048,256]{1,0:T(8,128)(2,1)}, f32[2048,256]{1,0:T(8,128)}, f32[2048,256]{1,0:T(8,128)}, f32[8,256,128]{2,1,0:T(8,128)}, f32[256,128]{1,0:T(8,1...) custom-call(s32[8]{0:T(128)} %refs_0_.17, ...), custom_call_target="tpu_custom_call" | custom-call | flops 17179869184 | tf_op jit(solution)/shard_map/attend/pallas_call | solution.py:76
  111.0 6.7 %collective-permute-done.5.refs_1_.refs_3_.refs_2_ = f32[4,768,128]{2,1,0:T(8,128)} collective-permute-done((f32[4,768,128]{2,1,0:T(8,128)}, f32[4,768,128]{2,1,0:T(8,128)}, u32[]{:S(2)}, u32[]{:S(2)}) %collective-permute-start.5) | collective-permute-done | bytes 1572896 | tf_op jit(solution)/shard_map/ppermute | solution.py:451
  117.7 5.3 %collective-permute-done.6.refs_3_.refs_6_ = f32[4,768,128]{2,1,0:T(8,128)} collective-permute-done((f32[4,768,128]{2,1,0:T(8,128)}, f32[4,768,128]{2,1,0:T(8,128)}, u32[]{:S(2)}, u32[]{:S(2)}) %collective-permute-start.6) | collective-permute-done | bytes 1572896 | tf_op jit(solution)/shard_map/ppermute | solution.py:451
  123.0 3.1 %sums.7 = (f32[2,768,128]{2,1,0:T(8,128)}, f32[2,768,128]{2,1,0:T(8,128)}) custom-call(f32[2,768,128]{2,1,0:T(8,128)} %get-tuple-element.105.refs_0_, f32[4,768,128]{2,1,0:T(8,128)} %collective-permute-done.5.refs_1_.refs_3_.refs_2_, f32[2,768,128]{2,1,0:T(8,128)} %get-tuple-element.107.refs_2_, f32[4,768,128]{2,1,0:T(8,128)} %collective-permute-done.6.refs_3_.refs_6_, ...), custom_call_target="tpu_custom_call" | custom-call | tf_op jit(solution)/shard_map/sums/pallas_call | solution.py:76
  129.5 3.3 %far_sums.2.refs_4_ = f32[512,1024]{1,0:T(8,128)} custom-call(f32[2,512,1024]{2,1,0:T(8,128)} %get-tuple-element.102.refs_0_.refs_1_, f32[2,512,1024]{2,1,0:T(8,128)} %collective-permute-done.3.refs_1_.refs_2_, f32[256,128]{1,0:T(8,128)} %get-tuple-element.112.refs_2_.refs_1_), custom_call_target="tpu_custom_call" | custom-call | tf_op jit(solution)/shard_map/far_sums/pallas_call | solution.py:76
  139.1 2.6 %collective-permute-start.12 = (f32[2,768,128]{2,1,0:T(8,128)}, f32[2,768,128]{2,1,0:T(8,128)}, u32[]{:S(2)}, u32[]{:S(2)}) collective-permute-start(f32[2,768,128]{2,1,0:T(8,128)} %get-tuple-element.132), channel_id=1, source_target_pairs={{0,16},{4,20},{8,24},{12,28},{16,0},{20,4},{24,8},{28,12},{1,17},{... | collective-permute-start | bytes 2359304 | tf_op jit(solution)/shard_map/ppermute | solution.py:451
  141.7 2.1 collective-permute-done.9.refs_13_
  143.9 12.0 %keys.1 = (bf16[2048,512]{1,0:T(8,128)(2,1)}, f32[8,512]{1,0:T(8,128)}, f32[4,512,128]{2,1,0:T(8,128)}, f32[2,512,128]{2,1,0:T(8,128)}, f32[2,512,128]{2,1,0:T(8,128)}) custom-call(s32[8]{0:T(128)} %refs_0_.17, bf16[2048,256]{1,0:T(8,128)(2,1)} %get-tuple-element.91.refs_2_.refs_1_, bf16[2048,256]{1,0:T(8,128)(2,1)} %get-tuple-element.92.refs_3_.refs_2_, ...), custom_call_target="tpu_custom_call" | custom-call | flops 53687091200 | tf_op jit(solution)/shard_map/keys/pallas_call | solution.py:76
  156.9 9.0 %inward.2 = (f32[2,512,1024]{2,1,0:T(8,128)}, f32[8,1024]{1,0:T(8,128)}, f32[8,1024]{1,0:T(8,128)}) custom-call(bf16[2048,1024]{1,0:T(8,128)(2,1)} %refs_0_.21, bf16[2048,256]{1,0:T(8,128)(2,1)} %get-tuple-element.113.refs_1_, bf16[2048,768]{1,0:T(8,128)(2,1)} %get-tuple-element.114.refs_2_, bf16[2048,256]{1,0:T(8,128)(2,1)} %get-tuple-element.109.refs_4_.refs_3_, ...), custom_call_target="tpu_custom_call" | custom-call | flops 13958643712 | tf_op jit(solution)/shard_map/inward/pallas_call | solution.py:76
  166.0 11.9 %all_to_all.5.refs_0_.refs_1_ = f32[2,512,1024]{2,1,0:T(8,128)} all-to-all(f32[2,512,1024]{2,1,0:T(8,128)} %get-tuple-element.133.refs_2_), channel_id=1, replica_groups={{0,1},{2,3},{4,5},{6,7},{8,9},{10,11},{12,13},{14,15},{16,17},{18,19},{..., dimensions={0} | all-to-all | bytes 8388608 | tf_op jit(solution)/shard_map/all_to_all | solution.py:1182
  177.8 3.3 %far_sums.3.refs_8_ = f32[512,1024]{1,0:T(8,128)} custom-call(f32[2,512,1024]{2,1,0:T(8,128)} %all_to_all.5.refs_0_.refs_1_, f32[2,512,1024]{2,1,0:T(8,128)} %all_to_all.5.refs_0_.refs_1_, f32[2,512,1024]{2,1,0:T(8,128)} %get-tuple-element.133.refs_2_), custom_call_target="tpu_custom_call" | custom-call | tf_op jit(solution)/shard_map/far_sums/pallas_call | solution.py:76
  182.7 4.2 %collective-permute-done.11.refs_4_.refs_3_ = f32[2,768,128]{2,1,0:T(8,128)} collective-permute-done((f32[2,768,128]{2,1,0:T(8,128)}, f32[2,768,128]{2,1,0:T(8,128)}, u32[]{:S(2)}, u32[]{:S(2)}) %collective-permute-start.11) | collective-permute-done | bytes 786464 | tf_op jit(solution)/shard_map/ppermute | solution.py:451
  186.9 4.6 %collective-permute-done.12.refs_7_ = f32[2,768,128]{2,1,0:T(8,128)} collective-permute-done((f32[2,768,128]{2,1,0:T(8,128)}, f32[2,768,128]{2,1,0:T(8,128)}, u32[]{:S(2)}, u32[]{:S(2)}) %collective-permute-start.12) | collective-permute-done | bytes 786464 | tf_op jit(solution)/shard_map/ppermute | solution.py:451
  191.5 3.1 %sums.8 = (f32[2,512,128]{2,1,0:T(8,128)}, f32[1,768,128]{2,1,0:T(8,128)}, f32[1,768,128]{2,1,0:T(8,128)}) custom-call(f32[2,512,128]{2,1,0:T(8,128)} %get-tuple-element.127.refs_0_, f32[4,512,128]{2,1,0:T(8,128)} %collective-permute-done.10.refs_1_.refs_2_, f32[2,768,128]{2,1,0:T(8,128)} %get-tuple-element.129.refs_2_.refs_1_, ...), custom_call_target="tpu_custom_call" | custom-call | tf_op jit(solution)/shard_map/sums/pallas_call | solution.py:76
  194.6 3.2 %collective-permute-start.18 = (f32[1,768,128]{2,1,0:T(8,128)}, f32[1,768,128]{2,1,0:T(8,128)}, u32[]{:S(2)}, u32[]{:S(2)}) collective-permute-start(f32[1,768,128]{2,1,0:T(8,128)} %get-tuple-element.146), channel_id=1, source_target_pairs={{0,16},{4,20},{8,24},{12,28},{16,0},{20,4},{24,8},{28,12},{1,17},{... | collective-permute-start | bytes 1179656 | tf_op jit(solution)/shard_map/ppermute | solution.py:451
  198.0 10.5 %inward.3 = (f32[256,1024]{1,0:T(8,128)}, f32[256,1024]{1,0:T(8,128)}, f32[512,1024]{1,0:T(8,128)}, f32[8,1024]{1,0:T(8,128)}, f32[8,1024]{1,0:T(8,128)}) custom-call(bf16[2048,1024]{1,0:T(8,128)(2,1)} %refs_0_.21, bf16[2048,256]{1,0:T(8,128)(2,1)} %get-tuple-element.113.refs_1_, bf16[2048,768]{1,0:T(8,128)(2,1)} %get-tuple-element.114.refs_2_, ...), custom_call_target="tpu_custom_call" | custom-call | tf_op jit(solution)/shard_map/inward/pallas_call | solution.py:76
  210.1 1.9 collective-permute-start.16
  212.0 4.1 %finish_output.1.refs_2_ = bf16[512,1024]{1,0:T(8,128)(2,1)} custom-call(bf16[2048,1024]{1,0:T(8,128)(2,1)} %refs_0_.21, f32[2,512,1024]{2,1,0:T(8,128)} %get-tuple-element.102.refs_0_.refs_1_, f32[2,512,1024]{2,1,0:T(8,128)} %collective-permute-done.3.refs_1_.refs_2_, f32[512,1024]{1,0:T(8,128)} %collective-permute-done.7.refs_10_.refs_3_, ...), custom_call_target="tpu_custom_call" | custom-call | tf_op jit(solution)/shard_map/finish_output/pallas_call | solution.py:76
  217.5 3.0 %finish_feed.1 = (f32[1024,128]{1,0:T(8,128)}, f32[128,1024]{1,0:T(8,128)}) custom-call(f32[1,512,128]{2,1,0:T(8,128)} %reduce-scatter.3.cloned.1.call-done.refs_5_.refs_0_, f32[2,768,128]{2,1,0:T(8,128)} %get-tuple-element.129.refs_2_.refs_1_, f32[4,768,128]{2,1,0:T(8,128)} %collective-permute-done.5.refs_1_.refs_3_.refs_2_, ...), custom_call_target="tpu_custom_call" | custom-call | tf_op jit(solution)/shard_map/finish_feed/pallas_call | solution.py:76
  220.6 2.0 collective-permute-done.17.refs_1_
  224.2 6.5 %collective-permute-done.20.refs_1_ = f32[80,128]{1,0:T(8,128)} collective-permute-done((f32[80,128]{1,0:T(8,128)}, f32[80,128]{1,0:T(8,128)}, u32[]{:S(2)}, u32[]{:S(2)}) %collective-permute-start.20) | collective-permute-done | bytes 40992 | tf_op jit(solution)/shard_map/ppermute | solution.py:451
  232.6 1.9 sums.12.refs_2_
  237.5 2.7 %collective-permute-done.23.refs_1_ = f32[80,128]{1,0:T(8,128)} collective-permute-done((f32[80,128]{1,0:T(8,128)}, f32[80,128]{1,0:T(8,128)}, u32[]{:S(2)}, u32[]{:S(2)}) %collective-permute-start.23) | collective-permute-done | bytes 40992 | tf_op jit(solution)/shard_map/ppermute | solution.py:451
  241.7 5.2 %finish_input.1.refs_5_ = f32[512,1024]{1,0:T(8,128)} custom-call(bf16[2048,1024]{1,0:T(8,128)(2,1)} %refs_0_.21, bf16[2048,1024]{1,0:T(8,128)(2,1)} %refs_1_.5, f32[1,1024]{1,0:T(1,128)} %bitcast.12, f32[512,1024]{1,0:T(8,128)} %get-tuple-element.144.refs_3_, f32[256,1024]{1,0:T(8,128)} %collective-permute-done.13.refs_4_, ...), custom_call_target="tpu_custom_call" | custom-call | tf_op jit(solution)/shard_map/finish_input/pallas_call | solution.py:76
  246.9 2.2 collective-permute-done.24.refs_4_
  249.1 2.1 finish_heads.1
  (53 shorter events, 33.2 us)
Async XLA Ops:
  7.2 115.8 %reduce-scatter.3.cloned.1.call-start = ((), (), s32[]{:S(2)}) async-start(), calls=%async_computation.3 | async-start | bytes 2359296 | tf_op jit(solution)/shard_map/reduce_scatter | solution.py:1135
  28.9 212.8 %reduce-scatter.5.cloned.1.call-start = ((), (), s32[]{:S(2)}) async-start(), calls=%async_computation.4 | async-start | bytes 2359296 | tf_op jit(solution)/shard_map/reduce_scatter | solution.py:1135
  29.1 11.8 %collective-permute-start = (f32[256,128]{1,0:T(8,128)}, f32[256,128]{1,0:T(8,128)}, u32[]{:S(2)}, u32[]{:S(2)}) collective-permute-start(f32[256,128]{1,0:T(8,128)} %get-tuple-element.96.refs_1_), channel_id=1, source_target_pairs={{0,4},{4,0},{8,12},{12,8},{16,20},{20,16},{24,28},{28,24},{1,5},{5... | collective-permute-start | bytes 393224 | tf_op jit(solution)/shard_map/ppermute | solution.py:451
  42.6 10.4 %collective-permute-start.1 = (f32[256,128]{1,0:T(8,128)}, f32[256,128]{1,0:T(8,128)}, u32[]{:S(2)}, u32[]{:S(2)}) collective-permute-start(f32[256,128]{1,0:T(8,128)} %get-tuple-element.98.refs_2_), channel_id=1, source_target_pairs={{0,8},{4,12},{8,0},{12,4},{16,24},{20,28},{24,16},{28,20},{1,9},{5... | collective-permute-start | bytes 393224 | tf_op jit(solution)/shard_map/ppermute | solution.py:451
  54.8 26.1 %collective-permute-start.2 = (f32[256,128]{1,0:T(8,128)}, f32[256,128]{1,0:T(8,128)}, u32[]{:S(2)}, u32[]{:S(2)}) collective-permute-start(f32[256,128]{1,0:T(8,128)} %get-tuple-element.101.refs_16_), channel_id=1, source_target_pairs={{0,16},{4,20},{8,24},{12,28},{16,0},{20,4},{24,8},{28,12},{1,17},{... | collective-permute-start | bytes 393224 | tf_op jit(solution)/shard_map/ppermute | solution.py:451
  77.2 40.5 %collective-permute-start.5 = (f32[4,768,128]{2,1,0:T(8,128)}, f32[4,768,128]{2,1,0:T(8,128)}, u32[]{:S(2)}, u32[]{:S(2)}) collective-permute-start(f32[4,768,128]{2,1,0:T(8,128)} %get-tuple-element.106), channel_id=1, source_target_pairs={{0,4},{4,0},{8,12},{12,8},{16,20},{20,16},{24,28},{28,24},{1,5},{5... | collective-permute-start | bytes 4718600 | tf_op jit(solution)/shard_map/ppermute | solution.py:451
  78.2 44.8 %collective-permute-start.6 = (f32[4,768,128]{2,1,0:T(8,128)}, f32[4,768,128]{2,1,0:T(8,128)}, u32[]{:S(2)}, u32[]{:S(2)}) collective-permute-start(f32[4,768,128]{2,1,0:T(8,128)} %get-tuple-element.108), channel_id=1, source_target_pairs={{0,8},{4,12},{8,0},{12,4},{16,24},{20,28},{24,16},{28,20},{1,9},{5... | collective-permute-start | bytes 4718600 | tf_op jit(solution)/shard_map/ppermute | solution.py:451
  110.4 15.7 %collective-permute-start.4 = (f32[256,128]{1,0:T(8,128)}, f32[256,128]{1,0:T(8,128)}, u32[]{:S(2)}, u32[]{:S(2)}) collective-permute-start(f32[256,128]{1,0:T(8,128)} %get-tuple-element.104.refs_1_), channel_id=1, source_target_pairs={{0,4},{4,0},{8,12},{12,8},{16,20},{20,16},{24,28},{28,24},{1,5},{5... | collective-permute-start | bytes 393224 | tf_op jit(solution)/shard_map/ppermute | solution.py:451
  111.0 18.5 %collective-permute-start.3 = (f32[2,512,1024]{2,1,0:T(8,128)}, f32[2,512,1024]{2,1,0:T(8,128)}, u32[]{:S(2)}, u32[]{:S(2)}) collective-permute-start(f32[2,512,1024]{2,1,0:T(8,128)} %get-tuple-element.103), channel_id=1, source_target_pairs={{0,1},{1,0},{2,3},{3,2},{4,5},{5,4},{6,7},{7,6},{8,9},{9,8},{10,11... | collective-permute-start | bytes 12582920 | tf_op jit(solution)/shard_map/ppermute | solution.py:451
  127.8 5.3 %collective-permute-start.8 = (f32[256,128]{1,0:T(8,128)}, f32[256,128]{1,0:T(8,128)}, u32[]{:S(2)}, u32[]{:S(2)}) collective-permute-start(f32[256,128]{1,0:T(8,128)} %get-tuple-element.119.refs_2_), channel_id=1, source_target_pairs={{0,8},{4,12},{8,0},{12,4},{16,24},{20,28},{24,16},{28,20},{1,9},{5... | collective-permute-start | bytes 393224 | tf_op jit(solution)/shard_map/ppermute | solution.py:451
  134.9 9.0 %collective-permute-start.9 = (f32[256,128]{1,0:T(8,128)}, f32[256,128]{1,0:T(8,128)}, u32[]{:S(2)}, u32[]{:S(2)}) collective-permute-start(f32[256,128]{1,0:T(8,128)} %get-tuple-element.121.refs_12_), channel_id=1, source_target_pairs={{0,16},{4,20},{8,24},{12,28},{16,0},{20,4},{24,8},{28,12},{1,17},{... | collective-permute-start | bytes 393224 | tf_op jit(solution)/shard_map/ppermute | solution.py:451
  135.2 73.4 %collective-permute-start.7 = (f32[512,1024]{1,0:T(8,128)}, f32[512,1024]{1,0:T(8,128)}, u32[]{:S(2)}, u32[]{:S(2)}) collective-permute-start(f32[512,1024]{1,0:T(8,128)} %far_sums.2.refs_4_), channel_id=1, source_target_pairs={{0,2},{1,3},{2,0},{3,1},{4,6},{5,7},{6,4},{7,5},{8,10},{9,11},{10,... | collective-permute-start | bytes 6291464 | tf_op jit(solution)/shard_map/ppermute | solution.py:451
  137.3 49.7 %collective-permute-start.11 = (f32[2,768,128]{2,1,0:T(8,128)}, f32[2,768,128]{2,1,0:T(8,128)}, u32[]{:S(2)}, u32[]{:S(2)}) collective-permute-start(f32[2,768,128]{2,1,0:T(8,128)} %get-tuple-element.130), channel_id=1, source_target_pairs={{0,8},{4,12},{8,0},{12,4},{16,24},{20,28},{24,16},{28,20},{1,9},{5... | collective-permute-start | bytes 2359304 | tf_op jit(solution)/shard_map/ppermute | solution.py:451
  139.1 52.4 %collective-permute-start.12 = (f32[2,768,128]{2,1,0:T(8,128)}, f32[2,768,128]{2,1,0:T(8,128)}, u32[]{:S(2)}, u32[]{:S(2)}) collective-permute-start(f32[2,768,128]{2,1,0:T(8,128)} %get-tuple-element.132), channel_id=1, source_target_pairs={{0,16},{4,20},{8,24},{12,28},{16,0},{20,4},{24,8},{28,12},{1,17},{... | collective-permute-start | bytes 2359304 | tf_op jit(solution)/shard_map/ppermute | solution.py:451
  155.8 35.7 %collective-permute-start.10 = (f32[4,512,128]{2,1,0:T(8,128)}, f32[4,512,128]{2,1,0:T(8,128)}, u32[]{:S(2)}, u32[]{:S(2)}) collective-permute-start(f32[4,512,128]{2,1,0:T(8,128)} %get-tuple-element.128), channel_id=1, source_target_pairs={{0,4},{4,0},{8,12},{12,8},{16,20},{20,16},{24,28},{28,24},{1,5},{5... | collective-permute-start | bytes 3145736 | tf_op jit(solution)/shard_map/ppermute | solution.py:451
  181.1 60.6 %collective-permute-start.15 = (f32[512,1024]{1,0:T(8,128)}, f32[512,1024]{1,0:T(8,128)}, u32[]{:S(2)}, u32[]{:S(2)}) collective-permute-start(f32[512,1024]{1,0:T(8,128)} %far_sums.3.refs_8_), channel_id=1, source_target_pairs={{0,2},{1,3},{2,0},{3,1},{4,6},{5,7},{6,4},{7,5},{8,10},{9,11},{10,... | collective-permute-start | bytes 6291464 | tf_op jit(solution)/shard_map/ppermute | solution.py:451
  194.6 38.0 %collective-permute-start.22 = (f32[2,512,128]{2,1,0:T(8,128)}, f32[2,512,128]{2,1,0:T(8,128)}, u32[]{:S(2)}, u32[]{:S(2)}) collective-permute-start(f32[2,512,128]{2,1,0:T(8,128)} %get-tuple-element.134.refs_7_), channel_id=1, source_target_pairs={{0,8},{4,12},{8,0},{12,4},{16,24},{20,28},{24,16},{28,20},{1,9},{5... | collective-permute-start | bytes 1572872 | tf_op jit(solution)/shard_map/ppermute | solution.py:451
  194.6 22.9 %collective-permute-start.18 = (f32[1,768,128]{2,1,0:T(8,128)}, f32[1,768,128]{2,1,0:T(8,128)}, u32[]{:S(2)}, u32[]{:S(2)}) collective-permute-start(f32[1,768,128]{2,1,0:T(8,128)} %get-tuple-element.146), channel_id=1, source_target_pairs={{0,16},{4,20},{8,24},{12,28},{16,0},{20,4},{24,8},{28,12},{1,17},{... | collective-permute-start | bytes 1179656 | tf_op jit(solution)/shard_map/ppermute | solution.py:451
  197.8 19.7 %collective-permute-start.19 = (f32[1,768,128]{2,1,0:T(8,128)}, f32[1,768,128]{2,1,0:T(8,128)}, u32[]{:S(2)}, u32[]{:S(2)}) collective-permute-start(f32[1,768,128]{2,1,0:T(8,128)} %get-tuple-element.147), channel_id=1, source_target_pairs={{0,4},{4,0},{8,12},{12,8},{16,20},{20,16},{24,28},{28,24},{1,5},{5... | collective-permute-start | bytes 1179656 | tf_op jit(solution)/shard_map/ppermute | solution.py:451
  210.1 6.0 %collective-permute-start.16 = (f32[80,128]{1,0:T(8,128)}, f32[80,128]{1,0:T(8,128)}, u32[]{:S(2)}, u32[]{:S(2)}) collective-permute-start(f32[80,128]{1,0:T(8,128)} %pack_small.1.refs_5_.refs_0_), channel_id=1, source_target_pairs={{0,4},{4,0},{8,12},{12,8},{16,20},{20,16},{24,28},{28,24},{1,5},{5... | collective-permute-start | bytes 122888 | tf_op jit(solution)/shard_map/ppermute | solution.py:451
  217.5 5.1 %collective-permute-start.17 = (f32[80,128]{1,0:T(8,128)}, f32[80,128]{1,0:T(8,128)}, u32[]{:S(2)}, u32[]{:S(2)}) collective-permute-start(f32[80,128]{1,0:T(8,128)} %sums.9.refs_9_.refs_0_), channel_id=1, source_target_pairs={{0,8},{4,12},{8,0},{12,4},{16,24},{20,28},{24,16},{28,20},{1,9},{5... | collective-permute-start | bytes 122888 | tf_op jit(solution)/shard_map/ppermute | solution.py:451
  224.0 6.7 %collective-permute-start.20 = (f32[80,128]{1,0:T(8,128)}, f32[80,128]{1,0:T(8,128)}, u32[]{:S(2)}, u32[]{:S(2)}) collective-permute-start(f32[80,128]{1,0:T(8,128)} %sums.10.refs_0_.refs_2_), channel_id=1, source_target_pairs={{0,16},{4,20},{8,24},{12,28},{16,0},{20,4},{24,8},{28,12},{1,17},{... | collective-permute-start | bytes 122888 | tf_op jit(solution)/shard_map/ppermute | solution.py:451
  232.1 2.4 collective-permute-start.21
  232.1 9.5 %collective-permute-start.14 = (f32[256,1024]{1,0:T(8,128)}, f32[256,1024]{1,0:T(8,128)}, u32[]{:S(2)}, u32[]{:S(2)}) collective-permute-start(f32[256,1024]{1,0:T(8,128)} %get-tuple-element.145), channel_id=1, source_target_pairs={{0,1},{1,0},{2,3},{3,2},{4,5},{5,4},{6,7},{7,6},{8,9},{9,8},{10,11... | collective-permute-start | bytes 3145736 | tf_op jit(solution)/shard_map/ppermute | solution.py:451
  232.6 9.0 %collective-permute-start.13 = (f32[256,1024]{1,0:T(8,128)}, f32[256,1024]{1,0:T(8,128)}, u32[]{:S(2)}, u32[]{:S(2)}) collective-permute-start(f32[256,1024]{1,0:T(8,128)} %get-tuple-element.143.refs_9_), channel_id=1, source_target_pairs={{0,1},{1,0},{2,3},{3,2},{4,5},{5,4},{6,7},{7,6},{8,9},{9,8},{10,11... | collective-permute-start | bytes 3145736 | tf_op jit(solution)/shard_map/ppermute | solution.py:451
  234.5 14.6 %collective-permute-start.24 = (f32[1,512,128]{2,1,0:T(8,128)}, f32[1,512,128]{2,1,0:T(8,128)}, u32[]{:S(2)}, u32[]{:S(2)}) collective-permute-start(f32[1,512,128]{2,1,0:T(8,128)} %sums.12.refs_2_), channel_id=1, source_target_pairs={{0,16},{4,20},{8,24},{12,28},{16,0},{20,4},{24,8},{28,12},{1,17},{... | collective-permute-start | bytes 786440 | tf_op jit(solution)/shard_map/ppermute | solution.py:451
  235.9 4.3 %collective-permute-start.23 = (f32[80,128]{1,0:T(8,128)}, f32[80,128]{1,0:T(8,128)}, u32[]{:S(2)}, u32[]{:S(2)}) collective-permute-start(f32[80,128]{1,0:T(8,128)} %sums.13.refs_0_.refs_2_), channel_id=1, source_target_pairs={{0,2},{1,3},{2,0},{3,1},{4,6},{5,7},{6,4},{7,5},{8,10},{9,11},{10,... | collective-permute-start | bytes 122888 | tf_op jit(solution)/shard_map/ppermute | solution.py:451
Sparse Core Ops, SparseCore 0:
  29.0 80.9 reduce-scatter.2
  137.4 94.6 reduce-scatter.4

commit v4 on v3

--- a/solution.py
+++ b/solution.py
@@ -23,7 +23,7 @@
 COST_FAR = 13 * STEP
 COST_NEAR = 0
 COST_END = 10 * STEP
-COST_ATTEND = 16 * STEP
+COST_ATTEND = 6 * STEP
 COST_KEYS = 50 * STEP
 PARTS = ((3, 1), (0, 3))
 
@@ -512,7 +512,7 @@
 def attend_kernel(
     head, tokens, per_step, base, lengths, qf, kf, v, qt, ga, cs, expand, basis_i,
     normed, cot, hidden0, hidden1, down_w, out_w, entered_i, own_i, came_i,
-    gq_o, gk_o, gv_o, back_o, total_o, qb_o, send_o, keep_o, *refs,
+    gq_o, gk_o, gv_o, back_o, total_o, qb_o, keep_o, far0_o, far1_o, near_o, *refs,
 ):
     piece_o, state_s, q_acc, o_acc, total_s = refs
     step = pl.program_id(0)
@@ -630,7 +630,7 @@
     state_s[...] = state
     total_s[...] = total
     outward = outward + nn(below(*mixes), out_w[...])
-    by_core(step & 1, send_o, keep_o, outward)
+    by_core(step, outward, keep_o, far0_o, far1_o, near_o)
 
     @pl.when(step == pl.num_programs(0) - 1)
     def _():
@@ -641,16 +641,22 @@
             write_up(piece_o, i, i * LANE, q_acc)
 
 
-def by_core(core, send, keep, value):
-    mine = lax.axis_index("branch") & 1
-
-    @pl.when(core != mine)
-    def _():
-        send[0] = value
-
-    @pl.when(core == mine)
+def by_core(share, value, keep, far0, far1, near):
+    core, chip = branch_place()
+    other, mine = share & 1 != core, share >> 1 == chip
+
+    @pl.when(jnp.logical_not(other))
     def _():
         keep[0] = value
+
+    @pl.when(other & jnp.logical_not(mine))
+    def _():
+        far0[...] = value[: ROWS // 2]
+        far1[...] = value[ROWS // 2 :]
+
+    @pl.when(other & mine)
+    def _():
+        near[...] = value
 
 
 def attend(
@@ -663,7 +669,8 @@
     chunks = tokens // CHUNK
     part = hidden0.shape[1]
     piece = shaped((model // LANE, 2 * width, LANE))
-    chip = pl.BlockSpec((1, ROWS, model), lambda i: (i >> 1, 0, 0))
+    chip = pl.BlockSpec((1, ROWS, model), lambda i: (i >> 1 ^ (1 - branch_place()[1]), 0, 0))
+    sent = [shaped((rows, model)) for rows in (ROWS // 2, ROWS // 2, ROWS)]
     row = rows_at(ROWS, width)
     packed = whole(width, LANE)
 
@@ -694,7 +701,7 @@
             packed,
             whole(8, width),
             chip,
-            chip,
+            *[whole(*a.shape) for a in sent],
             whole(*piece.shape),
         ],
         [
@@ -704,7 +711,8 @@
             shaped((chunks, width, LANE)),
             shaped((width, LANE)),
             shaped((8, width)),
-            *[shaped((tokens // ROWS // 2, ROWS, model))] * 2,
+            shaped((tokens // ROWS // 2, ROWS, model)),
+            *sent,
             piece,
         ],
         **rest,
@@ -968,20 +976,26 @@
     )
 
 
-def far_sums(call, one, other, far=(lambda: 0, lambda: 0), **rest):
-    rows, model = CHUNK, one.shape[2]
-    specs = [pl.BlockSpec((1, rows, model), lambda i, at=at: (at(), i, 0)) for at in far]
-
-    def body(one, other, out):
-        out[...] = one[0] + other[0]
+def far_sums(call, keep, came, **rest):
+    rows, model = CHUNK, keep.shape[2]
+    steps = keep.shape[1] // rows
+    halves = isinstance(came, tuple)
+    spec = lambda at: pl.BlockSpec((1, rows, model), lambda i: (at, i, 0))
+
+    def body(keep, *refs):
+        *came, out = refs
+        if halves:
+            out[...] = keep[0] + jnp.where(pl.program_id(0) == 0, came[0][...], came[1][...])
+        else:
+            out[...] = keep[0] + came[0][0]
 
     return call(
         body,
-        (one, other),
-        specs,
+        (keep, *came) if halves else (keep, came),
+        [spec(0), *([whole(rows, model)] * 2 if halves else [spec(1)])],
         [rows_at(rows, model)],
-        [shaped(one.shape[1:])],
-        grid=(one.shape[1] // rows,),
+        [shaped(keep.shape[1:])],
+        grid=(steps,),
         name="far_sums",
         **rest,
     )
@@ -993,19 +1007,18 @@
     return own, rows_at(CHUNK, model), steps
 
 
-def finish_output(call, x, keep, came_core, came_chip, bias, near):
+def finish_output(call, x, keep, came_core, came_chip, bias):
     share, model = came_chip.shape
     own, row, steps = finish_specs(share, model)
-    part = pl.BlockSpec((1, CHUNK, model), lambda i: (near(), i, 0))
 
     def body(x, keep, core, chip, bias, out):
-        total = (keep[0] + core[0]) + chip[...]
+        total = (keep[0] + core[...]) + chip[...]
         out[...] = (x[...].astype(f32) + total + bias[...]).astype(bf16)
 
     return call(
         body,
         (x, keep, came_core, came_chip, bias),
-        [own, part, part, row, whole(1, model)],
+        [own, pl.BlockSpec((1, CHUNK, model), lambda i: (1, i, 0)), row, row, whole(1, model)],
         [row],
         [shaped((share, model), bf16)],
         grid=(steps,),
@@ -1147,24 +1160,21 @@
     )
     down, up = pieces[:3], pieces[3:]
     down_first, up_first = send(down[0], y_first, 0), send(up[0], z_first, 0)
-    gq, gk, gv, back, state, qb, out_send, out_keep, oq = attend(
-        call, head, len(bits) - 1, lengths, qf, kf, value, qt, ga, cs, expand, basis,
-        normed, cotangent, hidden0, hidden1, down_weight, out_weight, *states,
+    gq, gk, gv, back, state, qb, out_keep, far0, far1, out_near, oq = attend(
+        call, head, len(bits) - 1, lengths, qf, kf, value, qt, ga, cs, expand, basis, normed, cotangent,
+        hidden0, hidden1, down_weight, out_weight, *states,
     )
     came = swapped(state, "batch", 1)
-    out_core = swapped(out_send, "branch", 1)
-    far_chip = lambda: 1 - branch_place()[1]
-    near_chip = lambda: branch_place()[1]
-    down_2, up_2 = sums_of(
+    far_core = swapped(far0, "branch", 1), swapped(far1, "branch", 1)
+    (out_far,) = far_sums(call, out_keep, far_core)
+    out_chip = swapped(out_far, "branch", 2)
+    entered, state = join_states(call, False, tokens, 0, lengths, None, state, came)
+    came = swapped(state, "batch", bits[1])
+    down_2, up_2, out_near = sums_of(
         call, [whole_of(down[1]), (down_first, 2, 0)], [whole_of(up[1]), (up_first, 2, 0)],
-        after=(sum0,),
-    )
-    entered, state = join_states(
-        call, False, tokens, 0, lengths, None, state, came, flops=50 * STEP
-    )
-    came = swapped(state, "batch", bits[1])
-    (out_far,) = far_sums(call, out_keep, out_core, (far_chip, far_chip))
-    out_chip = swapped(out_far, "branch", 2)
+        after=(sum0,), through=(out_near,),
+    )
+    out_core = swapped(out_near, "branch", 1)
     for i in range(1, len(bits) - 1):
         entered, state = join_states(call, False, tokens, i, lengths, entered, state, came)
         came = swapped(state, "batch", bits[i + 1])
@@ -1180,7 +1190,7 @@
     far, gain0, shift0 = inward(call, True, *in_args, flops=COST_FAR)
     cores = [[i, i + 1] for i in range(0, branch, 2)]
     far = lax.all_to_all(far, "branch", 0, 0, axis_index_groups=cores, tiled=True)
-    (grad_far,) = far_sums(call, far, far, (lambda: 0, lambda: 1))
+    (grad_far,) = far_sums(call, far, far)
     grad_chip = swapped(grad_far, "branch", 2)
     kv_2, down_3, up_3 = sums_of(
         call, [whole_of(kv[1]), (kv_first, 2, 0)],
@@ -1196,7 +1206,7 @@
     came = swapped(small, "batch", 1)
     grad_core = swapped(near0, "branch", 1), swapped(near1, "branch", 1)
     output = finish_output(
-        call, inputs, out_keep, out_core, out_chip, out_bias.reshape(1, model), near_chip
+        call, inputs, out_keep, out_core, out_chip, out_bias.reshape(1, model)
     )
     (small,) = sums_of(call, [whole_of(small), whole_of(came)])
     came = swapped(small, "batch", bits[1])

time: 259 us -> 250 us (0.965)
  waiting for transfers between devices: 45.4 us -> 35.3 us
    ppermute x25 -> x27, waiting for transfers between devices: 45.3 us -> 35.3 us  [swapped(): return lax.ppermute(value, axis, [(i, i ^ distance) for i in range(size)])]
    ppermute x25 -> x27, starting transfers between devices: 28.4 us -> 29.1 us  [swapped(): return lax.ppermute(value, axis, [(i, i ^ distance) for i in range(size)])]
  transfers between devices with their start and end apart: 27 -> 29, of which waited for: 11 -> 12; matrix products, arithmetic and copies ran while one was open for 0% -> 0% of each run, Pallas kernels for 51% -> 53%
where the time goes in v4:
time: 250 us; the launch traced here: 249 us
  Pallas kernels  157 us (63%)
  waiting for transfers between devices  35.3 us (14%)
  starting transfers between devices  29.1 us (12%)
  between operations  14.1 us (6%)
  blocking collectives  11.9 us (5%)
    pallas_call x27, Pallas kernels, __call__(): pl.pallas_call(without, in_specs=[*in_specs, *[place] * len(skipped)], ou...  157 us
    ppermute x27, waiting for transfers between devices, swapped(): return lax.ppermute(value, axis, [(i, i ^ distance) for i in range(size)])  35.3 us
    ppermute x27, starting transfers between devices, swapped(): return lax.ppermute(value, axis, [(i, i ^ distance) for i in range(size)])  29.1 us
    all_to_all x1, blocking collectives, per_device(): lax.all_to_all(far, 'branch', 0, 0, axis_index_groups=cores, tiled=True)  11.9 us
  transfers between devices with their start and end apart: 29, of which 12 were waited for; matrix products, arithmetic and copies ran while one was open for 0% of the time, Pallas kernels for 53%

profile of v4, /device:TPU:0, one launch (start us, length us, event | category | flops | bytes accessed | tf_op | source)
XLA Modules:
  0.0 249.1 jit_solution(13715241420961551818)
XLA Ops:
  8.5 20.4 %front.1 = (bf16[2048,1024]{1,0:T(8,128)(2,1)}, f32[8,1024]{1,0:T(8,128)}, bf16[2048,256]{1,0:T(8,128)(2,1)}, bf16[2048,256]{1,0:T(8,128)(2,1)}, bf16[2048,256]{...) custom-call(s32[8]{0:T(128)} %refs_0_.17, ...), custom_call_target="tpu_custom_call" | custom-call | tf_op jit(solution)/shard_map/front/pallas_call | solution.py:76
  28.9 3.0 %collective-permute-start = (f32[256,128]{1,0:T(8,128)}, f32[256,128]{1,0:T(8,128)}, u32[]{:S(2)}, u32[]{:S(2)}) collective-permute-start(f32[256,128]{1,0:T(8,128)} %get-tuple-element.99.refs_1_), channel_id=1, source_target_pairs={{0,4},{4,0},{8,12},{12,8},{16,20},{20,16},{24,28},{28,24},{1,5},{5... | collective-permute-start | bytes 393224 | tf_op jit(solution)/shard_map/ppermute | solution.py:451
  32.0 8.7 %project_queries.1 = (bf16[2048,256]{1,0:T(8,128)(2,1)}, bf16[2048,256]{1,0:T(8,128)(2,1)}, f32[2048,256]{1,0:T(8,128)}) custom-call(bf16[2048,1024]{1,0:T(8,128)(2,1)} %get-tuple-element.88.refs_0_.refs_8_.refs_9_.refs_10_, bf16[1024,768]{1,0:T(8,128)(2,1)} %get-tuple-element.89.refs_1_.refs_6_, f32[1,768]{1,0:T(1,128)} %get-tuple-element.90.refs_2_, ...), custom_call_target="tpu_custom_call" | custom-call | tf_op jit(solution)/shard_map/project_queries/pallas_call | solution.py:76
  44.0 8.4 %collective-permute-done.1.refs_3_ = f32[256,128]{1,0:T(8,128)} collective-permute-done((f32[256,128]{1,0:T(8,128)}, f32[256,128]{1,0:T(8,128)}, u32[]{:S(2)}, u32[]{:S(2)}) %collective-permute-start.1) | collective-permute-done | bytes 131104 | tf_op jit(solution)/shard_map/ppermute | solution.py:451
  52.4 1.8 join_states.5
  55.8 21.2 %feed_forward.1 = (bf16[2048,768]{1,0:T(8,128)(2,1)}, bf16[2048,768]{1,0:T(8,128)(2,1)}, f32[8,768]{1,0:T(8,128)}, f32[4,768,128]{2,1,0:T(8,128)}, f32[2,768,128...) custom-call(bf16[2048,1024]{1,0:T(8,128)(2,1)} %get-tuple-element.88, ...), custom_call_target="tpu_custom_call" | custom-call | tf_op jit(solution)/shard_map/feed_forward/pallas_call | solution.py:76
  77.7 3.0 %collective-permute-start.4 = (f32[4,768,128]{2,1,0:T(8,128)}, f32[4,768,128]{2,1,0:T(8,128)}, u32[]{:S(2)}, u32[]{:S(2)}) collective-permute-start(f32[4,768,128]{2,1,0:T(8,128)} %get-tuple-element.109), channel_id=1, source_target_pairs={{0,8},{4,12},{8,0},{12,4},{16,24},{20,28},{24,16},{28,20},{1,9},{5... | collective-permute-start | bytes 4718600 | tf_op jit(solution)/shard_map/ppermute | solution.py:451
  80.7 29.9 %attend.1 = (bf16[2048,256]{1,0:T(8,128)(2,1)}, f32[2048,256]{1,0:T(8,128)}, f32[2048,256]{1,0:T(8,128)}, f32[8,256,128]{2,1,0:T(8,128)}, f32[256,128]{1,0:T(8,1...) custom-call(s32[8]{0:T(128)} %refs_0_.17, ...), custom_call_target="tpu_custom_call" | custom-call | flops 6442450944 | tf_op jit(solution)/shard_map/attend/pallas_call | solution.py:76
  111.6 2.1 collective-permute-done.6.refs_1_
  115.2 3.4 %far_sums.2.refs_3_ = f32[512,1024]{1,0:T(8,128)} custom-call(f32[2,512,1024]{2,1,0:T(8,128)} %get-tuple-element.105.refs_0_.refs_1_, f32[256,1024]{1,0:T(8,128)} %collective-permute-done.6.refs_1_, f32[256,1024]{1,0:T(8,128)} %collective-permute-done.7.refs_2_, bf16[2048,256]{1,0:T(8,128)(2,1)} %get-tuple-element.113.refs_3_), custom_call_target="tpu_custom_call" | custom-call | tf_op jit(solution)/shard_map/far_sums/pallas_call | solution.py:76
  121.1 1.8 collective-permute-start.10
  122.9 3.1 %sums.7 = (f32[2,768,128]{2,1,0:T(8,128)}, f32[2,768,128]{2,1,0:T(8,128)}, f32[512,1024]{1,0:T(8,128)}) custom-call(f32[2,768,128]{2,1,0:T(8,128)} %get-tuple-element.106.refs_0_, f32[4,768,128]{2,1,0:T(8,128)} %collective-permute-done.3.refs_1_.refs_3_.refs_2_, f32[2,768,128]{2,1,0:T(8,128)} %get-tuple-element.108.refs_2_, ...), custom_call_target="tpu_custom_call", output_to_operand_aliasing={{2}: (6, {})} | custom-call | tf_op jit(solution)/shard_map/sums/pallas_call | solution.py:76
  126.4 1.8 join_states.7
  132.6 2.5 collective-permute-start.14
  136.5 12.1 %keys.1 = (bf16[2048,512]{1,0:T(8,128)(2,1)}, f32[8,512]{1,0:T(8,128)}, f32[4,512,128]{2,1,0:T(8,128)}, f32[2,512,128]{2,1,0:T(8,128)}, f32[2,512,128]{2,1,0:T(8,128)}) custom-call(s32[8]{0:T(128)} %refs_0_.17, bf16[2048,256]{1,0:T(8,128)(2,1)} %get-tuple-element.94.refs_2_.refs_1_, bf16[2048,256]{1,0:T(8,128)(2,1)} %get-tuple-element.95.refs_3_.refs_2_, ...), custom_call_target="tpu_custom_call" | custom-call | flops 53687091200 | tf_op jit(solution)/shard_map/keys/pallas_call | solution.py:76
  149.1 9.1 %inward.2 = (f32[2,512,1024]{2,1,0:T(8,128)}, f32[8,1024]{1,0:T(8,128)}, f32[8,1024]{1,0:T(8,128)}) custom-call(bf16[2048,1024]{1,0:T(8,128)(2,1)} %refs_0_.21, bf16[2048,256]{1,0:T(8,128)(2,1)} %get-tuple-element.118.refs_1_, bf16[2048,768]{1,0:T(8,128)(2,1)} %get-tuple-element.119.refs_2_, bf16[2048,256]{1,0:T(8,128)(2,1)} %get-tuple-element.113.refs_3_, ...), custom_call_target="tpu_custom_call" | custom-call | flops 13958643712 | tf_op jit(solution)/shard_map/inward/pallas_call | solution.py:76
  158.2 11.9 %all_to_all.5.refs_0_.refs_1_ = f32[2,512,1024]{2,1,0:T(8,128)} all-to-all(f32[2,512,1024]{2,1,0:T(8,128)} %get-tuple-element.139.refs_2_), channel_id=1, replica_groups={{0,1},{2,3},{4,5},{6,7},{8,9},{10,11},{12,13},{14,15},{16,17},{18,19},{..., dimensions={0} | all-to-all | bytes 8388608 | tf_op jit(solution)/shard_map/all_to_all | solution.py:1192
  170.0 3.3 %far_sums.3.refs_8_ = f32[512,1024]{1,0:T(8,128)} custom-call(f32[2,512,1024]{2,1,0:T(8,128)} %all_to_all.5.refs_0_.refs_1_, f32[2,512,1024]{2,1,0:T(8,128)} %all_to_all.5.refs_0_.refs_1_, f32[2,512,1024]{2,1,0:T(8,128)} %get-tuple-element.139.refs_2_), custom_call_target="tpu_custom_call" | custom-call | tf_op jit(solution)/shard_map/far_sums/pallas_call | solution.py:76
  173.3 7.7 %collective-permute-done.13.refs_4_.refs_3_ = f32[2,768,128]{2,1,0:T(8,128)} collective-permute-done((f32[2,768,128]{2,1,0:T(8,128)}, f32[2,768,128]{2,1,0:T(8,128)}, u32[]{:S(2)}, u32[]{:S(2)}) %collective-permute-start.13) | collective-permute-done | bytes 786464 | tf_op jit(solution)/shard_map/ppermute | solution.py:451
  181.0 2.5 collective-permute-done.14.refs_7_
  183.5 3.1 %sums.8 = (f32[2,512,128]{2,1,0:T(8,128)}, f32[1,768,128]{2,1,0:T(8,128)}, f32[1,768,128]{2,1,0:T(8,128)}) custom-call(f32[2,512,128]{2,1,0:T(8,128)} %get-tuple-element.133.refs_0_, f32[4,512,128]{2,1,0:T(8,128)} %collective-permute-done.12.refs_1_.refs_2_, f32[2,768,128]{2,1,0:T(8,128)} %get-tuple-element.135.refs_2_.refs_1_, ...), custom_call_target="tpu_custom_call" | custom-call | tf_op jit(solution)/shard_map/sums/pallas_call | solution.py:76
  186.6 2.1 collective-permute-start.20
  190.2 10.5 %inward.3 = (f32[256,1024]{1,0:T(8,128)}, f32[256,1024]{1,0:T(8,128)}, f32[512,1024]{1,0:T(8,128)}, f32[8,1024]{1,0:T(8,128)}, f32[8,1024]{1,0:T(8,128)}) custom-call(bf16[2048,1024]{1,0:T(8,128)(2,1)} %refs_0_.21, bf16[2048,256]{1,0:T(8,128)(2,1)} %get-tuple-element.118.refs_1_, bf16[2048,768]{1,0:T(8,128)(2,1)} %get-tuple-element.119.refs_2_, ...), custom_call_target="tpu_custom_call" | custom-call | tf_op jit(solution)/shard_map/inward/pallas_call | solution.py:76
  202.7 4.1 %finish_output.1.refs_2_ = bf16[512,1024]{1,0:T(8,128)(2,1)} custom-call(bf16[2048,1024]{1,0:T(8,128)(2,1)} %refs_0_.21, f32[2,512,1024]{2,1,0:T(8,128)} %get-tuple-element.105.refs_0_.refs_1_, f32[512,1024]{1,0:T(8,128)} %collective-permute-done.8.refs_2_, f32[512,1024]{1,0:T(8,128)} %collective-permute-done.9.refs_10_.refs_3_, f32[1,1024]{1,0:T(1,128)} %bitcast.13, ...), custom_call_target="tpu_custom_call" | custom-call | tf_op jit(solution)/shard_map/finish_output/pallas_call | solution.py:76
  208.3 3.0 %finish_feed.1 = (f32[1024,128]{1,0:T(8,128)}, f32[128,1024]{1,0:T(8,128)}) custom-call(f32[1,512,128]{2,1,0:T(8,128)} %reduce-scatter.3.cloned.1.call-done.refs_5_.refs_0_, f32[2,768,128]{2,1,0:T(8,128)} %get-tuple-element.135.refs_2_.refs_1_, f32[4,768,128]{2,1,0:T(8,128)} %collective-permute-done.3.refs_1_.refs_3_.refs_2_, ...), custom_call_target="tpu_custom_call" | custom-call | tf_op jit(solution)/shard_map/finish_feed/pallas_call | solution.py:76
  215.6 5.2 %collective-permute-done.22.refs_1_ = f32[80,128]{1,0:T(8,128)} collective-permute-done((f32[80,128]{1,0:T(8,128)}, f32[80,128]{1,0:T(8,128)}, u32[]{:S(2)}, u32[]{:S(2)}) %collective-permute-start.22) | collective-permute-done | bytes 40992 | tf_op jit(solution)/shard_map/ppermute | solution.py:451
  222.7 1.9 sums.12.refs_2_
  226.5 2.8 %collective-permute-start.25 = (f32[80,128]{1,0:T(8,128)}, f32[80,128]{1,0:T(8,128)}, u32[]{:S(2)}, u32[]{:S(2)}) collective-permute-start(f32[80,128]{1,0:T(8,128)} %sums.13.refs_0_.refs_2_), channel_id=1, source_target_pairs={{0,2},{1,3},{2,0},{3,1},{4,6},{5,7},{6,4},{7,5},{8,10},{9,11},{10,... | collective-permute-start | bytes 122888 | tf_op jit(solution)/shard_map/ppermute | solution.py:451
  229.3 2.3 collective-permute-done.25.refs_1_
  233.1 5.2 %finish_input.1.refs_5_ = f32[512,1024]{1,0:T(8,128)} custom-call(bf16[2048,1024]{1,0:T(8,128)(2,1)} %refs_0_.21, bf16[2048,1024]{1,0:T(8,128)(2,1)} %refs_1_.5, f32[1,1024]{1,0:T(1,128)} %bitcast.12, f32[512,1024]{1,0:T(8,128)} %get-tuple-element.150.refs_3_, f32[256,1024]{1,0:T(8,128)} %collective-permute-done.15.refs_4_, ...), custom_call_target="tpu_custom_call" | custom-call | tf_op jit(solution)/shard_map/finish_input/pallas_call | solution.py:76
  238.3 1.8 collective-permute-done.26.refs_4_
  240.1 2.1 finish_heads.1
  (57 shorter events, 33.3 us)
Async XLA Ops:
  7.2 115.7 %reduce-scatter.3.cloned.1.call-start = ((), (), s32[]{:S(2)}) async-start(), calls=%async_computation.3 | async-start | bytes 2359296 | tf_op jit(solution)/shard_map/reduce_scatter | solution.py:1148
  28.9 204.2 %reduce-scatter.5.cloned.1.call-start = ((), (), s32[]{:S(2)}) async-start(), calls=%async_computation.4 | async-start | bytes 2359296 | tf_op jit(solution)/shard_map/reduce_scatter | solution.py:1148
  28.9 11.8 %collective-permute-start = (f32[256,128]{1,0:T(8,128)}, f32[256,128]{1,0:T(8,128)}, u32[]{:S(2)}, u32[]{:S(2)}) collective-permute-start(f32[256,128]{1,0:T(8,128)} %get-tuple-element.99.refs_1_), channel_id=1, source_target_pairs={{0,4},{4,0},{8,12},{12,8},{16,20},{20,16},{24,28},{28,24},{1,5},{5... | collective-permute-start | bytes 393224 | tf_op jit(solution)/shard_map/ppermute | solution.py:451
  42.4 10.0 %collective-permute-start.1 = (f32[256,128]{1,0:T(8,128)}, f32[256,128]{1,0:T(8,128)}, u32[]{:S(2)}, u32[]{:S(2)}) collective-permute-start(f32[256,128]{1,0:T(8,128)} %get-tuple-element.101.refs_2_), channel_id=1, source_target_pairs={{0,8},{4,12},{8,0},{12,4},{16,24},{20,28},{24,16},{28,20},{1,9},{5... | collective-permute-start | bytes 393224 | tf_op jit(solution)/shard_map/ppermute | solution.py:451
  54.2 26.5 %collective-permute-start.2 = (f32[256,128]{1,0:T(8,128)}, f32[256,128]{1,0:T(8,128)}, u32[]{:S(2)}, u32[]{:S(2)}) collective-permute-start(f32[256,128]{1,0:T(8,128)} %get-tuple-element.104.refs_16_), channel_id=1, source_target_pairs={{0,16},{4,20},{8,24},{12,28},{16,0},{20,4},{24,8},{28,12},{1,17},{... | collective-permute-start | bytes 393224 | tf_op jit(solution)/shard_map/ppermute | solution.py:451
  77.0 45.9 %collective-permute-start.3 = (f32[4,768,128]{2,1,0:T(8,128)}, f32[4,768,128]{2,1,0:T(8,128)}, u32[]{:S(2)}, u32[]{:S(2)}) collective-permute-start(f32[4,768,128]{2,1,0:T(8,128)} %get-tuple-element.107), channel_id=1, source_target_pairs={{0,4},{4,0},{8,12},{12,8},{16,20},{20,16},{24,28},{28,24},{1,5},{5... | collective-permute-start | bytes 4718600 | tf_op jit(solution)/shard_map/ppermute | solution.py:451
  77.7 45.2 %collective-permute-start.4 = (f32[4,768,128]{2,1,0:T(8,128)}, f32[4,768,128]{2,1,0:T(8,128)}, u32[]{:S(2)}, u32[]{:S(2)}) collective-permute-start(f32[4,768,128]{2,1,0:T(8,128)} %get-tuple-element.109), channel_id=1, source_target_pairs={{0,8},{4,12},{8,0},{12,4},{16,24},{20,28},{24,16},{28,20},{1,9},{5... | collective-permute-start | bytes 4718600 | tf_op jit(solution)/shard_map/ppermute | solution.py:451
  110.6 3.1 %collective-permute-start.6 = (f32[256,1024]{1,0:T(8,128)}, f32[256,1024]{1,0:T(8,128)}, u32[]{:S(2)}, u32[]{:S(2)}) collective-permute-start(f32[256,1024]{1,0:T(8,128)} %get-tuple-element.111), channel_id=1, source_target_pairs={{0,1},{1,0},{2,3},{3,2},{4,5},{5,4},{6,7},{7,6},{8,9},{9,8},{10,11... | collective-permute-start | bytes 3145736 | tf_op jit(solution)/shard_map/ppermute | solution.py:451
  110.7 4.5 %collective-permute-start.7 = (f32[256,1024]{1,0:T(8,128)}, f32[256,1024]{1,0:T(8,128)}, u32[]{:S(2)}, u32[]{:S(2)}) collective-permute-start(f32[256,1024]{1,0:T(8,128)} %get-tuple-element.112), channel_id=1, source_target_pairs={{0,1},{1,0},{2,3},{3,2},{4,5},{5,4},{6,7},{7,6},{8,9},{9,8},{10,11... | collective-permute-start | bytes 3145736 | tf_op jit(solution)/shard_map/ppermute | solution.py:451
  111.2 8.2 %collective-permute-start.5 = (f32[256,128]{1,0:T(8,128)}, f32[256,128]{1,0:T(8,128)}, u32[]{:S(2)}, u32[]{:S(2)}) collective-permute-start(f32[256,128]{1,0:T(8,128)} %get-tuple-element.110.refs_1_), channel_id=1, source_target_pairs={{0,4},{4,0},{8,12},{12,8},{16,20},{20,16},{24,28},{28,24},{1,5},{5... | collective-permute-start | bytes 393224 | tf_op jit(solution)/shard_map/ppermute | solution.py:451
  121.1 5.3 %collective-permute-start.10 = (f32[256,128]{1,0:T(8,128)}, f32[256,128]{1,0:T(8,128)}, u32[]{:S(2)}, u32[]{:S(2)}) collective-permute-start(f32[256,128]{1,0:T(8,128)} %get-tuple-element.124.refs_2_), channel_id=1, source_target_pairs={{0,8},{4,12},{8,0},{12,4},{16,24},{20,28},{24,16},{28,20},{1,9},{5... | collective-permute-start | bytes 393224 | tf_op jit(solution)/shard_map/ppermute | solution.py:451
  128.2 8.3 %collective-permute-start.11 = (f32[256,128]{1,0:T(8,128)}, f32[256,128]{1,0:T(8,128)}, u32[]{:S(2)}, u32[]{:S(2)}) collective-permute-start(f32[256,128]{1,0:T(8,128)} %get-tuple-element.127.refs_12_), channel_id=1, source_target_pairs={{0,16},{4,20},{8,24},{12,28},{16,0},{20,4},{24,8},{28,12},{1,17},{... | collective-permute-start | bytes 393224 | tf_op jit(solution)/shard_map/ppermute | solution.py:451
  129.2 59.5 %collective-permute-start.9 = (f32[512,1024]{1,0:T(8,128)}, f32[512,1024]{1,0:T(8,128)}, u32[]{:S(2)}, u32[]{:S(2)}) collective-permute-start(f32[512,1024]{1,0:T(8,128)} %far_sums.2.refs_3_), channel_id=1, source_target_pairs={{0,2},{1,3},{2,0},{3,1},{4,6},{5,7},{6,4},{7,5},{8,10},{9,11},{10,... | collective-permute-start | bytes 6291464 | tf_op jit(solution)/shard_map/ppermute | solution.py:451
  131.1 49.9 %collective-permute-start.13 = (f32[2,768,128]{2,1,0:T(8,128)}, f32[2,768,128]{2,1,0:T(8,128)}, u32[]{:S(2)}, u32[]{:S(2)}) collective-permute-start(f32[2,768,128]{2,1,0:T(8,128)} %get-tuple-element.136), channel_id=1, source_target_pairs={{0,8},{4,12},{8,0},{12,4},{16,24},{20,28},{24,16},{28,20},{1,9},{5... | collective-permute-start | bytes 2359304 | tf_op jit(solution)/shard_map/ppermute | solution.py:451
  132.6 50.9 %collective-permute-start.14 = (f32[2,768,128]{2,1,0:T(8,128)}, f32[2,768,128]{2,1,0:T(8,128)}, u32[]{:S(2)}, u32[]{:S(2)}) collective-permute-start(f32[2,768,128]{2,1,0:T(8,128)} %get-tuple-element.138), channel_id=1, source_target_pairs={{0,16},{4,20},{8,24},{12,28},{16,0},{20,4},{24,8},{28,12},{1,17},{... | collective-permute-start | bytes 2359304 | tf_op jit(solution)/shard_map/ppermute | solution.py:451
  135.1 67.2 %collective-permute-start.8 = (f32[512,1024]{1,0:T(8,128)}, f32[512,1024]{1,0:T(8,128)}, u32[]{:S(2)}, u32[]{:S(2)}) collective-permute-start(f32[512,1024]{1,0:T(8,128)} %get-tuple-element.117), channel_id=1, source_target_pairs={{0,1},{1,0},{2,3},{3,2},{4,5},{5,4},{6,7},{7,6},{8,9},{9,8},{10,11... | collective-permute-start | bytes 6291464 | tf_op jit(solution)/shard_map/ppermute | solution.py:451
  148.6 34.9 %collective-permute-start.12 = (f32[4,512,128]{2,1,0:T(8,128)}, f32[4,512,128]{2,1,0:T(8,128)}, u32[]{:S(2)}, u32[]{:S(2)}) collective-permute-start(f32[4,512,128]{2,1,0:T(8,128)} %get-tuple-element.134), channel_id=1, source_target_pairs={{0,4},{4,0},{8,12},{12,8},{16,20},{20,16},{24,28},{28,24},{1,5},{5... | collective-permute-start | bytes 3145736 | tf_op jit(solution)/shard_map/ppermute | solution.py:451
  181.0 52.0 %collective-permute-start.17 = (f32[512,1024]{1,0:T(8,128)}, f32[512,1024]{1,0:T(8,128)}, u32[]{:S(2)}, u32[]{:S(2)}) collective-permute-start(f32[512,1024]{1,0:T(8,128)} %far_sums.3.refs_8_), channel_id=1, source_target_pairs={{0,2},{1,3},{2,0},{3,1},{4,6},{5,7},{6,4},{7,5},{8,10},{9,11},{10,... | collective-permute-start | bytes 6291464 | tf_op jit(solution)/shard_map/ppermute | solution.py:451
  186.5 36.2 %collective-permute-start.24 = (f32[2,512,128]{2,1,0:T(8,128)}, f32[2,512,128]{2,1,0:T(8,128)}, u32[]{:S(2)}, u32[]{:S(2)}) collective-permute-start(f32[2,512,128]{2,1,0:T(8,128)} %get-tuple-element.140.refs_7_), channel_id=1, source_target_pairs={{0,8},{4,12},{8,0},{12,4},{16,24},{20,28},{24,16},{28,20},{1,9},{5... | collective-permute-start | bytes 1572872 | tf_op jit(solution)/shard_map/ppermute | solution.py:451
  186.6 21.7 %collective-permute-start.20 = (f32[1,768,128]{2,1,0:T(8,128)}, f32[1,768,128]{2,1,0:T(8,128)}, u32[]{:S(2)}, u32[]{:S(2)}) collective-permute-start(f32[1,768,128]{2,1,0:T(8,128)} %get-tuple-element.152), channel_id=1, source_target_pairs={{0,16},{4,20},{8,24},{12,28},{16,0},{20,4},{24,8},{28,12},{1,17},{... | collective-permute-start | bytes 1179656 | tf_op jit(solution)/shard_map/ppermute | solution.py:451
  188.6 19.7 %collective-permute-start.21 = (f32[1,768,128]{2,1,0:T(8,128)}, f32[1,768,128]{2,1,0:T(8,128)}, u32[]{:S(2)}, u32[]{:S(2)}) collective-permute-start(f32[1,768,128]{2,1,0:T(8,128)} %get-tuple-element.153), channel_id=1, source_target_pairs={{0,4},{4,0},{8,12},{12,8},{16,20},{20,16},{24,28},{28,24},{1,5},{5... | collective-permute-start | bytes 1179656 | tf_op jit(solution)/shard_map/ppermute | solution.py:451
  202.3 4.5 %collective-permute-start.18 = (f32[80,128]{1,0:T(8,128)}, f32[80,128]{1,0:T(8,128)}, u32[]{:S(2)}, u32[]{:S(2)}) collective-permute-start(f32[80,128]{1,0:T(8,128)} %pack_small.1.refs_5_.refs_0_), channel_id=1, source_target_pairs={{0,4},{4,0},{8,12},{12,8},{16,20},{20,16},{24,28},{28,24},{1,5},{5... | collective-permute-start | bytes 122888 | tf_op jit(solution)/shard_map/ppermute | solution.py:451
  208.2 4.3 %collective-permute-start.19 = (f32[80,128]{1,0:T(8,128)}, f32[80,128]{1,0:T(8,128)}, u32[]{:S(2)}, u32[]{:S(2)}) collective-permute-start(f32[80,128]{1,0:T(8,128)} %sums.9.refs_9_.refs_0_), channel_id=1, source_target_pairs={{0,8},{4,12},{8,0},{12,4},{16,24},{20,28},{24,16},{28,20},{1,9},{5... | collective-permute-start | bytes 122888 | tf_op jit(solution)/shard_map/ppermute | solution.py:451
  214.0 6.8 %collective-permute-start.22 = (f32[80,128]{1,0:T(8,128)}, f32[80,128]{1,0:T(8,128)}, u32[]{:S(2)}, u32[]{:S(2)}) collective-permute-start(f32[80,128]{1,0:T(8,128)} %sums.10.refs_0_.refs_2_), channel_id=1, source_target_pairs={{0,16},{4,20},{8,24},{12,28},{16,0},{20,4},{24,8},{28,12},{1,17},{... | collective-permute-start | bytes 122888 | tf_op jit(solution)/shard_map/ppermute | solution.py:451
  222.2 2.9 %collective-permute-start.23 = (f32[80,128]{1,0:T(8,128)}, f32[80,128]{1,0:T(8,128)}, u32[]{:S(2)}, u32[]{:S(2)}) collective-permute-start(f32[80,128]{1,0:T(8,128)} %sums.11.refs_3_.refs_0_), channel_id=1, source_target_pairs={{0,1},{1,0},{2,3},{3,2},{4,5},{5,4},{6,7},{7,6},{8,9},{9,8},{10,11... | collective-permute-start | bytes 122888 | tf_op jit(solution)/shard_map/ppermute | solution.py:451
  222.2 10.8 %collective-permute-start.16 = (f32[256,1024]{1,0:T(8,128)}, f32[256,1024]{1,0:T(8,128)}, u32[]{:S(2)}, u32[]{:S(2)}) collective-permute-start(f32[256,1024]{1,0:T(8,128)} %get-tuple-element.151), channel_id=1, source_target_pairs={{0,1},{1,0},{2,3},{3,2},{4,5},{5,4},{6,7},{7,6},{8,9},{9,8},{10,11... | collective-permute-start | bytes 3145736 | tf_op jit(solution)/shard_map/ppermute | solution.py:451
  222.7 10.3 %collective-permute-start.15 = (f32[256,1024]{1,0:T(8,128)}, f32[256,1024]{1,0:T(8,128)}, u32[]{:S(2)}, u32[]{:S(2)}) collective-permute-start(f32[256,1024]{1,0:T(8,128)} %get-tuple-element.149.refs_9_), channel_id=1, source_target_pairs={{0,1},{1,0},{2,3},{3,2},{4,5},{5,4},{6,7},{7,6},{8,9},{9,8},{10,11... | collective-permute-start | bytes 3145736 | tf_op jit(solution)/shard_map/ppermute | solution.py:451
  224.6 15.6 %collective-permute-start.26 = (f32[1,512,128]{2,1,0:T(8,128)}, f32[1,512,128]{2,1,0:T(8,128)}, u32[]{:S(2)}, u32[]{:S(2)}) collective-permute-start(f32[1,512,128]{2,1,0:T(8,128)} %sums.12.refs_2_), channel_id=1, source_target_pairs={{0,16},{4,20},{8,24},{12,28},{16,0},{20,4},{24,8},{28,12},{1,17},{... | collective-permute-start | bytes 786440 | tf_op jit(solution)/shard_map/ppermute | solution.py:451
  226.5 5.1 %collective-permute-start.25 = (f32[80,128]{1,0:T(8,128)}, f32[80,128]{1,0:T(8,128)}, u32[]{:S(2)}, u32[]{:S(2)}) collective-permute-start(f32[80,128]{1,0:T(8,128)} %sums.13.refs_0_.refs_2_), channel_id=1, source_target_pairs={{0,2},{1,3},{2,0},{3,1},{4,6},{5,7},{6,4},{7,5},{8,10},{9,11},{10,... | collective-permute-start | bytes 122888 | tf_op jit(solution)/shard_map/ppermute | solution.py:451
Sparse Core Ops, SparseCore 0:
  29.0 80.9 reduce-scatter.2
  131.2 95.6 reduce-scatter.4

commit v5 on v4

--- a/solution.py
+++ b/solution.py
@@ -22,7 +22,7 @@
 STEP = 2**30
 COST_FAR = 13 * STEP
 COST_NEAR = 0
-COST_END = 10 * STEP
+COST_END = 12 * STEP
 COST_ATTEND = 6 * STEP
 COST_KEYS = 50 * STEP
 PARTS = ((3, 1), (0, 3))
@@ -1187,7 +1187,7 @@
     )
     kv_first = send(kv[0], y_first, 0)
     in_args = (inputs, gpre0, gpre1, gq, gkv, up_weight, w_perm)
-    far, gain0, shift0 = inward(call, True, *in_args, flops=COST_FAR)
+    far, gain0, shift0 = inward(call, True, *in_args, after=(out_core,), flops=COST_FAR)
     cores = [[i, i + 1] for i in range(0, branch, 2)]
     far = lax.all_to_all(far, "branch", 0, 0, axis_index_groups=cores, tiled=True)
     (grad_far,) = far_sums(call, far, far)
@@ -1216,16 +1216,16 @@
     for bit in bits[2:]:
         (small,) = sums_of(call, [whole_of(small), whole_of(came)])
         came = swapped(small, "batch", bit)
+    (kv_3,) = sums_of(call, [(kv[2], 1, 1), (kv_first, 1, 3), (kv_2, 1, 1)])
+    kv_3 = send(kv_3, y_first, 2)
     (small,) = sums_of(call, [whole_of(small), whole_of(came)])
     came = swapped(small, "branch", 1)
-    (kv_3,) = sums_of(call, [(kv[2], 1, 1), (kv_first, 1, 3), (kv_2, 1, 1)])
-    kv_3 = send(kv_3, y_first, 2)
     (small,) = sums_of(call, [whole_of(small), whole_of(came)], flops=COST_END)
     came = swapped(small, "branch", 2)
-    small = finish_small(call, small, came, [model, model, model, 3 * width * branch, up_bias.size * branch])
     input_grad = finish_input(
         call, inputs, cotangent, gain, grad_keep, grad_core, grad_chip, after=(sum_oq,)
     )
+    small = finish_small(call, small, came, [model, model, model, 3 * width * branch, up_bias.size * branch])
     out_sum, qkv_sum = finish_heads(call, head, sum_oq, (kv, kv_first, kv_2, kv_3))
     down_sum, out_sum = finish(down_sum, 1, low), finish(out_sum, 1, low)
     up_sum, qkv_sum = finish(up_sum, 0, low), finish(qkv_sum, 0, low)

time: 250 us -> 249 us (level)
  transfers between devices with their start and end apart: 29 -> 29, of which waited for: 12 -> 13; matrix products, arithmetic and copies ran while one was open for 0% -> 0% of each run, Pallas kernels for 53% -> 54%
where the time goes in v5:
time: 249 us; the launch traced here: 248 us
  Pallas kernels  157 us (63%)
  waiting for transfers between devices  32.9 us (13%)
  starting transfers between devices  30 us (12%)
  between operations  14.1 us (6%)
  blocking collectives  11.9 us (5%)
    pallas_call x27, Pallas kernels, __call__(): pl.pallas_call(without, in_specs=[*in_specs, *[place] * len(skipped)], ou...  157 us
    ppermute x27, waiting for transfers between devices, swapped(): return lax.ppermute(value, axis, [(i, i ^ distance) for i in range(size)])  32.9 us
    ppermute x27, starting transfers between devices, swapped(): return lax.ppermute(value, axis, [(i, i ^ distance) for i in range(size)])  30 us
    all_to_all x1, blocking collectives, per_device(): lax.all_to_all(far, 'branch', 0, 0, axis_index_groups=cores, tiled=True)  11.9 us
  transfers between devices with their start and end apart: 29, of which 13 were waited for; matrix products, arithmetic and copies ran while one was open for 0% of the time, Pallas kernels for 54%

profile of v5, /device:TPU:0, one launch (start us, length us, event | category | flops | bytes accessed | tf_op | source)
XLA Modules:
  0.0 247.6 jit_solution(1274723925807873829)
XLA Ops:
  8.5 20.4 %front.1 = (bf16[2048,1024]{1,0:T(8,128)(2,1)}, f32[8,1024]{1,0:T(8,128)}, bf16[2048,256]{1,0:T(8,128)(2,1)}, bf16[2048,256]{1,0:T(8,128)(2,1)}, bf16[2048,256]{...) custom-call(s32[8]{0:T(128)} %refs_0_.17, ...), custom_call_target="tpu_custom_call" | custom-call | tf_op jit(solution)/shard_map/front/pallas_call | solution.py:76
  28.9 3.0 %collective-permute-start = (f32[256,128]{1,0:T(8,128)}, f32[256,128]{1,0:T(8,128)}, u32[]{:S(2)}, u32[]{:S(2)}) collective-permute-start(f32[256,128]{1,0:T(8,128)} %get-tuple-element.99.refs_1_), channel_id=1, source_target_pairs={{0,4},{4,0},{8,12},{12,8},{16,20},{20,16},{24,28},{28,24},{1,5},{5... | collective-permute-start | bytes 393224 | tf_op jit(solution)/shard_map/ppermute | solution.py:451
  32.0 8.7 %project_queries.1 = (bf16[2048,256]{1,0:T(8,128)(2,1)}, bf16[2048,256]{1,0:T(8,128)(2,1)}, f32[2048,256]{1,0:T(8,128)}) custom-call(bf16[2048,1024]{1,0:T(8,128)(2,1)} %get-tuple-element.88.refs_0_.refs_8_.refs_9_.refs_10_, bf16[1024,768]{1,0:T(8,128)(2,1)} %get-tuple-element.89.refs_1_.refs_6_, f32[1,768]{1,0:T(1,128)} %get-tuple-element.90.refs_2_, ...), custom_call_target="tpu_custom_call" | custom-call | tf_op jit(solution)/shard_map/project_queries/pallas_call | solution.py:76
  44.0 8.4 %collective-permute-done.1.refs_3_ = f32[256,128]{1,0:T(8,128)} collective-permute-done((f32[256,128]{1,0:T(8,128)}, f32[256,128]{1,0:T(8,128)}, u32[]{:S(2)}, u32[]{:S(2)}) %collective-permute-start.1) | collective-permute-done | bytes 131104 | tf_op jit(solution)/shard_map/ppermute | solution.py:451
  52.4 1.8 join_states.5
  55.8 21.2 %feed_forward.1 = (bf16[2048,768]{1,0:T(8,128)(2,1)}, bf16[2048,768]{1,0:T(8,128)(2,1)}, f32[8,768]{1,0:T(8,128)}, f32[4,768,128]{2,1,0:T(8,128)}, f32[2,768,128...) custom-call(bf16[2048,1024]{1,0:T(8,128)(2,1)} %get-tuple-element.88, ...), custom_call_target="tpu_custom_call" | custom-call | tf_op jit(solution)/shard_map/feed_forward/pallas_call | solution.py:76
  77.7 3.0 %collective-permute-start.4 = (f32[4,768,128]{2,1,0:T(8,128)}, f32[4,768,128]{2,1,0:T(8,128)}, u32[]{:S(2)}, u32[]{:S(2)}) collective-permute-start(f32[4,768,128]{2,1,0:T(8,128)} %get-tuple-element.109), channel_id=1, source_target_pairs={{0,8},{4,12},{8,0},{12,4},{16,24},{20,28},{24,16},{28,20},{1,9},{5... | collective-permute-start | bytes 4718600 | tf_op jit(solution)/shard_map/ppermute | solution.py:451
  80.7 29.9 %attend.1 = (bf16[2048,256]{1,0:T(8,128)(2,1)}, f32[2048,256]{1,0:T(8,128)}, f32[2048,256]{1,0:T(8,128)}, f32[8,256,128]{2,1,0:T(8,128)}, f32[256,128]{1,0:T(8,1...) custom-call(s32[8]{0:T(128)} %refs_0_.17, ...), custom_call_target="tpu_custom_call" | custom-call | flops 6442450944 | tf_op jit(solution)/shard_map/attend/pallas_call | solution.py:76
  111.6 2.1 collective-permute-done.6.refs_1_
  115.2 3.4 %far_sums.2.refs_3_ = f32[512,1024]{1,0:T(8,128)} custom-call(f32[2,512,1024]{2,1,0:T(8,128)} %get-tuple-element.105.refs_0_.refs_1_, f32[256,1024]{1,0:T(8,128)} %collective-permute-done.6.refs_1_, f32[256,1024]{1,0:T(8,128)} %collective-permute-done.7.refs_2_, bf16[2048,256]{1,0:T(8,128)(2,1)} %get-tuple-element.113.refs_3_), custom_call_target="tpu_custom_call" | custom-call | tf_op jit(solution)/shard_map/far_sums/pallas_call | solution.py:76
  119.4 1.7 join_states.6
  121.1 1.8 collective-permute-start.10
  122.9 3.1 %sums.7 = (f32[2,768,128]{2,1,0:T(8,128)}, f32[2,768,128]{2,1,0:T(8,128)}, f32[512,1024]{1,0:T(8,128)}) custom-call(f32[2,768,128]{2,1,0:T(8,128)} %get-tuple-element.106.refs_0_, f32[4,768,128]{2,1,0:T(8,128)} %collective-permute-done.3.refs_1_.refs_3_.refs_2_, f32[2,768,128]{2,1,0:T(8,128)} %get-tuple-element.108.refs_2_, ...), custom_call_target="tpu_custom_call", output_to_operand_aliasing={{2}: (6, {})} | custom-call | tf_op jit(solution)/shard_map/sums/pallas_call | solution.py:76
  126.4 1.8 join_states.7
  132.6 2.5 %collective-permute-start.14 = (f32[2,768,128]{2,1,0:T(8,128)}, f32[2,768,128]{2,1,0:T(8,128)}, u32[]{:S(2)}, u32[]{:S(2)}) collective-permute-start(f32[2,768,128]{2,1,0:T(8,128)} %get-tuple-element.138), channel_id=1, source_target_pairs={{0,16},{4,20},{8,24},{12,28},{16,0},{20,4},{24,8},{28,12},{1,17},{... | collective-permute-start | bytes 2359304 | tf_op jit(solution)/shard_map/ppermute | solution.py:451
  136.5 12.1 %keys.1 = (bf16[2048,512]{1,0:T(8,128)(2,1)}, f32[8,512]{1,0:T(8,128)}, f32[4,512,128]{2,1,0:T(8,128)}, f32[2,512,128]{2,1,0:T(8,128)}, f32[2,512,128]{2,1,0:T(8,128)}) custom-call(s32[8]{0:T(128)} %refs_0_.17, bf16[2048,256]{1,0:T(8,128)(2,1)} %get-tuple-element.94.refs_2_.refs_1_, bf16[2048,256]{1,0:T(8,128)(2,1)} %get-tuple-element.95.refs_3_.refs_2_, ...), custom_call_target="tpu_custom_call" | custom-call | flops 53687091200 | tf_op jit(solution)/shard_map/keys/pallas_call | solution.py:76
  149.1 9.1 %inward.2 = (f32[2,512,1024]{2,1,0:T(8,128)}, f32[8,1024]{1,0:T(8,128)}, f32[8,1024]{1,0:T(8,128)}) custom-call(bf16[2048,1024]{1,0:T(8,128)(2,1)} %refs_0_.21, bf16[2048,256]{1,0:T(8,128)(2,1)} %get-tuple-element.118.refs_1_, bf16[2048,768]{1,0:T(8,128)(2,1)} %get-tuple-element.119.refs_2_, bf16[2048,256]{1,0:T(8,128)(2,1)} %get-tuple-element.113.refs_3_, ...), custom_call_target="tpu_custom_call" | custom-call | flops 13958643712 | tf_op jit(solution)/shard_map/inward/pallas_call | solution.py:76
  158.2 11.9 %all_to_all.5.refs_0_.refs_1_ = f32[2,512,1024]{2,1,0:T(8,128)} all-to-all(f32[2,512,1024]{2,1,0:T(8,128)} %get-tuple-element.139.refs_2_), channel_id=1, replica_groups={{0,1},{2,3},{4,5},{6,7},{8,9},{10,11},{12,13},{14,15},{16,17},{18,19},{..., dimensions={0} | all-to-all | bytes 8388608 | tf_op jit(solution)/shard_map/all_to_all | solution.py:1192
  170.1 3.3 %far_sums.3.refs_8_ = f32[512,1024]{1,0:T(8,128)} custom-call(f32[2,512,1024]{2,1,0:T(8,128)} %all_to_all.5.refs_0_.refs_1_, f32[2,512,1024]{2,1,0:T(8,128)} %all_to_all.5.refs_0_.refs_1_, f32[2,512,1024]{2,1,0:T(8,128)} %get-tuple-element.139.refs_2_), custom_call_target="tpu_custom_call" | custom-call | tf_op jit(solution)/shard_map/far_sums/pallas_call | solution.py:76
  173.4 2.8 %collective-permute-start.17 = (f32[512,1024]{1,0:T(8,128)}, f32[512,1024]{1,0:T(8,128)}, u32[]{:S(2)}, u32[]{:S(2)}) collective-permute-start(f32[512,1024]{1,0:T(8,128)} %far_sums.3.refs_8_), channel_id=1, source_target_pairs={{0,2},{1,3},{2,0},{3,1},{4,6},{5,7},{6,4},{7,5},{8,10},{9,11},{10,... | collective-permute-start | bytes 6291464 | tf_op jit(solution)/shard_map/ppermute | solution.py:451
  176.2 4.8 %collective-permute-done.13.refs_4_.refs_3_ = f32[2,768,128]{2,1,0:T(8,128)} collective-permute-done((f32[2,768,128]{2,1,0:T(8,128)}, f32[2,768,128]{2,1,0:T(8,128)}, u32[]{:S(2)}, u32[]{:S(2)}) %collective-permute-start.13) | collective-permute-done | bytes 786464 | tf_op jit(solution)/shard_map/ppermute | solution.py:451
  181.0 2.5 collective-permute-done.14.refs_7_
  183.5 3.1 %sums.8 = (f32[2,512,128]{2,1,0:T(8,128)}, f32[1,768,128]{2,1,0:T(8,128)}, f32[1,768,128]{2,1,0:T(8,128)}) custom-call(f32[2,512,128]{2,1,0:T(8,128)} %get-tuple-element.133.refs_0_, f32[4,512,128]{2,1,0:T(8,128)} %collective-permute-done.12.refs_1_.refs_2_, f32[2,768,128]{2,1,0:T(8,128)} %get-tuple-element.135.refs_2_.refs_1_, ...), custom_call_target="tpu_custom_call" | custom-call | tf_op jit(solution)/shard_map/sums/pallas_call | solution.py:76
  186.6 2.1 collective-permute-start.20
  190.2 10.4 %inward.3 = (f32[256,1024]{1,0:T(8,128)}, f32[256,1024]{1,0:T(8,128)}, f32[512,1024]{1,0:T(8,128)}, f32[8,1024]{1,0:T(8,128)}, f32[8,1024]{1,0:T(8,128)}) custom-call(bf16[2048,1024]{1,0:T(8,128)(2,1)} %refs_0_.21, bf16[2048,256]{1,0:T(8,128)(2,1)} %get-tuple-element.118.refs_1_, bf16[2048,768]{1,0:T(8,128)(2,1)} %get-tuple-element.119.refs_2_, ...), custom_call_target="tpu_custom_call" | custom-call | tf_op jit(solution)/shard_map/inward/pallas_call | solution.py:76
  202.6 4.1 %finish_output.1.refs_2_ = bf16[512,1024]{1,0:T(8,128)(2,1)} custom-call(bf16[2048,1024]{1,0:T(8,128)(2,1)} %refs_0_.21, f32[2,512,1024]{2,1,0:T(8,128)} %get-tuple-element.105.refs_0_.refs_1_, f32[512,1024]{1,0:T(8,128)} %collective-permute-done.8.refs_8_.refs_2_, f32[512,1024]{1,0:T(8,128)} %collective-permute-done.9.refs_10_.refs_3_, f32[1,1024]{1,0:T(1,128)} %bitcast.13, ...), custom_call_target="tpu_custom_call" | custom-call | tf_op jit(solution)/shard_map/finish_output/pallas_call | solution.py:76
  208.3 3.0 %finish_feed.1 = (f32[1024,128]{1,0:T(8,128)}, f32[128,1024]{1,0:T(8,128)}) custom-call(f32[1,512,128]{2,1,0:T(8,128)} %reduce-scatter.3.cloned.1.call-done.refs_5_.refs_0_, f32[2,768,128]{2,1,0:T(8,128)} %get-tuple-element.135.refs_2_.refs_1_, f32[4,768,128]{2,1,0:T(8,128)} %collective-permute-done.3.refs_1_.refs_3_.refs_2_, ...), custom_call_target="tpu_custom_call" | custom-call | tf_op jit(solution)/shard_map/finish_feed/pallas_call | solution.py:76
  215.5 1.9 sums.11.refs_2_
  217.4 4.4 %collective-permute-done.22.refs_1_ = f32[80,128]{1,0:T(8,128)} collective-permute-done((f32[80,128]{1,0:T(8,128)}, f32[80,128]{1,0:T(8,128)}, u32[]{:S(2)}, u32[]{:S(2)}) %collective-permute-start.22) | collective-permute-done | bytes 40992 | tf_op jit(solution)/shard_map/ppermute | solution.py:451
  227.9 5.2 %finish_input.1.refs_2_ = f32[512,1024]{1,0:T(8,128)} custom-call(bf16[2048,1024]{1,0:T(8,128)(2,1)} %refs_0_.21, bf16[2048,1024]{1,0:T(8,128)(2,1)} %refs_1_.5, f32[1,1024]{1,0:T(1,128)} %bitcast.12, f32[512,1024]{1,0:T(8,128)} %get-tuple-element.150.refs_3_, f32[256,1024]{1,0:T(8,128)} %collective-permute-done.15.refs_4_, ...), custom_call_target="tpu_custom_call" | custom-call | tf_op jit(solution)/shard_map/finish_input/pallas_call | solution.py:76
  234.6 4.1 %collective-permute-done.26.refs_4_ = f32[1,512,128]{2,1,0:T(8,128)} collective-permute-done((f32[1,512,128]{2,1,0:T(8,128)}, f32[1,512,128]{2,1,0:T(8,128)}, u32[]{:S(2)}, u32[]{:S(2)}) %collective-permute-start.26) | collective-permute-done | bytes 262176 | tf_op jit(solution)/shard_map/ppermute | solution.py:451
  238.6 2.1 finish_heads.1
  (57 shorter events, 33.8 us)
Async XLA Ops:
  7.2 115.7 %reduce-scatter.3.cloned.1.call-start = ((), (), s32[]{:S(2)}) async-start(), calls=%async_computation.3 | async-start | bytes 2359296 | tf_op jit(solution)/shard_map/reduce_scatter | solution.py:1148
  28.9 199.0 %reduce-scatter.5.cloned.1.call-start = ((), (), s32[]{:S(2)}) async-start(), calls=%async_computation.4 | async-start | bytes 2359296 | tf_op jit(solution)/shard_map/reduce_scatter | solution.py:1148
  28.9 11.8 %collective-permute-start = (f32[256,128]{1,0:T(8,128)}, f32[256,128]{1,0:T(8,128)}, u32[]{:S(2)}, u32[]{:S(2)}) collective-permute-start(f32[256,128]{1,0:T(8,128)} %get-tuple-element.99.refs_1_), channel_id=1, source_target_pairs={{0,4},{4,0},{8,12},{12,8},{16,20},{20,16},{24,28},{28,24},{1,5},{5... | collective-permute-start | bytes 393224 | tf_op jit(solution)/shard_map/ppermute | solution.py:451
  42.4 10.0 %collective-permute-start.1 = (f32[256,128]{1,0:T(8,128)}, f32[256,128]{1,0:T(8,128)}, u32[]{:S(2)}, u32[]{:S(2)}) collective-permute-start(f32[256,128]{1,0:T(8,128)} %get-tuple-element.101.refs_2_), channel_id=1, source_target_pairs={{0,8},{4,12},{8,0},{12,4},{16,24},{20,28},{24,16},{28,20},{1,9},{5... | collective-permute-start | bytes 393224 | tf_op jit(solution)/shard_map/ppermute | solution.py:451
  54.2 26.5 %collective-permute-start.2 = (f32[256,128]{1,0:T(8,128)}, f32[256,128]{1,0:T(8,128)}, u32[]{:S(2)}, u32[]{:S(2)}) collective-permute-start(f32[256,128]{1,0:T(8,128)} %get-tuple-element.104.refs_16_), channel_id=1, source_target_pairs={{0,16},{4,20},{8,24},{12,28},{16,0},{20,4},{24,8},{28,12},{1,17},{... | collective-permute-start | bytes 393224 | tf_op jit(solution)/shard_map/ppermute | solution.py:451
  77.0 45.9 %collective-permute-start.3 = (f32[4,768,128]{2,1,0:T(8,128)}, f32[4,768,128]{2,1,0:T(8,128)}, u32[]{:S(2)}, u32[]{:S(2)}) collective-permute-start(f32[4,768,128]{2,1,0:T(8,128)} %get-tuple-element.107), channel_id=1, source_target_pairs={{0,4},{4,0},{8,12},{12,8},{16,20},{20,16},{24,28},{28,24},{1,5},{5... | collective-permute-start | bytes 4718600 | tf_op jit(solution)/shard_map/ppermute | solution.py:451
  77.7 45.2 %collective-permute-start.4 = (f32[4,768,128]{2,1,0:T(8,128)}, f32[4,768,128]{2,1,0:T(8,128)}, u32[]{:S(2)}, u32[]{:S(2)}) collective-permute-start(f32[4,768,128]{2,1,0:T(8,128)} %get-tuple-element.109), channel_id=1, source_target_pairs={{0,8},{4,12},{8,0},{12,4},{16,24},{20,28},{24,16},{28,20},{1,9},{5... | collective-permute-start | bytes 4718600 | tf_op jit(solution)/shard_map/ppermute | solution.py:451
  110.6 3.1 %collective-permute-start.6 = (f32[256,1024]{1,0:T(8,128)}, f32[256,1024]{1,0:T(8,128)}, u32[]{:S(2)}, u32[]{:S(2)}) collective-permute-start(f32[256,1024]{1,0:T(8,128)} %get-tuple-element.111), channel_id=1, source_target_pairs={{0,1},{1,0},{2,3},{3,2},{4,5},{5,4},{6,7},{7,6},{8,9},{9,8},{10,11... | collective-permute-start | bytes 3145736 | tf_op jit(solution)/shard_map/ppermute | solution.py:451
  110.7 4.5 %collective-permute-start.7 = (f32[256,1024]{1,0:T(8,128)}, f32[256,1024]{1,0:T(8,128)}, u32[]{:S(2)}, u32[]{:S(2)}) collective-permute-start(f32[256,1024]{1,0:T(8,128)} %get-tuple-element.112), channel_id=1, source_target_pairs={{0,1},{1,0},{2,3},{3,2},{4,5},{5,4},{6,7},{7,6},{8,9},{9,8},{10,11... | collective-permute-start | bytes 3145736 | tf_op jit(solution)/shard_map/ppermute | solution.py:451
  111.2 8.2 %collective-permute-start.5 = (f32[256,128]{1,0:T(8,128)}, f32[256,128]{1,0:T(8,128)}, u32[]{:S(2)}, u32[]{:S(2)}) collective-permute-start(f32[256,128]{1,0:T(8,128)} %get-tuple-element.110.refs_1_), channel_id=1, source_target_pairs={{0,4},{4,0},{8,12},{12,8},{16,20},{20,16},{24,28},{28,24},{1,5},{5... | collective-permute-start | bytes 393224 | tf_op jit(solution)/shard_map/ppermute | solution.py:451
  121.1 5.3 %collective-permute-start.10 = (f32[256,128]{1,0:T(8,128)}, f32[256,128]{1,0:T(8,128)}, u32[]{:S(2)}, u32[]{:S(2)}) collective-permute-start(f32[256,128]{1,0:T(8,128)} %get-tuple-element.124.refs_2_), channel_id=1, source_target_pairs={{0,8},{4,12},{8,0},{12,4},{16,24},{20,28},{24,16},{28,20},{1,9},{5... | collective-permute-start | bytes 393224 | tf_op jit(solution)/shard_map/ppermute | solution.py:451
  128.2 8.3 %collective-permute-start.11 = (f32[256,128]{1,0:T(8,128)}, f32[256,128]{1,0:T(8,128)}, u32[]{:S(2)}, u32[]{:S(2)}) collective-permute-start(f32[256,128]{1,0:T(8,128)} %get-tuple-element.127.refs_12_), channel_id=1, source_target_pairs={{0,16},{4,20},{8,24},{12,28},{16,0},{20,4},{24,8},{28,12},{1,17},{... | collective-permute-start | bytes 393224 | tf_op jit(solution)/shard_map/ppermute | solution.py:451
  129.2 71.5 %collective-permute-start.9 = (f32[512,1024]{1,0:T(8,128)}, f32[512,1024]{1,0:T(8,128)}, u32[]{:S(2)}, u32[]{:S(2)}) collective-permute-start(f32[512,1024]{1,0:T(8,128)} %far_sums.2.refs_3_), channel_id=1, source_target_pairs={{0,2},{1,3},{2,0},{3,1},{4,6},{5,7},{6,4},{7,5},{8,10},{9,11},{10,... | collective-permute-start | bytes 6291464 | tf_op jit(solution)/shard_map/ppermute | solution.py:451
  131.1 49.9 %collective-permute-start.13 = (f32[2,768,128]{2,1,0:T(8,128)}, f32[2,768,128]{2,1,0:T(8,128)}, u32[]{:S(2)}, u32[]{:S(2)}) collective-permute-start(f32[2,768,128]{2,1,0:T(8,128)} %get-tuple-element.136), channel_id=1, source_target_pairs={{0,8},{4,12},{8,0},{12,4},{16,24},{20,28},{24,16},{28,20},{1,9},{5... | collective-permute-start | bytes 2359304 | tf_op jit(solution)/shard_map/ppermute | solution.py:451
  132.6 50.9 %collective-permute-start.14 = (f32[2,768,128]{2,1,0:T(8,128)}, f32[2,768,128]{2,1,0:T(8,128)}, u32[]{:S(2)}, u32[]{:S(2)}) collective-permute-start(f32[2,768,128]{2,1,0:T(8,128)} %get-tuple-element.138), channel_id=1, source_target_pairs={{0,16},{4,20},{8,24},{12,28},{16,0},{20,4},{24,8},{28,12},{1,17},{... | collective-permute-start | bytes 2359304 | tf_op jit(solution)/shard_map/ppermute | solution.py:451
  135.1 14.0 %collective-permute-start.8 = (f32[512,1024]{1,0:T(8,128)}, f32[512,1024]{1,0:T(8,128)}, u32[]{:S(2)}, u32[]{:S(2)}) collective-permute-start(f32[512,1024]{1,0:T(8,128)} %get-tuple-element.117), channel_id=1, source_target_pairs={{0,1},{1,0},{2,3},{3,2},{4,5},{5,4},{6,7},{7,6},{8,9},{9,8},{10,11... | collective-permute-start | bytes 6291464 | tf_op jit(solution)/shard_map/ppermute | solution.py:451
  148.6 34.9 %collective-permute-start.12 = (f32[4,512,128]{2,1,0:T(8,128)}, f32[4,512,128]{2,1,0:T(8,128)}, u32[]{:S(2)}, u32[]{:S(2)}) collective-permute-start(f32[4,512,128]{2,1,0:T(8,128)} %get-tuple-element.134), channel_id=1, source_target_pairs={{0,4},{4,0},{8,12},{12,8},{16,20},{20,16},{24,28},{28,24},{1,5},{5... | collective-permute-start | bytes 3145736 | tf_op jit(solution)/shard_map/ppermute | solution.py:451
  173.4 54.5 %collective-permute-start.17 = (f32[512,1024]{1,0:T(8,128)}, f32[512,1024]{1,0:T(8,128)}, u32[]{:S(2)}, u32[]{:S(2)}) collective-permute-start(f32[512,1024]{1,0:T(8,128)} %far_sums.3.refs_8_), channel_id=1, source_target_pairs={{0,2},{1,3},{2,0},{3,1},{4,6},{5,7},{6,4},{7,5},{8,10},{9,11},{10,... | collective-permute-start | bytes 6291464 | tf_op jit(solution)/shard_map/ppermute | solution.py:451
  186.5 29.0 %collective-permute-start.23 = (f32[2,512,128]{2,1,0:T(8,128)}, f32[2,512,128]{2,1,0:T(8,128)}, u32[]{:S(2)}, u32[]{:S(2)}) collective-permute-start(f32[2,512,128]{2,1,0:T(8,128)} %get-tuple-element.140.refs_7_), channel_id=1, source_target_pairs={{0,8},{4,12},{8,0},{12,4},{16,24},{20,28},{24,16},{28,20},{1,9},{5... | collective-permute-start | bytes 1572872 | tf_op jit(solution)/shard_map/ppermute | solution.py:451
  186.6 21.7 %collective-permute-start.20 = (f32[1,768,128]{2,1,0:T(8,128)}, f32[1,768,128]{2,1,0:T(8,128)}, u32[]{:S(2)}, u32[]{:S(2)}) collective-permute-start(f32[1,768,128]{2,1,0:T(8,128)} %get-tuple-element.152), channel_id=1, source_target_pairs={{0,16},{4,20},{8,24},{12,28},{16,0},{20,4},{24,8},{28,12},{1,17},{... | collective-permute-start | bytes 1179656 | tf_op jit(solution)/shard_map/ppermute | solution.py:451
  188.6 19.6 %collective-permute-start.21 = (f32[1,768,128]{2,1,0:T(8,128)}, f32[1,768,128]{2,1,0:T(8,128)}, u32[]{:S(2)}, u32[]{:S(2)}) collective-permute-start(f32[1,768,128]{2,1,0:T(8,128)} %get-tuple-element.153), channel_id=1, source_target_pairs={{0,4},{4,0},{8,12},{12,8},{16,20},{20,16},{24,28},{28,24},{1,5},{5... | collective-permute-start | bytes 1179656 | tf_op jit(solution)/shard_map/ppermute | solution.py:451
  202.2 4.5 %collective-permute-start.18 = (f32[80,128]{1,0:T(8,128)}, f32[80,128]{1,0:T(8,128)}, u32[]{:S(2)}, u32[]{:S(2)}) collective-permute-start(f32[80,128]{1,0:T(8,128)} %pack_small.1.refs_5_.refs_0_), channel_id=1, source_target_pairs={{0,4},{4,0},{8,12},{12,8},{16,20},{20,16},{24,28},{28,24},{1,5},{5... | collective-permute-start | bytes 122888 | tf_op jit(solution)/shard_map/ppermute | solution.py:451
  208.2 4.3 %collective-permute-start.19 = (f32[80,128]{1,0:T(8,128)}, f32[80,128]{1,0:T(8,128)}, u32[]{:S(2)}, u32[]{:S(2)}) collective-permute-start(f32[80,128]{1,0:T(8,128)} %sums.9.refs_9_.refs_0_), channel_id=1, source_target_pairs={{0,8},{4,12},{8,0},{12,4},{16,24},{20,28},{24,16},{28,20},{1,9},{5... | collective-permute-start | bytes 122888 | tf_op jit(solution)/shard_map/ppermute | solution.py:451
  213.9 7.9 %collective-permute-start.22 = (f32[80,128]{1,0:T(8,128)}, f32[80,128]{1,0:T(8,128)}, u32[]{:S(2)}, u32[]{:S(2)}) collective-permute-start(f32[80,128]{1,0:T(8,128)} %sums.10.refs_3_.refs_0_), channel_id=1, source_target_pairs={{0,16},{4,20},{8,24},{12,28},{16,0},{20,4},{24,8},{28,12},{1,17},{... | collective-permute-start | bytes 122888 | tf_op jit(solution)/shard_map/ppermute | solution.py:451
  223.2 1.6 collective-permute-start.24
  223.2 4.6 %collective-permute-start.15 = (f32[256,1024]{1,0:T(8,128)}, f32[256,1024]{1,0:T(8,128)}, u32[]{:S(2)}, u32[]{:S(2)}) collective-permute-start(f32[256,1024]{1,0:T(8,128)} %get-tuple-element.149.refs_9_), channel_id=1, source_target_pairs={{0,1},{1,0},{2,3},{3,2},{4,5},{5,4},{6,7},{7,6},{8,9},{9,8},{10,11... | collective-permute-start | bytes 3145736 | tf_op jit(solution)/shard_map/ppermute | solution.py:451
  223.8 4.1 %collective-permute-start.16 = (f32[256,1024]{1,0:T(8,128)}, f32[256,1024]{1,0:T(8,128)}, u32[]{:S(2)}, u32[]{:S(2)}) collective-permute-start(f32[256,1024]{1,0:T(8,128)} %get-tuple-element.151), channel_id=1, source_target_pairs={{0,1},{1,0},{2,3},{3,2},{4,5},{5,4},{6,7},{7,6},{8,9},{9,8},{10,11... | collective-permute-start | bytes 3145736 | tf_op jit(solution)/shard_map/ppermute | solution.py:451
  223.8 14.9 %collective-permute-start.26 = (f32[1,512,128]{2,1,0:T(8,128)}, f32[1,512,128]{2,1,0:T(8,128)}, u32[]{:S(2)}, u32[]{:S(2)}) collective-permute-start(f32[1,512,128]{2,1,0:T(8,128)} %sums.11.refs_2_), channel_id=1, source_target_pairs={{0,16},{4,20},{8,24},{12,28},{16,0},{20,4},{24,8},{28,12},{1,17},{... | collective-permute-start | bytes 786440 | tf_op jit(solution)/shard_map/ppermute | solution.py:451
  226.2 6.9 %collective-permute-start.25 = (f32[80,128]{1,0:T(8,128)}, f32[80,128]{1,0:T(8,128)}, u32[]{:S(2)}, u32[]{:S(2)}) collective-permute-start(f32[80,128]{1,0:T(8,128)} %sums.13.refs_7_.refs_0_), channel_id=1, source_target_pairs={{0,2},{1,3},{2,0},{3,1},{4,6},{5,7},{6,4},{7,5},{8,10},{9,11},{10,... | collective-permute-start | bytes 122888 | tf_op jit(solution)/shard_map/ppermute | solution.py:451
Sparse Core Ops, SparseCore 0:
  29.0 80.9 reduce-scatter.2
  131.2 95.1 reduce-scatter.4
